TPU v7x, 128 devices: a whole 4x4x4 slice. The times are simulated.
128 devices in a mesh: ctx: 32 (over z, x, y_hi), tp: 4 (over y_lo, core).
Axes of the slice: x: 4, y: 4 (y_hi: 2, y_lo: 2; y = y_hi * 2 + y_lo), z: 4, core: 2. Of those that a mesh axis runs over, the one named last changes fastest.
Arguments:
- block_input: bfloat16 [2, 4096, 1024], P(None, 'ctx'), may hold values from -40 to 40
- cotangent: bfloat16 [2, 4096, 1024], P(None, 'ctx'), may hold values from -6 to 6
- w_query: bfloat16 [1024, 1024], P('ctx', 'tp'), may hold values from -0.1875 to 0.1875
- key_weight: bfloat16 [1024, 512], P('ctx', 'tp'), may hold values from -0.1875 to 0.1875
- w_value: bfloat16 [1024, 512], P('ctx', 'tp'), may hold values from -0.1875 to 0.1875
- w_out: bfloat16 [1024, 1024], P('ctx', 'tp'), may hold values from -2 to 2
- w_gate: bfloat16 [1024, 4608], P('ctx', 'tp'), may hold values from -0.1875 to 0.1875
- w_up: bfloat16 [1024, 4608], P('ctx', 'tp'), may hold values from -0.1875 to 0.1875
- w_down: bfloat16 [1024, 4608], P('ctx', 'tp'), may hold values from -0.09375 to 0.09375
- norm_gains: bfloat16 [2, 1024], P(None, 'ctx'), may hold values from 0.5 to 1.5
- head_gains: bfloat16 [2, 64], P(None, 'ctx'), may hold values from 0.5 to 1.5
Outputs:
- block_output: bfloat16 [2, 4096, 1024], P(None, 'ctx')
- input_grad: float32 [2, 4096, 1024], P(None, 'ctx')
- grad_query: float32 [1024, 1024], P('ctx', 'tp')
- grad_key: float32 [1024, 512], P('ctx', 'tp')
- grad_value: float32 [1024, 512], P('ctx', 'tp')
- grad_out: float32 [1024, 1024], P('ctx', 'tp')
- grad_gate: float32 [1024, 4608], P('ctx', 'tp')
- grad_up: float32 [1024, 4608], P('ctx', 'tp')
- grad_down: float32 [1024, 4608], P('ctx', 'tp')
- grad_norm_gains: float32 [2, 1024], P(None, 'ctx')
- grad_head_gains: float32 [2, 64], P(None, 'ctx')
All inputs are finite; a program needn't handle non-finite values.
Results may differ from a plain program's by a relative error of at most 0.035.
Values may be sent and summed in bfloat16 or wider, within the bound.
A program may use at most 128 MiB of HBM per device.

v0:
```python
import math

import jax
import jax.numpy as jnp
from jax import lax
from jax.sharding import PartitionSpec as P

HEAD_SIZE = 64


EPSILON = 1e-06
ROPE_BASE = 1000000.0


def sent_together(arrays, axis, dim, along):
    ends, at = ([], 0)
    for a in arrays[:-1]:
        at += a.shape[along]
        ends.append(at)
    both = jnp.concatenate(arrays, axis=along)
    return tuple(jnp.split(lax.all_gather(both, axis, axis=dim, tiled=True), ends, axis=along))


def from_everyone(x, axis):
    length = lax.axis_size(axis)
    return lax.all_to_all(jnp.broadcast_to(x[None], (length, *x.shape)), axis, 0, 0, tiled=True)


def taken_together(x, axis):
    return from_everyone(x, axis).sum(axis=0)


def of_everyone(x, axis):
    everything = from_everyone(x, axis)
    return jnp.sum(everything.astype(jnp.float32), axis=0)


def side_by_side(arrays, axis, dim, along):
    columns = [a.reshape(*a.shape[:along], -1) for a in arrays]
    both = jnp.concatenate(columns, axis=along)
    filled, at, outs = (lax.psum_scatter(both, axis, scatter_dimension=dim, tiled=True), 0, [])
    for a, column in zip(arrays, columns):
        piece = filled[..., at : at + column.shape[along]]
        outs.append(piece.reshape(*piece.shape[:along], *a.shape[along:]))
        at += column.shape[along]
    return tuple(outs)


def rms_scale(value_rows):
    return lax.rsqrt(jnp.mean(value_rows * value_rows, axis=-1, keepdims=True) + EPSILON)


def rope_tables(sequence_length, offset, width):
    half_width = width // 2
    inverse = ROPE_BASE ** (-(jnp.arange(half_width, dtype=jnp.float32) * 2.0 / width))
    places = (offset + jnp.arange(sequence_length, dtype=jnp.int32)).astype(jnp.float32)
    angles = places[:, None] * inverse[None, :]
    return (jnp.cos(angles), jnp.sin(angles))


def rotary_apply(value_rows, cosine_table, sine_table, direction):
    half_width = value_rows.shape[-1] // 2
    former = value_rows[..., :half_width]
    latter = value_rows[..., half_width:]
    cosine = cosine_table[:, None, :]
    sine = sine_table[:, None, :] * direction
    return jnp.concatenate(
        [former * cosine - latter * sine, latter * cosine + former * sine], axis=-1
    )


def head_norm(value_rows, gain_row):
    hatted = value_rows * rms_scale(value_rows)
    return (hatted * gain_row, hatted)


def head_norm_reverse(grads, value_rows, hatted, gain_row):
    scaled = grads * gain_row
    return rms_scale(value_rows) * (
        scaled - hatted * jnp.mean(scaled * hatted, axis=-1, keepdims=True)
    )


def row_norm_back(grads, normed, scale_rows, gain_row):
    scaled = grads * gain_row
    return scale_rows * (scaled - normed * jnp.mean(scaled * normed, axis=-1, keepdims=True))


def block_scores(grouped, keys_block, score_scale):
    return (
        jnp.einsum("btkgd,bskd->bkgts", grouped, keys_block, preferred_element_type=jnp.float32)
        * score_scale
    )


def backward_block(
    query_block, grad_block, log_block, delta_block, keys_block, values_block, causal, score_scale
):
    scores = block_scores(query_block, keys_block, score_scale)
    probs = jnp.where(causal, jnp.exp(scores - log_block[..., None]), 0.0)
    grad_probs = jnp.einsum(
        "btkgd,bskd->bkgts", grad_block, values_block, preferred_element_type=jnp.float32
    )
    grad_scores = (probs * (grad_probs - delta_block[..., None]) * score_scale).astype(jnp.bfloat16)
    return (probs.astype(jnp.bfloat16), grad_scores)


def local(
    block_input,
    cotangent,
    w_query,
    key_weight,
    w_value,
    w_out,
    w_gate,
    w_up,
    w_down,
    norm_gains,
    head_gains,
):
    gathered = (
        *sent_together((w_query, key_weight, w_value, w_out, w_gate, w_up, w_down), "ctx", 0, 1),
        lax.all_gather(norm_gains, "ctx", axis=1, tiled=True),
        lax.all_gather(head_gains, "ctx", axis=1, tiled=True),
    )
    (
        query_full,
        key_full,
        value_full,
        out_full,
        gate_full,
        up_full,
        down_full,
        gains_full,
        heads_full,
    ) = gathered
    seqs, tokens, width = block_input.shape
    rows = seqs * tokens
    qheads = query_full.shape[1] // HEAD_SIZE
    kheads = key_full.shape[1] // HEAD_SIZE
    query_group_count = qheads // kheads
    key_width = kheads * HEAD_SIZE
    query_width = qheads * HEAD_SIZE
    score_scale = HEAD_SIZE ** (-0.5)
    inputs = block_input.astype(jnp.float32).reshape(rows, width)
    gain_attn = gains_full[0].astype(jnp.float32)
    gain_ffn = gains_full[1].astype(jnp.float32)
    gain_query = heads_full[0].astype(jnp.float32)
    key_gain_vector = heads_full[1].astype(jnp.float32)
    scale_attn = rms_scale(inputs)
    normed_attn = inputs * scale_attn
    attention_hidden = (normed_attn * gain_attn).astype(jnp.bfloat16)
    query_raw = jnp.dot(attention_hidden, query_full, preferred_element_type=jnp.float32).reshape(
        seqs, tokens, qheads, HEAD_SIZE
    )
    key_projected = jnp.dot(attention_hidden, key_full, preferred_element_type=jnp.float32).reshape(
        seqs, tokens, kheads, HEAD_SIZE
    )
    value_rows = (
        jnp.dot(attention_hidden, value_full, preferred_element_type=jnp.float32)
        .astype(jnp.bfloat16)
        .reshape(seqs, tokens, key_width)
    )
    query_normed, query_hat = head_norm(query_raw, gain_query)
    key_after_norm, key_unit_scaled = head_norm(key_projected, key_gain_vector)
    first_row = lax.axis_index("ctx") * tokens
    last_row = first_row + tokens - 1
    cosine_table, sine_table = rope_tables(tokens, first_row, HEAD_SIZE)
    query_rotated = (
        rotary_apply(query_normed, cosine_table, sine_table, 1.0)
        .astype(jnp.bfloat16)
        .reshape(seqs, tokens, query_width)
    )
    key_rotated = (
        rotary_apply(key_after_norm, cosine_table, sine_table, 1.0)
        .astype(jnp.bfloat16)
        .reshape(seqs, tokens, key_width)
    )
    grouped = query_rotated.reshape(seqs, tokens, kheads, query_group_count, HEAD_SIZE)
    query_pos = first_row + jnp.arange(tokens, dtype=jnp.int32)
    start_state = (
        jnp.zeros((seqs, tokens, query_width), jnp.float32),
        jnp.zeros((seqs, kheads, query_group_count, tokens), jnp.float32),
    )
    keys_piece, values_piece = sent_together((key_rotated, value_rows), "ctx", 1, 0)
    sequence_length = keys_piece.shape[1]
    block_rows = math.gcd(sequence_length, 512)

    def forward_one_block(number, carried):
        block_start = number * block_rows

        def forward_compute(current):
            weighted, denominator = current
            keys_block = lax.dynamic_slice_in_dim(
                keys_piece, number * block_rows, block_rows, 1
            ).reshape(seqs, block_rows, kheads, HEAD_SIZE)
            values_block = lax.dynamic_slice_in_dim(
                values_piece, number * block_rows, block_rows, 1
            ).reshape(seqs, block_rows, kheads, HEAD_SIZE)
            scores = block_scores(grouped, keys_block, score_scale)
            causal = (
                query_pos[:, None]
                >= (block_start + jnp.arange(block_rows, dtype=jnp.int32))[None, :]
            )
            powered = jnp.where(causal, jnp.exp(scores), 0.0)
            update = jnp.einsum(
                "bkgts,bskd->btkgd",
                powered.astype(jnp.bfloat16),
                values_block,
                preferred_element_type=jnp.float32,
            )
            return (
                weighted + update.reshape(seqs, tokens, query_width),
                denominator + jnp.sum(powered, axis=-1),
            )

        return lax.cond(block_start <= last_row, forward_compute, lambda current: current, carried)

    weighted, denominator = lax.fori_loop(
        0, sequence_length // block_rows, forward_one_block, start_state
    )
    attended = (
        (
            weighted.reshape(seqs, tokens, kheads, query_group_count, HEAD_SIZE)
            / denominator.transpose(0, 3, 1, 2)[..., None]
        )
        .astype(jnp.bfloat16)
        .reshape(rows, query_width)
    )
    log_total = jnp.log(denominator)
    attn_part = jnp.dot(attended, out_full.T, preferred_element_type=jnp.float32)
    residual = inputs + taken_together(attn_part, "tp")
    scale_ffn = rms_scale(residual)
    normed_ffn = residual * scale_ffn
    hidden_ffn = (normed_ffn * gain_ffn).astype(jnp.bfloat16)
    gate_raw = jnp.dot(hidden_ffn, gate_full, preferred_element_type=jnp.float32)
    up_raw = jnp.dot(hidden_ffn, up_full, preferred_element_type=jnp.float32)
    sigmoid_gate = jax.nn.sigmoid(gate_raw)
    activated = gate_raw * sigmoid_gate
    hidden_units = (activated * up_raw).astype(jnp.bfloat16)
    ffn_part = jnp.dot(hidden_units, down_full.T, preferred_element_type=jnp.float32)
    block_output = (
        (residual + of_everyone(ffn_part.astype(jnp.bfloat16), "tp").astype(jnp.float32))
        .astype(jnp.bfloat16)
        .reshape(seqs, tokens, width)
    )
    cot_rows = cotangent.reshape(rows, width)
    upstream = cot_rows.astype(jnp.float32)
    grad_units = jnp.dot(cot_rows, down_full, preferred_element_type=jnp.float32)
    grad_down = jnp.dot(cot_rows.T, hidden_units, preferred_element_type=jnp.float32)
    grad_gate_in = (
        grad_units * up_raw * sigmoid_gate * (1.0 + gate_raw * (1.0 - sigmoid_gate))
    ).astype(jnp.bfloat16)
    grad_up_in = (grad_units * activated).astype(jnp.bfloat16)
    grad_gate = jnp.dot(hidden_ffn.T, grad_gate_in, preferred_element_type=jnp.float32)
    grad_up = jnp.dot(hidden_ffn.T, grad_up_in, preferred_element_type=jnp.float32)
    ffn_back = jnp.dot(grad_gate_in, gate_full.T, preferred_element_type=jnp.float32) + jnp.dot(
        grad_up_in, up_full.T, preferred_element_type=jnp.float32
    )
    grad_hidden_ffn = taken_together(ffn_back, "tp")
    ffn_gain_grad = jnp.sum(grad_hidden_ffn * normed_ffn, axis=0)
    grad_residual = upstream + row_norm_back(grad_hidden_ffn, normed_ffn, scale_ffn, gain_ffn)
    residual_bf = grad_residual.astype(jnp.bfloat16)
    attended_gradient = jnp.dot(residual_bf, out_full, preferred_element_type=jnp.float32).astype(
        jnp.bfloat16
    )
    grad_out = jnp.dot(residual_bf.T, attended, preferred_element_type=jnp.float32)
    early_sums = tuple(
        (
            part.astype(jnp.float32)
            for part in side_by_side(
                (
                    grad_out.astype(jnp.bfloat16),
                    grad_gate.astype(jnp.bfloat16),
                    grad_up.astype(jnp.bfloat16),
                    grad_down.astype(jnp.bfloat16),
                    ffn_gain_grad.astype(jnp.bfloat16),
                ),
                "ctx",
                0,
                1,
            )
        )
    )
    products_total = jnp.sum(
        (attended_gradient.astype(jnp.float32) * attended.astype(jnp.float32)).reshape(
            seqs, tokens, qheads, HEAD_SIZE
        ),
        axis=-1,
    )
    delta_local = products_total.reshape(seqs, tokens, kheads, query_group_count).transpose(
        0, 2, 3, 1
    )
    grad_rows = attended_gradient.reshape(seqs, tokens, query_width)
    grad_grouped = attended_gradient.reshape(seqs, tokens, kheads, query_group_count, HEAD_SIZE)
    zero_query = jnp.zeros((seqs, tokens, query_width), jnp.float32)
    query_keys_piece, query_values_piece = sent_together((key_rotated, value_rows), "ctx", 1, 0)
    sequence_length = query_keys_piece.shape[1]
    query_block_rows = math.gcd(sequence_length, 512)

    def query_one_block(number, carried):
        block_start = number * query_block_rows

        def query_compute(current):
            keys_block = lax.dynamic_slice_in_dim(
                query_keys_piece, number * query_block_rows, query_block_rows, 1
            ).reshape(seqs, query_block_rows, kheads, HEAD_SIZE)
            values_block = lax.dynamic_slice_in_dim(
                query_values_piece, number * query_block_rows, query_block_rows, 1
            ).reshape(seqs, query_block_rows, kheads, HEAD_SIZE)
            causal = (
                query_pos[:, None]
                >= (block_start + jnp.arange(query_block_rows, dtype=jnp.int32))[None, :]
            )
            probs_bf, grad_scores = backward_block(
                grouped,
                grad_grouped,
                log_total,
                delta_local,
                keys_block,
                values_block,
                causal,
                score_scale,
            )
            update = jnp.einsum(
                "bkgts,bskd->btkgd", grad_scores, keys_block, preferred_element_type=jnp.float32
            )
            return current + update.reshape(seqs, tokens, query_width)

        return lax.cond(block_start <= last_row, query_compute, lambda current: current, carried)

    grad_query_rot = lax.fori_loop(
        0, sequence_length // query_block_rows, query_one_block, zero_query
    )
    local_keys = key_rotated.reshape(seqs, tokens, kheads, HEAD_SIZE)
    local_values = value_rows.reshape(seqs, tokens, kheads, HEAD_SIZE)
    log_rows = log_total.transpose(0, 3, 1, 2).reshape(seqs, tokens, qheads)
    log_all, delta_all = sent_together((log_rows, products_total), "ctx", 1, 0)
    zero_keys = jnp.zeros((seqs, tokens, key_width), jnp.float32)
    query_piece, grad_piece = sent_together((query_rotated, grad_rows), "ctx", 1, 0)
    sequence_length = query_piece.shape[1]
    key_block_rows = math.gcd(sequence_length, 512)

    def key_one_block(number, carried):
        block_start = number * key_block_rows

        def key_compute(current):
            key_acc, value_acc = current
            begin = number * key_block_rows
            query_block = lax.dynamic_slice_in_dim(query_piece, begin, key_block_rows, 1).reshape(
                seqs, key_block_rows, kheads, query_group_count, HEAD_SIZE
            )
            grad_block = lax.dynamic_slice_in_dim(grad_piece, begin, key_block_rows, 1).reshape(
                seqs, key_block_rows, kheads, query_group_count, HEAD_SIZE
            )
            log_block = (
                lax.dynamic_slice_in_dim(log_all, block_start, key_block_rows, 1)
                .reshape(seqs, key_block_rows, kheads, query_group_count)
                .transpose(0, 2, 3, 1)
            )
            delta_block = (
                lax.dynamic_slice_in_dim(delta_all, block_start, key_block_rows, 1)
                .reshape(seqs, key_block_rows, kheads, query_group_count)
                .transpose(0, 2, 3, 1)
            )
            causal = (block_start + jnp.arange(key_block_rows, dtype=jnp.int32))[
                :, None
            ] >= query_pos[None, :]
            probs_bf, grad_scores = backward_block(
                query_block,
                grad_block,
                log_block,
                delta_block,
                local_keys,
                local_values,
                causal,
                score_scale,
            )
            key_new = jnp.einsum(
                "bkgts,btkgd->bskd", grad_scores, query_block, preferred_element_type=jnp.float32
            )
            value_new = jnp.einsum(
                "bkgts,btkgd->bskd", probs_bf, grad_block, preferred_element_type=jnp.float32
            )
            return (
                key_acc + key_new.reshape(seqs, tokens, key_width),
                value_acc + value_new.reshape(seqs, tokens, key_width),
            )

        return lax.cond(
            block_start + key_block_rows - 1 >= first_row,
            key_compute,
            lambda current: current,
            carried,
        )

    key_gradient, value_gradient = lax.fori_loop(
        0, sequence_length // key_block_rows, key_one_block, (zero_keys, zero_keys)
    )
    grad_query_heads = rotary_apply(
        grad_query_rot.reshape(seqs, tokens, qheads, HEAD_SIZE), cosine_table, sine_table, -1.0
    )
    query_gain_grad = jnp.sum(grad_query_heads * query_hat, axis=(0, 1, 2))
    grad_query_in = (
        head_norm_reverse(grad_query_heads, query_raw, query_hat, gain_query)
        .astype(jnp.bfloat16)
        .reshape(rows, query_width)
    )
    key_heads_gradient = rotary_apply(
        key_gradient.reshape(seqs, tokens, kheads, HEAD_SIZE), cosine_table, sine_table, -1.0
    )
    key_gain_grad = jnp.sum(key_heads_gradient * key_unit_scaled, axis=(0, 1, 2))
    key_input_gradient = (
        head_norm_reverse(key_heads_gradient, key_projected, key_unit_scaled, key_gain_vector)
        .astype(jnp.bfloat16)
        .reshape(rows, key_width)
    )
    value_input = value_gradient.astype(jnp.bfloat16).reshape(rows, key_width)
    grad_query = jnp.dot(attention_hidden.T, grad_query_in, preferred_element_type=jnp.float32)
    grad_key = jnp.dot(attention_hidden.T, key_input_gradient, preferred_element_type=jnp.float32)
    grad_value = jnp.dot(attention_hidden.T, value_input, preferred_element_type=jnp.float32)
    attn_back = (
        jnp.dot(grad_query_in, query_full.T, preferred_element_type=jnp.float32)
        + jnp.dot(key_input_gradient, key_full.T, preferred_element_type=jnp.float32)
        + jnp.dot(value_input, value_full.T, preferred_element_type=jnp.float32)
    )
    grad_hidden_attn, head_grads = (
        of_everyone(attn_back.astype(jnp.bfloat16), "tp").astype(jnp.float32),
        of_everyone(jnp.stack([query_gain_grad, key_gain_grad]).astype(jnp.bfloat16), "tp").astype(
            jnp.float32
        ),
    )
    attn_gain_grad = jnp.sum(grad_hidden_attn * normed_attn, axis=0)
    input_grad = (
        grad_residual + row_norm_back(grad_hidden_attn, normed_attn, scale_attn, gain_attn)
    ).reshape(seqs, tokens, width)
    late_sums = (
        *tuple(
            (
                part.astype(jnp.float32)
                for part in side_by_side(
                    (
                        grad_query.astype(jnp.bfloat16),
                        grad_key.astype(jnp.bfloat16),
                        grad_value.astype(jnp.bfloat16),
                        attn_gain_grad.astype(jnp.bfloat16),
                    ),
                    "ctx",
                    0,
                    1,
                )
            )
        ),
        lax.psum_scatter(
            head_grads.astype(jnp.bfloat16), "ctx", scatter_dimension=1, tiled=True
        ).astype(jnp.float32),
    )
    norm_sum = jnp.stack([late_sums[3], early_sums[4]])
    return (
        block_output,
        input_grad,
        late_sums[0],
        late_sums[1],
        late_sums[2],
        early_sums[0],
        early_sums[1],
        early_sums[2],
        early_sums[3],
        norm_sum,
        late_sums[4],
    )


def solution(mesh):
    placed = (
        P(None, "ctx", None),
        P(None, "ctx", None),
        P("ctx", "tp"),
        P("ctx", "tp"),
        P("ctx", "tp"),
        P("ctx", "tp"),
        P("ctx", "tp"),
        P("ctx", "tp"),
        P("ctx", "tp"),
        P(None, "ctx"),
        P(None, "ctx"),
    )
    return jax.shard_map(
        local,
        mesh=mesh,
        in_specs=placed,
        out_specs=(
            P(None, "ctx", None),
            P(None, "ctx", None),
            P("ctx", "tp"),
            P("ctx", "tp"),
            P("ctx", "tp"),
            P("ctx", "tp"),
            P("ctx", "tp"),
            P("ctx", "tp"),
            P("ctx", "tp"),
            P(None, "ctx"),
            P(None, "ctx"),
        ),
        check_vma=False,
    )
```

profile of v0, /device:TPU:0, one launch (start us, length us, event | category | flops | bytes accessed | tf_op | source)
XLA Modules:
  0.0 1001.4 jit_solution(13908013163753144367)
XLA Ops:
  13.6 96.0 %all-gather = bf16[32,32,2]{1,2,0:T(2,128)(2,1)S(1)} all-gather(bf16[1,32,2]{1,2,0:T(2,128)(2,1)} %bitcast.349), channel_id=1, replica_groups=mesh['ctx'=32,'tp'=4] {'ctx'}, dimensions={0}, use_global_device_ids=true | all-gather | bytes 4224 | tf_op jit(solution)/shard_map/all_gather | solution.py:123
  110.5 86.9 %all-gather.1 = bf16[32,2,2]{2,1,0:T(2,128)(2,1)S(1)} all-gather(bf16[1,2,2]{2,1,0:T(2,128)(2,1)S(1)} %bitcast.350), channel_id=1, replica_groups=mesh['ctx'=32,'tp'=4] {'ctx'}, dimensions={0}, use_global_device_ids=true | all-gather | bytes 264 | tf_op jit(solution)/shard_map/all_gather | solution.py:124
  208.8 76.0 %all-gather.8.cloned.1.call-done = bf16[4,4096,128]{1,2,0:T(8,128)(2,1)} async-done(((bf16[4,128,128]{1,2,0:T(8,128)(2,1)}), bf16[4,4096,128]{1,2,0:T(8,128)(2,1)}) %all-gather.8.cloned.1.call-update) | async-done | bytes 4194320 | tf_op jit(solution)/shard_map/all_gather | solution.py:21
  284.8 4.7 fusion.111
  289.6 2.8 while.54
  289.6 2.4 conditional.10
  294.9 2.5 broadcast_in_dim.37
  297.4 5.0 all-to-all-start
  302.4 3.6 convolution_bitcast_fusion
  305.9 44.6 %all-to-all-done = f32[4,256,1024]{2,1,0:T(8,128)} async-done(((f32[4,256,1024]{2,1,0:T(8,128)}), f32[4,256,1024]{2,1,0:T(8,128)}, u32[]{:S(2)}, u32[]{:S(2)}) %all-to-all-start) | async-done | bytes 4194336 | tf_op jit(solution)/shard_map/all_to_all | solution.py:26
  350.6 2.7 reduce_sum.193
  354.4 2.8 fusion.52
  357.3 4.4 multiply_convert_fusion.1
  363.6 2.5 broadcast_in_dim.43
  366.0 5.0 all-to-all-start.2
  371.9 47.3 %all-to-all-done.2 = f32[4,256,1024]{2,1,0:T(8,128)} async-done(((f32[4,256,1024]{2,1,0:T(8,128)}), f32[4,256,1024]{2,1,0:T(8,128)}, u32[]{:S(2)}, u32[]{:S(2)}) %all-to-all-start.2) | async-done | bytes 4194336 | tf_op jit(solution)/shard_map/all_to_all | solution.py:26
  419.2 2.7 reduce_sum.198
  422.0 1.8 multiply_reduce_fusion
  424.8 2.1 convert_multiply_fusion.2
  431.1 2.1 fusion.66
  435.5 2.4 fusion.44
  437.9 2.5 fusion.43
  440.4 2.4 fusion.46
  448.6 5.5 while.55
  448.6 5.2 conditional.11
  448.7 1.8 constant_dynamic-slice_fusion.2
  451.7 2.0 fusion.20
  454.9 1.8 multiply_reduce_fusion.3
  459.3 148.2 %all_gather.24 = f32[4,4096,4]{1,0,2:T(4,128)S(1)} all-gather(f32[4,128,4]{1,0,2:T(4,128)S(1)} %pad_maximum_fusion.7), channel_id=1, replica_groups=mesh['ctx'=32,'tp'=4] {'ctx'}, dimensions={1}, use_global_device_ids=true | all-gather | bytes 270336 | tf_op jit(solution)/shard_map/all_gather | solution.py:21
  609.1 6.1 fusion.110
  615.3 70.4 %while.56 = (s32[]{:T(128)}, f32[2,128,128]{1,2,0:T(8,128)S(1)}, f32[2,128,128]{1,2,0:T(8,128)S(1)}, s32[]{:T(128)}, bf16[2,4096,256]{1,2,0:T(8,128)(2,1)}, /*in...) while((s32[]{:T(128)}, f32[2,128,128]{1,2,0:T(8,128)S(1)}, ...), condition=%wide.region_22.23_spmd.clone.clone, body=%wide.region_19.22_spmd.clone.clone.sunk | while | flops 272761472 | bytes 14064047 | solution.py:397
  615.3 8.8 conditional.12
  618.0 1.8 fusion.33
  621.6 2.1 fusion.34
  624.1 8.8 conditional.12
  626.8 1.8 fusion.33
  630.4 2.1 fusion.34
  632.9 8.8 conditional.12
  635.6 1.8 fusion.33
  639.2 2.1 fusion.34
  641.7 8.8 conditional.12
  644.4 1.8 fusion.33
  648.0 2.1 fusion.34
  650.5 8.8 conditional.12
  653.2 1.8 fusion.33
  656.8 2.1 fusion.34
  659.3 8.7 conditional.12
  665.6 2.1 fusion.34
  668.1 8.8 conditional.12
  674.4 2.1 fusion.34
  676.9 8.7 conditional.12
  683.2 2.1 fusion.34
  694.3 3.6 all-to-all-start.3
  698.0 2.7 fusion.63
  700.7 27.1 %all-to-all-done.3 = bf16[4,256,1024]{2,1,0:T(8,128)(2,1)S(1)} async-done(((bf16[4,256,1024]{2,1,0:T(8,128)(2,1)}), bf16[4,256,1024]{2,1,0:T(8,128)(2,1)S(1)}, u32[]{:S(2)}, u32[]{:S(2)}) %all-to-all-start.3) | async-done | bytes 2097184 | tf_op jit(solution)/shard_map/all_to_all | solution.py:26
  729.5 4.6 all-to-all-start.1
  739.8 20.9 %all-to-all-done.1 = bf16[4,256,1024]{2,1,0:T(8,128)(2,1)} async-done(((bf16[4,256,1024]{2,1,0:T(8,128)(2,1)}), bf16[4,256,1024]{2,1,0:T(8,128)(2,1)}, u32[]{:S(2)}, u32[]{:S(2)}) %all-to-all-start.1) | async-done | bytes 2097184 | tf_op jit(solution)/shard_map/all_to_all | solution.py:26
  760.7 3.1 convert_reduce_fusion.1
  763.9 40.5 %reduce-scatter.6.cloned.1.call-done = bf16[32,3713]{1,0:T(8,128)(2,1)} async-done(((bf16[1024,3713]{1,0:T(8,128)(2,1)}), bf16[32,3713]{1,0:T(8,128)(2,1)}) %reduce-scatter.6.cloned.1.call-update) | async-done | bytes 237648 | tf_op jit(solution)/shard_map/reduce_scatter | solution.py:41
  808.0 3.2 all-to-all-start.4
  812.1 2.8 all-to-all-done.4
  814.9 91.8 %all-reduce = bf16[2,64]{1,0:T(2,128)(2,1)S(1)} all-reduce(bf16[2,64]{1,0:T(2,128)(2,1)S(1)} %reduce_sum.211), channel_id=4, replica_groups=mesh['ctx'=32,'tp'=4] {'ctx'}, use_global_device_ids=true, to_apply=%region_33.34.clone | all-reduce | flops 128 | bytes 512
  907.4 3.4 fusion.77
  910.8 78.8 %reduce-scatter.8.cloned.1.call-done = bf16[32,513]{1,0:T(8,128)(2,1)} async-done(((bf16[1024,513]{1,0:T(8,128)(2,1)}), bf16[32,513]{1,0:T(8,128)(2,1)}) %reduce-scatter.8.cloned.1.call-update) | async-done | bytes 32848
  (405 shorter events, 115.7 us)
Async XLA Ops:
  7.2 193.6 %copy-start.2 = (bf16[2,128,1024]{2,1,0:T(8,128)(2,1)S(1)}, bf16[2,128,1024]{2,1,0:T(8,128)(2,1)}, u32[]{:S(2)}) copy-start(bf16[2,128,1024]{2,1,0:T(8,128)(2,1)} %param.23) | copy-start | bytes 1572868
  7.2 193.8 %all-gather.6.cloned.1.call-start = ((), (), s32[]{:S(2)}) async-start(), calls=%async_computation.7 | async-start | bytes 8921088 | tf_op jit(solution)/shard_map/all_gather | solution.py:21
  13.5 271.3 %all-gather.8.cloned.1.call-start = ((), (), s32[]{:S(2)}) async-start(), calls=%async_computation.8 | async-start | bytes 4325376 | tf_op jit(solution)/shard_map/all_gather | solution.py:21
  198.7 5.2 copy-start.47
  198.7 9.2 copy-start.48
  198.8 3.4 copy-start.40
  198.8 3.4 copy-start.35
  198.8 155.4 %copy-start.32 = (f32[1,1024]{1,0:T(1,128)}, f32[1,1024]{1,0:T(1,128)S(1)}, u32[]{:S(2)}) copy-start(f32[1,1024]{1,0:T(1,128)S(1)} %get-tuple-element.1162) | copy-start | bytes 12292
  199.6 254.6 %copy-start.26 = (f32[128,32]{0,1:T(8,128)}, f32[128,32]{0,1:T(8,128)S(1)}, u32[]{:S(2)}) copy-start(f32[128,32]{0,1:T(8,128)S(1)} %get-tuple-element.1168) | copy-start | bytes 49156
  200.8 6.8 copy-start.6
  202.5 5.4 copy-start.12
  202.5 1.5 copy-start.39
  203.8 2.4 copy-start.30
  208.0 81.6 %copy-start.37 = (f32[2,128,4]{1,2,0:T(4,128)}, f32[2,128,4]{1,2,0:T(4,128)S(1)}, u32[]{:S(2)}) copy-start(f32[2,128,4]{1,2,0:T(4,128)S(1)} %add_rsqrt_fusion) | copy-start | bytes 12292
  293.5 3.9 copy-start.15
  297.4 5.0 copy-start.9
  297.4 53.2 %all-to-all-start = ((f32[4,256,1024]{2,1,0:T(8,128)}), f32[4,256,1024]{2,1,0:T(8,128)}, u32[]{:S(2)}, u32[]{:S(2)}) async-start(f32[4,256,1024]{2,1,0:T(8,128)} %broadcast_in_dim.37), calls=%async_computation | async-start | bytes 8388608 | tf_op jit(solution)/shard_map/all_to_all | solution.py:26
  353.3 77.7 %copy-start = (f32[256,1024]{1,0:T(8,128)}, f32[256,1024]{1,0:T(8,128)S(1)}, u32[]{:S(2)}) copy-start(f32[256,1024]{1,0:T(8,128)S(1)} %reduce_sum.193) | copy-start | bytes 3145732
  354.2 3.1 copy-start.44
  354.2 3.1 copy-start.54
  354.2 7.4 slice-start
  354.4 2.9 copy-start.24
  354.4 7.2 slice-start.1
  357.3 4.4 slice-start.2
  361.7 0.9 copy-start.52
  361.7 1.0 copy-start.18
  366.0 5.2 copy-start.21
  366.0 5.2 copy-start.23
  366.0 53.2 %all-to-all-start.2 = ((f32[4,256,1024]{2,1,0:T(8,128)}), f32[4,256,1024]{2,1,0:T(8,128)}, u32[]{:S(2)}, u32[]{:S(2)}) async-start(f32[4,256,1024]{2,1,0:T(8,128)} %broadcast_in_dim.43), calls=%async_computation.2 | async-start | bytes 8388608 | tf_op jit(solution)/shard_map/all_to_all | solution.py:26
  371.0 238.1 %all-gather.10.cloned.1.call-start = ((), (), s32[]{:S(2)}) async-start(), calls=%async_computation.9 | async-start | bytes 8650752 | tf_op jit(solution)/shard_map/all_gather | solution.py:21
  421.9 9.1 copy-start.4
  421.9 2.4 copy-start.33
  422.0 2.4 copy-start.45
  423.8 1.0 copy-start.16
  430.3 374.1 %reduce-scatter.6.cloned.1.call-start = ((), (), s32[]{:S(2)}) async-start(), calls=%async_computation.10 | async-start | bytes 8110080 | tf_op jit(solution)/shard_map/reduce_scatter | solution.py:41
  433.1 2.3 copy-start.19
  433.1 2.3 copy-start.25
  435.5 2.4 copy-start.53
  437.9 2.5 copy-start.51
  440.4 2.4 copy-start.46
  443.8 0.8 copy-start.31
  443.8 1.7 copy-start.28
  443.8 2.9 copy-start.14
  443.8 3.0 copy-start.17
  447.2 1.4 copy-start.38
  617.2 0.8 copy-start.3
  643.6 0.8 copy-start.3
  685.7 5.7 copy-start.13
  694.3 33.5 %all-to-all-start.3 = ((bf16[4,256,1024]{2,1,0:T(8,128)(2,1)}), bf16[4,256,1024]{2,1,0:T(8,128)(2,1)S(1)}, u32[]{:S(2)}, u32[]{:S(2)}) async-start(bf16[4,256,1024]{2,1,0:T(8,128)(2,1)} %broadcast_in_dim.45), calls=%async_computation.3 | async-start | bytes 4194304 | tf_op jit(solution)/shard_map/all_to_all | solution.py:26
  729.5 4.7 copy-start.7
  729.5 31.2 %all-to-all-start.1 = ((bf16[4,256,1024]{2,1,0:T(8,128)(2,1)}), bf16[4,256,1024]{2,1,0:T(8,128)(2,1)}, u32[]{:S(2)}, u32[]{:S(2)}) async-start(bf16[4,256,1024]{2,1,0:T(8,128)(2,1)} %broadcast_in_dim.38), calls=%async_computation.1 | async-start | bytes 4194304 | tf_op jit(solution)/shard_map/all_to_all | solution.py:26
  734.1 255.5 %reduce-scatter.8.cloned.1.call-start = ((), (), s32[]{:S(2)}) async-start(), calls=%async_computation.11 | async-start | bytes 1351680
  734.7 1.7 copy-start.36
  734.7 1.6 copy-start.41
  735.4 1.0 copy-start.8
  736.9 1.6 copy-start.50
  738.3 69.1 %copy-start.49 = (bf16[64]{0:T(256)(128)(2,1)S(1)}, bf16[64]{0:T(256)(128)(2,1)}, u32[]{:S(2)}) copy-start(bf16[64]{0:T(256)(128)(2,1)} %get-tuple-element.1064) | copy-start | bytes 388
  738.4 169.0 %copy-start.1 = (f32[256,1024]{1,0:T(8,128)S(1)}, f32[256,1024]{1,0:T(8,128)}, u32[]{:S(2)}) copy-start(f32[256,1024]{1,0:T(8,128)} %copy-done) | copy-start | bytes 3145732
  738.4 169.0 %copy-start.5 = (f32[256,1024]{1,0:T(8,128)S(1)}, f32[256,1024]{1,0:T(8,128)}, u32[]{:S(2)}) copy-start(f32[256,1024]{1,0:T(8,128)} %copy-done.4) | copy-start | bytes 3145732
  738.4 169.0 %copy-start.10 = (bf16[2,128,1024]{2,1,0:T(8,128)(2,1)S(1)}, bf16[2,128,1024]{2,1,0:T(8,128)(2,1)}, u32[]{:S(2)}) copy-start(bf16[2,128,1024]{2,1,0:T(8,128)(2,1)} %param.24) | copy-start | bytes 1572868
  738.4 169.0 %copy-start.34 = (f32[1,1024]{1,0:T(1,128)S(1)}, f32[1,1024]{1,0:T(1,128)}, u32[]{:S(2)}) copy-start(f32[1,1024]{1,0:T(1,128)} %copy-done.32) | copy-start | bytes 12292
  738.4 169.0 %copy-start.42 = (f32[2,128]{1,0:T(2,128)S(1)}, f32[2,128]{1,0:T(2,128)}, u32[]{:S(2)}) copy-start(f32[2,128]{1,0:T(2,128)} %get-tuple-element.1169) | copy-start | bytes 3076
  738.4 169.0 %copy-start.43 = (f32[2,128]{1,0:T(2,128)S(1)}, f32[2,128]{1,0:T(2,128)}, u32[]{:S(2)}) copy-start(f32[2,128]{1,0:T(2,128)} %get-tuple-element.1164) | copy-start | bytes 3076
  808.0 6.9 all-to-all-start.4
  (11 other events, 8.1 us)
Sparse Core Ops, SparseCore 0:
  13.7 108.3 all-gather.5
  206.4 78.4 all-gather.7
  430.4 123.8 all-gather.9
  559.5 244.8 reduce-scatter.5
  806.7 182.8 reduce-scatter.7
where the time goes:
time: 1010 us; the launch traced here: 1000 us
  blocking collectives  423 us (42%)
  waiting for transfers between devices  338 us (33%)
  local copies, waits for them, and re-layouts  89.2 us (9%)
  matrix products  71.8 us (7%)
  other arithmetic  39.8 us (4%)
  starting transfers between devices  21.7 us (2%)
  between operations  15.7 us (2%)
    all_gather x1, blocking collectives, sent_together(): lax.all_gather(both, axis, axis=dim, tiled=True)  148 us
    all_to_all x5, waiting for transfers between devices, from_everyone(): lax.all_to_all(jnp.broadcast_to(x[None], (length, *x.shape)), axis, 0, 0,...  143 us
    all_gather x1, blocking collectives, local(): lax.all_gather(norm_gains, 'ctx', axis=1, tiled=True)  96 us
    unnamed x1, blocking collectives  91.8 us
    all_gather x1, blocking collectives, local(): lax.all_gather(head_gains, 'ctx', axis=1, tiled=True)  86.9 us
    unnamed x6, waiting for transfers between devices  78.9 us
    all_gather x3, waiting for transfers between devices, sent_together(): lax.all_gather(both, axis, axis=dim, tiled=True)  76.1 us
    reduce_scatter x1, waiting for transfers between devices, side_by_side(): lax.psum_scatter(both, axis, scatter_dimension=dim, tiled=True)  40.5 us
  transfers between devices with their start and end apart: 10, of which 8 were waited for; matrix products, arithmetic and copies ran while one was open for 14% of the time, Pallas kernels for 0%

commit v1 on v0

v1 whole, which is shorter than its diff:
```python
import functools

import jax
import jax.numpy as jnp
from jax import lax
from jax.experimental import pallas as pl
from jax.experimental.pallas import tpu as pltpu
from jax.sharding import PartitionSpec as P

HEAD_SIZE = 64
EPSILON = 1e-06
ROPE_BASE = 1000000.0
MESH = pl.DeviceIdType.MESH
F32 = jnp.float32
BF16 = jnp.bfloat16
ANY = pl.BlockSpec(memory_space=pl.ANY)
VMEM = pl.BlockSpec(memory_space=pltpu.VMEM)
NCTX = 32
PAIRS = 4
WORKERS = 8
SLOTS = 4
BLOCK = 128


def group(kind):
    c, t = lax.axis_index("ctx"), lax.axis_index("tp")
    h = lax.rem(c, 2)
    if kind == "ctx":
        return NCTX, c, lambda p: (p, t)
    if kind == "tp":
        return 4, t, lambda p: (c, p)
    if kind == "pair":
        return 2, h, lambda p: (c - h + p, t)
    return 8, h * 4 + t, lambda p: (c - h + p // 4, lax.rem(p, 4))


PICKS = {
    "same": lambda ref, p: ref,
    "own": lambda ref, p: ref.at[p],
    "half": lambda ref, p: ref.at[lax.rem(p, 2)],
    "plane": lambda ref, p: ref.at[p // WORKERS],
}


def greet(kinds):
    barrier = pltpu.get_barrier_semaphore()
    total = 0
    for kind in kinds:
        n, me, dev = group(kind)

        @pl.loop(1, n)
        def _(i):
            pl.semaphore_signal(
                barrier, inc=1, device_id=dev(lax.rem(me + i, n)), device_id_type=MESH
            )

        total += n - 1
    pl.semaphore_wait(barrier, total)


def begin(kind, pick, src, dst, send, recv):
    n, me, dev = group(kind)
    choose = PICKS[pick]

    @pl.loop(1, n)
    def _(i):
        p = lax.rem(me + i, n)
        pltpu.make_async_remote_copy(
            src_ref=choose(src, p),
            dst_ref=dst.at[me],
            send_sem=send.at[p],
            recv_sem=recv.at[me],
            device_id=dev(p),
            device_id_type=MESH,
        ).start()

    pltpu.make_async_copy(choose(src, me), dst.at[me], recv.at[me]).start()


def finish(kind, pick, src, dst, send, recv):
    n, me, dev = group(kind)
    choose = PICKS[pick]

    @pl.loop(1, n)
    def _(i):
        p = lax.rem(me + i, n)
        copy = pltpu.make_async_remote_copy(
            src_ref=choose(src, p),
            dst_ref=dst.at[p],
            send_sem=send.at[p],
            recv_sem=recv.at[p],
            device_id=dev(p),
            device_id_type=MESH,
        )
        copy.wait_send()
        copy.wait_recv()

    pltpu.make_async_copy(choose(src, me), dst.at[me], recv.at[me]).wait()


SIZES = {"ctx": NCTX, "tp": 4, "pair": 2, "rows": 8}


def piece_shape(pick, array):
    return array.shape if pick == "same" else array.shape[1:]


def landing(kind, pick, array):
    return jax.ShapeDtypeStruct((SIZES[kind], *piece_shape(pick, array)), array.dtype)


def sems(kinds):
    return [pltpu.SemaphoreType.DMA((SIZES[k],)) for k in kinds for _ in range(2)]


def exchange_body(plan, kinds, *refs):
    n = len(plan)
    srcs, dsts, rest = refs[:n], refs[n : 2 * n], refs[2 * n :]
    greet(kinds)
    for k, (kind, pick) in enumerate(plan):
        begin(kind, pick, srcs[k], dsts[k], rest[2 * k], rest[2 * k + 1])
    for k, (kind, pick) in enumerate(plan):
        finish(kind, pick, srcs[k], dsts[k], rest[2 * k], rest[2 * k + 1])


def exchange(number, kinds, items):
    plan = tuple((kind, pick) for kind, pick, _ in items)
    return pl.pallas_call(
        functools.partial(exchange_body, plan, kinds),
        out_shape=[landing(*item) for item in items],
        in_specs=[ANY] * len(items),
        out_specs=[ANY] * len(items),
        scratch_shapes=sems([kind for kind, _ in plan]),
        compiler_params=pltpu.CompilerParams(collective_id=number, has_side_effects=True),
        name=f"exchange{number}",
    )(*[array for _, _, array in items])


def places():
    c, t = lax.axis_index("ctx"), lax.axis_index("tp")
    slot, low = c // WORKERS, lax.rem(c, WORKERS)
    to = low + lax.rem(slot, 2) * (WORKERS - 1 - 2 * low)
    return c, t, slot, low, to


def block_of(low, j):
    return j * WORKERS + (low if j % 2 == 0 else WORKERS - 1 - low)


def to_workers(src, dst, send, recv, act):
    c, t, slot, low, to = places()
    for p in range(PAIRS):
        target = p * WORKERS + to
        far = pltpu.make_async_remote_copy(
            src_ref=src.at[p],
            dst_ref=dst.at[slot],
            send_sem=send.at[p],
            recv_sem=recv.at[slot],
            device_id=(target, t),
            device_id_type=MESH,
        )
        near = pltpu.make_async_copy(src.at[p], dst.at[slot], send.at[p])

        @pl.when(target != c)
        def _():
            far.start() if act == "start" else far.wait_send()

        @pl.when(target == c)
        def _():
            near.start() if act == "start" else near.wait()


def from_owners(src, dst, send, recv):
    c, t, slot, low, to = places()
    for j in range(SLOTS):
        owner = block_of(low, j)

        @pl.when(owner != c)
        def _():
            pltpu.make_async_remote_copy(
                src_ref=src.at[j],
                dst_ref=dst.at[j],
                send_sem=send.at[j],
                recv_sem=recv.at[j],
                device_id=(owner, t),
                device_id_type=MESH,
            ).wait_recv()


def to_owner(src, dst, send, recv, j, act):
    c, t, slot, low, to = places()
    owner = block_of(low, j)
    far = pltpu.make_async_remote_copy(
        src_ref=src.at[j],
        dst_ref=dst.at[slot],
        send_sem=send.at[j],
        recv_sem=recv.at[slot],
        device_id=(owner, t),
        device_id_type=MESH,
    )
    near = pltpu.make_async_copy(src.at[j], dst.at[slot], send.at[j])

    @pl.when(owner != c)
    def _():
        far.start() if act == "start" else far.wait_send()

    @pl.when(owner == c)
    def _():
        near.start() if act == "start" else near.wait()


def from_workers(src, dst, send, recv):
    c, t, slot, low, to = places()
    for p in range(PAIRS):
        target = p * WORKERS + to

        @pl.when(target != c)
        def _():
            pltpu.make_async_remote_copy(
                src_ref=src.at[p],
                dst_ref=dst.at[p],
                send_sem=send.at[p],
                recv_sem=recv.at[p],
                device_id=(target, t),
                device_id_type=MESH,
            ).wait_recv()


def last_dims(a, b):
    return lax.dot_general(a, b, (((1,), (1,)), ((), ())), preferred_element_type=F32)


def first_dims(a, b):
    return lax.dot_general(a, b, (((0,), (0,)), ((), ())), preferred_element_type=F32)


def causal_mask(b, i):
    shape = (2 * BLOCK, 2 * BLOCK)
    rows = lax.broadcasted_iota(jnp.int32, shape, 0)
    token = b * BLOCK + jnp.where(rows >= BLOCK, rows - BLOCK, rows)
    key = i * 2 * BLOCK + lax.broadcasted_iota(jnp.int32, shape, 1)
    return token >= key


FORWARD_PLAN = (("ctx", "same"), ("ctx", "half"), ("ctx", "half"), ("pair", "same"))


def forward_body(
    q_src, kv_src, wo, gu, dn, cot,
    att, q_buf, kv_buf, o_buf, log_buf, wo_all, gu_all, dn_all, cot_all,
    acc, den, q_send, q_recv, o_send, o_recv, kv_send, kv_recv, *rest,
):
    c, t, slot, low, to = places()
    background = list(zip(FORWARD_PLAN, (wo, gu, dn, cot), (wo_all, gu_all, dn_all, cot_all)))
    greet(["ctx"])
    to_workers(q_src, q_buf, q_send, q_recv, "start")
    begin("ctx", "plane", kv_src, kv_buf, kv_send, kv_recv)
    for k, ((kind, pick), src, dst) in enumerate(background):
        begin(kind, pick, src, dst, rest[2 * k], rest[2 * k + 1])
    to_workers(q_src, q_buf, q_send, q_recv, "wait")
    from_owners(q_src, q_buf, q_send, q_recv)
    finish("ctx", "plane", kv_src, kv_buf, kv_send, kv_recv)
    lanes = lax.broadcasted_iota(jnp.int32, (2 * BLOCK, BLOCK), 1)
    for j in range(SLOTS):
        b = block_of(low, j)
        acc[...] = jnp.zeros_like(acc)
        den[...] = jnp.zeros_like(den)

        def chunk(i, masked):
            q = q_buf[j]
            kv = kv_buf[pl.ds(2 * i, 2)].reshape(2 * BLOCK, BLOCK)
            powered = jnp.exp(last_dims(q, kv))
            if masked:
                powered = jnp.where(causal_mask(b, i), powered, 0.0)
            den[...] += powered[:, :BLOCK] + powered[:, BLOCK:]
            acc[...] += jnp.dot(powered.astype(BF16), kv, preferred_element_type=F32)

        pl.loop(0, b // 2)(lambda i: chunk(i, False))
        chunk(b // 2, True)
        total = jnp.sum(den[...], axis=1, keepdims=True)
        o_buf[j] = jnp.where(lanes >= HEAD_SIZE, acc[...] / total, 0.0).astype(BF16)
        log_buf[j] = jnp.broadcast_to(jnp.log(total), (2 * BLOCK, BLOCK))
        to_owner(o_buf, att, o_send, o_recv, j, "start")
    for j in range(SLOTS):
        to_owner(o_buf, att, o_send, o_recv, j, "wait")
    from_workers(o_buf, att, o_send, o_recv)
    for k, ((kind, pick), src, dst) in enumerate(background):
        finish(kind, pick, src, dst, rest[2 * k], rest[2 * k + 1])


def forward(q_src, kv_src, wo, gu, dn, cot):
    stack = jax.ShapeDtypeStruct((SLOTS, 2 * BLOCK, BLOCK), BF16)
    kinds = [kind for kind, _ in FORWARD_PLAN]
    return pl.pallas_call(
        forward_body,
        out_shape=[
            stack,
            stack,
            jax.ShapeDtypeStruct((NCTX, BLOCK, BLOCK), BF16),
            stack,
            jax.ShapeDtypeStruct((SLOTS, 2 * BLOCK, BLOCK), F32),
        ]
        + [landing(k, p, a) for (k, p), a in zip(FORWARD_PLAN, (wo, gu, dn, cot))],
        in_specs=[ANY] * 6,
        out_specs=[ANY] + [VMEM] * 4 + [ANY] * 4,
        scratch_shapes=[
            pltpu.VMEM((2 * BLOCK, BLOCK), F32),
            pltpu.VMEM((2 * BLOCK, BLOCK), F32),
        ]
        + [pltpu.SemaphoreType.DMA((SLOTS,))] * 4
        + sems(["ctx"] + kinds),
        compiler_params=pltpu.CompilerParams(
            collective_id=2, has_side_effects=True, vmem_limit_bytes=24 * 2**20
        ),
        name="attention_forward",
    )(q_src, kv_src, wo, gu, dn, cot)


BACKWARD_PLAN = (("ctx", "own"), ("ctx", "own"), ("ctx", "own"), ("rows", "own"))


def backward_body(
    do_src, q_buf, kv_buf, o_buf, log_buf, wo, gu, dn, ffn,
    dq_all, dkv_all, wo_all, gu_all, dn_all, ffn_all,
    do_buf, dq_buf, dkv_buf, acc, dkv, do_send, do_recv, dq_send, dq_recv, kv_send, kv_recv, *rest,
):
    c, t, slot, low, to = places()
    background = list(zip(BACKWARD_PLAN, (wo, gu, dn, ffn), (wo_all, gu_all, dn_all, ffn_all)))
    greet(["ctx", "rows"])
    to_workers(do_src, do_buf, do_send, do_recv, "start")
    for k, ((kind, pick), src, dst) in enumerate(background):
        begin(kind, pick, src, dst, rest[2 * k], rest[2 * k + 1])
    dkv[...] = jnp.zeros_like(dkv)
    to_workers(do_src, do_buf, do_send, do_recv, "wait")
    from_owners(do_src, do_buf, do_send, do_recv)
    for j in range(SLOTS):
        b = block_of(low, j)
        acc[...] = jnp.zeros_like(acc)
        delta = jnp.sum(do_buf[j].astype(F32) * o_buf[j].astype(F32), axis=1, keepdims=True)

        def chunk(i, masked):
            q, do = q_buf[j], do_buf[j]
            kv = kv_buf[pl.ds(2 * i, 2)].reshape(2 * BLOCK, BLOCK)
            logs = log_buf[j]
            scores = last_dims(q, kv)
            probs = jnp.exp(scores - jnp.concatenate([logs, logs], axis=1))
            if masked:
                probs = jnp.where(causal_mask(b, i), probs, 0.0)
            grads = (probs * (last_dims(do, kv) - delta)).astype(BF16)
            acc[...] += jnp.dot(grads, kv, preferred_element_type=F32)
            update = first_dims(grads, q) + first_dims(probs.astype(BF16), do)
            dkv[pl.ds(2 * i, 2)] += update.reshape(2, BLOCK, BLOCK)

        pl.loop(0, b // 2)(lambda i: chunk(i, False))
        chunk(b // 2, True)
        dq_buf[j] = (acc[...] * (HEAD_SIZE**-0.5)).astype(BF16)
        to_owner(dq_buf, dq_all, dq_send, dq_recv, j, "start")
    dkv_buf[...] = dkv[...].astype(BF16)
    begin("ctx", "own", dkv_buf, dkv_all, kv_send, kv_recv)
    for j in range(SLOTS):
        to_owner(dq_buf, dq_all, dq_send, dq_recv, j, "wait")
    from_workers(dq_buf, dq_all, dq_send, dq_recv)
    finish("ctx", "own", dkv_buf, dkv_all, kv_send, kv_recv)
    for k, ((kind, pick), src, dst) in enumerate(background):
        finish(kind, pick, src, dst, rest[2 * k], rest[2 * k + 1])


def backward(do_src, q_buf, kv_buf, o_buf, log_buf, wo, gu, dn, ffn):
    kinds = [kind for kind, _ in BACKWARD_PLAN]
    return pl.pallas_call(
        backward_body,
        out_shape=[
            jax.ShapeDtypeStruct((SLOTS, 2 * BLOCK, BLOCK), BF16),
            jax.ShapeDtypeStruct((NCTX, BLOCK, BLOCK), BF16),
        ]
        + [landing(k, p, a) for (k, p), a in zip(BACKWARD_PLAN, (wo, gu, dn, ffn))],
        in_specs=[ANY] + [VMEM] * 4 + [ANY] * 4,
        out_specs=[ANY] * 6,
        scratch_shapes=[
            pltpu.VMEM((SLOTS, 2 * BLOCK, BLOCK), BF16),
            pltpu.VMEM((SLOTS, 2 * BLOCK, BLOCK), BF16),
            pltpu.VMEM((NCTX, BLOCK, BLOCK), BF16),
            pltpu.VMEM((2 * BLOCK, BLOCK), F32),
            pltpu.VMEM((NCTX, BLOCK, BLOCK), F32),
        ]
        + [pltpu.SemaphoreType.DMA((SLOTS,))] * 4
        + sems(["ctx"] + kinds),
        compiler_params=pltpu.CompilerParams(
            collective_id=6, has_side_effects=True, vmem_limit_bytes=24 * 2**20
        ),
        name="attention_backward",
    )(do_src, q_buf, kv_buf, o_buf, log_buf, wo, gu, dn, ffn)


def rms_scale(rows):
    return lax.rsqrt(jnp.mean(rows * rows, axis=-1, keepdims=True) + EPSILON)


def rope_tables(tokens, offset):
    half = HEAD_SIZE // 2
    inverse = ROPE_BASE ** (-(jnp.arange(half, dtype=F32) * 2.0 / HEAD_SIZE))
    places_ = (offset + jnp.arange(tokens, dtype=jnp.int32)).astype(F32)
    angles = places_[:, None] * inverse[None, :]
    return jnp.cos(angles), jnp.sin(angles)


def rotary(rows, cosine, sine, direction):
    half = HEAD_SIZE // 2
    first, second = rows[..., :half], rows[..., half:]
    cosine = cosine[:, None, :]
    sine = sine[:, None, :] * direction
    return jnp.concatenate([first * cosine - second * sine, second * cosine + first * sine], -1)


def head_back(grads, hatted, scale, gain):
    scaled = grads * gain
    return scale * (scaled - hatted * jnp.mean(scaled * hatted, axis=-1, keepdims=True))


def row_back(grads, normed, scale, gain):
    scaled = grads * gain
    return scale * (scaled - normed * jnp.mean(scaled * normed, axis=-1, keepdims=True))


def to_pairs(rows, heads, left):
    s, tokens = rows.shape[:2]
    kv = rows.shape[2] // heads
    x = rows.reshape(s, tokens, kv, heads, HEAD_SIZE).transpose(2, 0, 3, 1, 4)
    x = x.reshape(kv * s, heads * tokens, HEAD_SIZE)
    side = (0, HEAD_SIZE) if left else (HEAD_SIZE, 0)
    return jnp.pad(x, ((0, 0), (0, 0), side))


def from_pairs(x, s, heads):
    kv = x.shape[0] // s
    tokens = x.shape[1] // heads
    x = x.reshape(kv, s, heads, tokens, HEAD_SIZE).transpose(1, 3, 0, 2, 4)
    return x.reshape(s, tokens, kv * heads, HEAD_SIZE)


def halves(w):
    half = w.shape[1] // 2
    return jnp.stack([w[:, :half], w[:, half:]])


def local(
    block_input, cotangent, w_query, key_weight, w_value, w_out, w_gate, w_up, w_down,
    norm_gains, head_gains,
):
    c, t = lax.axis_index("ctx"), lax.axis_index("tp")
    seqs, tokens, width = block_input.shape
    rows = seqs * tokens
    own = rows // 4
    unit_half = w_gate.shape[1] // 2

    def mine(x):
        return lax.dynamic_slice_in_dim(x, t * own, own, 0)

    weight_rows = jnp.concatenate([w_query, key_weight, w_value], axis=1)
    gains = jnp.zeros((16, 128), BF16)
    gains = gains.at[0:2, 0:32].set(norm_gains).at[2:4, 0:2].set(head_gains)
    weights_all, gains_all = exchange(
        1, ["ctx"], [("ctx", "same", weight_rows), ("ctx", "same", gains)]
    )
    qkv_full = weights_all.reshape(width, weight_rows.shape[1])
    gain_attn = gains_all[:, 0, :32].reshape(width).astype(F32)
    gain_ffn = gains_all[:, 1, :32].reshape(width).astype(F32)
    gain_query = gains_all[:, 2, :2].reshape(HEAD_SIZE).astype(F32)
    gain_key = gains_all[:, 3, :2].reshape(HEAD_SIZE).astype(F32)

    inputs = block_input.astype(F32).reshape(rows, width)
    scale_attn = rms_scale(inputs)
    normed_attn = inputs * scale_attn
    hidden_attn = (normed_attn * gain_attn).astype(BF16)
    raw = jnp.dot(hidden_attn, qkv_full, preferred_element_type=F32)
    query_raw = raw[:, :256].reshape(seqs, tokens, 4, HEAD_SIZE)
    key_raw = raw[:, 256:384].reshape(seqs, tokens, 2, HEAD_SIZE)
    values = raw[:, 384:].astype(BF16).reshape(seqs, tokens, 2, HEAD_SIZE)
    query_scale, key_scale = rms_scale(query_raw), rms_scale(key_raw)
    query_hat, key_hat = query_raw * query_scale, key_raw * key_scale
    cosine, sine = rope_tables(tokens, c * tokens)
    query_rot = rotary(query_hat * gain_query, cosine, sine, 1.0).astype(BF16)
    key_rot = rotary(key_hat * gain_key, cosine, sine, 1.0).astype(BF16)
    q_src = to_pairs(query_rot * jnp.asarray(HEAD_SIZE**-0.5, BF16), 2, True)
    kv_src = jnp.concatenate([key_rot, values], axis=-1).transpose(2, 0, 1, 3)
    kv_src = kv_src.reshape(PAIRS, tokens, 2 * HEAD_SIZE)

    gu_src = jnp.concatenate([halves(w_gate), halves(w_up)], axis=2)
    dn_src = halves(w_down)
    att, q_buf, kv_buf, o_buf, log_buf, wo_all, gu_all, dn_all, cot_all = forward(
        q_src, kv_src, w_out, gu_src, dn_src, cotangent.reshape(rows, width)
    )
    attended = from_pairs(att[..., HEAD_SIZE:], seqs, 2).reshape(rows, 256)
    out_full = wo_all.reshape(width, 256)
    gu_full = gu_all.reshape(width, 2 * unit_half)
    dn_full = dn_all.reshape(width, unit_half)
    cot_rows = cot_all.reshape(2 * rows, width)

    attn_part = last_dims(attended, out_full).astype(BF16)
    (attn_parts,) = exchange(3, ["tp"], [("tp", "own", attn_part.reshape(4, own, width))])
    residual = mine(inputs) + jnp.sum(attn_parts.astype(F32), axis=0)
    scale_ffn = rms_scale(residual)
    normed_ffn = residual * scale_ffn
    hidden_own = (normed_ffn * gain_ffn).astype(BF16)
    (hidden_all,) = exchange(4, ["rows"], [("rows", "same", hidden_own)])
    hidden_ffn = hidden_all.reshape(2 * rows, width)

    gu_raw = jnp.dot(hidden_ffn, gu_full, preferred_element_type=F32)
    gate_raw, up_raw = gu_raw[:, :unit_half], gu_raw[:, unit_half:]
    sigmoid = jax.nn.sigmoid(gate_raw)
    activated = gate_raw * sigmoid
    hidden_units = (activated * up_raw).astype(BF16)
    grad_units = jnp.dot(cot_rows, dn_full, preferred_element_type=F32)
    grad_gate_in = grad_units * up_raw * sigmoid * (1.0 + gate_raw * (1.0 - sigmoid))
    grad_up_in = grad_units * activated
    grad_gu_in = jnp.concatenate([grad_gate_in, grad_up_in], axis=1).astype(BF16)
    ffn_back = last_dims(grad_gu_in, gu_full).astype(BF16)
    (back_parts,) = exchange(5, ["rows"], [("rows", "own", ffn_back.reshape(8, own, width))])
    grad_hidden_ffn = jnp.sum(back_parts.astype(F32), axis=0)
    ffn_gain_part = jnp.sum(grad_hidden_ffn * normed_ffn, axis=0)
    cot_own = mine(cotangent.reshape(rows, width)).astype(F32)
    grad_residual = cot_own + row_back(grad_hidden_ffn, normed_ffn, scale_ffn, gain_ffn)
    (residual_all,) = exchange(7, ["tp"], [("tp", "same", grad_residual.astype(BF16))])
    residual_bf = residual_all.reshape(rows, width)

    grad_attended = jnp.dot(residual_bf, out_full, preferred_element_type=F32).astype(BF16)
    do_src = to_pairs(grad_attended.reshape(seqs, tokens, 4, HEAD_SIZE), 2, False)
    grad_out = first_dims(residual_bf, attended).astype(BF16)
    grad_gu = first_dims(hidden_ffn, grad_gu_in).astype(BF16)
    grad_dn = first_dims(cot_rows, hidden_units).astype(BF16)
    ffn_part = last_dims(hidden_units, dn_full).astype(BF16)
    dq_all, dkv_all, wo_parts, gu_parts, dn_parts, ffn_parts = backward(
        do_src, q_buf, kv_buf, o_buf, log_buf,
        grad_out.reshape(NCTX, 32, 256),
        grad_gu.reshape(NCTX, 32, 2 * unit_half),
        grad_dn.reshape(NCTX, 32, unit_half),
        ffn_part.reshape(8, own, width),
    )

    output_own = (residual + jnp.sum(ffn_parts.astype(F32), axis=0)).astype(BF16)
    grad_query_rot = from_pairs(dq_all[..., :HEAD_SIZE].astype(F32), seqs, 2)
    dkv = jnp.sum(dkv_all.reshape(PAIRS, WORKERS, tokens, 2 * HEAD_SIZE).astype(F32), axis=1)
    key_grad = from_pairs(dkv[..., :HEAD_SIZE], seqs, 1)
    value_in = from_pairs(dkv[..., HEAD_SIZE:], seqs, 1).astype(BF16).reshape(rows, 128)
    gq = rotary(grad_query_rot, cosine, sine, -1.0)
    gk = rotary(key_grad, cosine, sine, -1.0)
    query_gain_part = jnp.sum(gq * query_hat, axis=(0, 1, 2))
    key_gain_part = jnp.sum(gk * key_hat, axis=(0, 1, 2))
    query_in = head_back(gq, query_hat, query_scale, gain_query).astype(BF16).reshape(rows, 256)
    key_in = head_back(gk, key_hat, key_scale, gain_key).astype(BF16).reshape(rows, 128)
    grad_in = jnp.concatenate([query_in, key_in, value_in], axis=1)
    grad_qkv = first_dims(hidden_attn, grad_in).astype(BF16)
    attn_back = last_dims(grad_in, qkv_full)
    attn_gain_part = jnp.sum(attn_back * normed_attn, axis=0)
    gain_parts = jnp.zeros((NCTX, 8, 128), F32)
    gain_parts = gain_parts.at[:, 0, :32].set(attn_gain_part.reshape(NCTX, 32))
    gain_parts = gain_parts.at[:, 1, :32].set(ffn_gain_part.reshape(NCTX, 32))
    gain_parts = gain_parts.at[:, 2, :2].set(query_gain_part.reshape(NCTX, 2))
    gain_parts = gain_parts.at[:, 3, :2].set(key_gain_part.reshape(NCTX, 2))
    attn_parts, qkv_parts, gain_all, output_all = exchange(
        8,
        ["ctx", "tp"],
        [
            ("tp", "own", attn_back.astype(BF16).reshape(4, own, width)),
            ("ctx", "own", grad_qkv.reshape(NCTX, 32, 512)),
            ("ctx", "own", gain_parts),
            ("tp", "same", output_own),
        ],
    )
    grad_hidden_attn = jnp.sum(attn_parts.astype(F32), axis=0)
    input_own = grad_residual + row_back(
        grad_hidden_attn, mine(normed_attn), mine(scale_attn), gain_attn
    )
    input_all, gain_tp = exchange(
        9,
        ["tp"],
        [("tp", "same", input_own.astype(BF16)), ("tp", "same", jnp.sum(gain_all, axis=0))],
    )
    gain_sum = jnp.sum(gain_tp, axis=0)
    qkv_grad = jnp.sum(qkv_parts.astype(F32), axis=0)
    out_grad = jnp.sum(wo_parts.astype(F32), axis=0)
    gu_grad = jnp.sum(gu_parts.reshape(16, 2, 32, 2 * unit_half).astype(F32), axis=0)
    dn_grad = jnp.sum(dn_parts.reshape(16, 2, 32, unit_half).astype(F32), axis=0)
    gate_grad = jnp.concatenate([gu_grad[0, :, :unit_half], gu_grad[1, :, :unit_half]], axis=1)
    up_grad = jnp.concatenate([gu_grad[0, :, unit_half:], gu_grad[1, :, unit_half:]], axis=1)
    down_grad = jnp.concatenate([dn_grad[0], dn_grad[1]], axis=1)
    return (
        output_all.reshape(seqs, tokens, width),
        input_all.astype(F32).reshape(seqs, tokens, width),
        qkv_grad[:, :256],
        qkv_grad[:, 256:384],
        qkv_grad[:, 384:],
        out_grad,
        gate_grad,
        up_grad,
        down_grad,
        gain_sum[0:2, :32],
        gain_sum[2:4, :2],
    )


def solution(mesh):
    tokens, weights = P(None, "ctx", None), P("ctx", "tp")
    return jax.shard_map(
        local,
        mesh=mesh,
        in_specs=(tokens,) * 2 + (weights,) * 7 + (P(None, "ctx"),) * 2,
        out_specs=(tokens,) * 2 + (weights,) * 7 + (P(None, "ctx"),) * 2,
        check_vma=False,
    )
```

time: 1010 us -> 401 us (0.40)
  blocking collectives: 423 us -> 0 us
  waiting for transfers between devices: 338 us -> 0 us
  Pallas kernels: 0 us -> 307 us
  local copies, waits for them, and re-layouts: 89.2 us -> 34.3 us
  matrix products: 71.8 us -> 22 us
  starting transfers between devices: 21.7 us -> 0 us
  between operations: 15.7 us -> 2.03 us
    all_gather x3 -> x0, blocking collectives: 331 us -> none  [the longest x1 148 us: sent_together(): lax.all_gather(both, axis, axis=dim, tiled=True)]
    pallas_call x0 -> x9, Pallas kernels: none -> 307 us  [the longest x7 123 us: exchange(): pl.pallas_call(functools.partial(exchange_body, plan, kinds), out_shape=[...]
    all_to_all x5 -> x0, waiting for transfers between devices: 143 us -> none  [from_everyone(): lax.all_to_all(jnp.broadcast_to(x[None], (length, *x.shape)), axis, 0, 0,...]
    unnamed x1 -> x0, blocking collectives: 91.8 us -> none
    unnamed x6 -> x0, waiting for transfers between devices: 78.9 us -> none
    all_gather x3 -> x0, waiting for transfers between devices: 76.1 us -> none  [sent_together(): lax.all_gather(both, axis, axis=dim, tiled=True)]
    dot_general x49 -> x12, matrix products: 71.8 us -> 22 us  [the longest x4 8 us: first_dims(): lax.dot_general(a, b, (((0,), (0,)), ((), ())), preferred_element_type=F32)]
    reduce_scatter x1 -> x0, waiting for transfers between devices: 40.5 us -> none  [side_by_side(): lax.psum_scatter(both, axis, scatter_dimension=dim, tiled=True)]
  transfers between devices with their start and end apart: 10 -> 0, of which waited for: 8 -> 0; matrix products, arithmetic and copies ran while one was open for 14% -> 0% of each run, Pallas kernels for 0% -> 0%
where the time goes in v1:
time: 401 us; the launch traced here: 400 us
  Pallas kernels  307 us (77%)
  local copies, waits for them, and re-layouts  34.3 us (9%)
  other arithmetic  34.1 us (9%)
  matrix products  22 us (5%)
    pallas_call x7, Pallas kernels, exchange(): pl.pallas_call(functools.partial(exchange_body, plan, kinds), out_shape=[...  123 us
    pallas_call x1, Pallas kernels, backward(): pl.pallas_call(backward_body, out_shape=[jax.ShapeDtypeStruct((SLOTS, 2 *...  94.1 us
    pallas_call x1, Pallas kernels, forward(): pl.pallas_call(forward_body, out_shape=[stack, stack, jax.ShapeDtypeStruc...  90.3 us
    unnamed x169, local copies, waits for them, and re-layouts  16.6 us

profile of v1, /device:TPU:0, one launch (start us, length us, event | category | flops | bytes accessed | tf_op | source)
XLA Modules:
  0.0 399.6 jit_solution(6847517982690266179)
XLA Ops:
  0.6 1.2 multiply_reduce_fusion.1
  2.4 1.4 pad_maximum_fusion.12.refs_0_
  3.8 0.7 scatter.20
  4.5 1.5 scatter.21.refs_1_
  6.5 26.8 %exchange1.1 = (bf16[32,32,512]{2,1,0:T(8,128)(2,1)}, bf16[32,16,128]{2,1,0:T(8,128)(2,1)}) custom-call(bf16[32,512]{1,0:T(8,128)(2,1)} %pad_maximum_fusion.12.refs_0_, bf16[16,128]{1,0:T(8,128)(2,1)} %copy-done.62), custom_call_target="tpu_custom_call" | custom-call | tf_op jit(solution)/shard_map/exchange1/pallas_call | solution.py:128
  33.4 1.7 convert_reduce_fusion.9
  35.1 1.2 multiply_convert_fusion.4
  37.2 1.1 convert_reduce_fusion.10
  39.3 0.8 broadcast_multiply_fusion.1
  42.1 90.3 %attention_forward.1 = (bf16[4,256,128]{2,1,0:T(8,128)(2,1)S(1)}, bf16[4,256,128]{2,1,0:T(8,128)(2,1)S(1)}, bf16[32,128,128]{2,1,0:T(8,128)(2,1)S(1)}, bf16[4,25...) custom-call(bf16[4,256,128]{2,1,0:T(8,128)(2,1)S(1)} %pad.35.q_src, ...), custom_call_target="tpu_custom_call" | custom-call | tf_op jit(solution)/shard_map/attention_forward/pallas_call | solution.py:294
  132.4 1.0 copy-done.6
  133.4 0.8 copy-done.10
  134.1 1.4 copy-done.19
  135.6 1.1 copy-done.21
  136.7 1.0 copy-done.24
  138.7 1.1 convolution_convert_fusion.6
  139.8 11.2 %exchange3.1 = bf16[4,64,1024]{2,1,0:T(8,128)(2,1)} custom-call(bf16[4,64,1024]{2,1,0:T(8,128)(2,1)} %bitcast.196), custom_call_target="tpu_custom_call" | custom-call | tf_op jit(solution)/shard_map/exchange3/pallas_call | solution.py:128
  151.0 1.8 convert_reduce_fusion.8
  152.9 1.1 bitcast_convert_fusion.1
  154.0 2.5 multiply_reduce_fusion.7
  156.5 1.4 reshape.607
  157.9 0.7 add_rsqrt_fusion.3
  159.1 1.7 multiply_convert_fusion.7.refs_0_
  160.8 14.4 %exchange4.1 = bf16[8,64,1024]{2,1,0:T(8,128)(2,1)} custom-call(bf16[64,1024]{1,0:T(8,128)(2,1)} %multiply_convert_fusion.7.refs_0_), custom_call_target="tpu_custom_call" | custom-call | tf_op jit(solution)/shard_map/exchange4/pallas_call | solution.py:128
  175.2 2.8 fusion.18
  178.1 2.1 multiply_convert_fusion.2
  180.2 2.5 convolution_convert_fusion.4
  182.8 16.3 %exchange5.1 = bf16[8,64,1024]{2,1,0:T(8,128)(2,1)} custom-call(bf16[8,64,1024]{2,1,0:T(8,128)(2,1)} %bitcast.204), custom_call_target="tpu_custom_call" | custom-call | tf_op jit(solution)/shard_map/exchange5/pallas_call | solution.py:128
  199.1 1.4 convert_reduce_fusion.5
  200.5 0.7 multiply_reduce_fusion.4
  201.8 0.8 fusion.14.refs_0_
  202.6 8.6 %exchange7.1 = bf16[4,64,1024]{2,1,0:T(8,128)(2,1)} custom-call(bf16[64,1024]{1,0:T(8,128)(2,1)} %fusion.14.refs_0_), custom_call_target="tpu_custom_call" | custom-call | tf_op jit(solution)/shard_map/exchange7/pallas_call | solution.py:128
  211.2 1.4 convolution_convert_fusion.7
  213.9 4.3 %convolution_convert_fusion = bf16[1024,1152]{1,0:T(8,128)(2,1)} fusion(bf16[512,1024]{1,0:T(8,128)(2,1)S(1)} %bitcast.203, bf16[512,576]{0,1:T(8,128)(2,1)} %copy-done.80, bf16[512,576]{0,1:T(8,128)(2,1)} %copy-done.79), kind=kOutput, calls=%fused_computation.1 | convolution fusion | flops 1211498496 | bytes 4587520 | tf_op jit(solution)/shard_map/dot_general | solution.py:234
  218.2 1.9 convolution_convert_fusion.1
  220.1 1.8 copy.139
  221.9 2.3 convolution_convert_fusion.3
  224.2 0.9 copy-done.15
  225.1 0.9 copy-done.17
  226.1 94.1 %attention_backward.1 = (bf16[4,256,128]{2,1,0:T(8,128)(2,1)S(1)}, bf16[32,128,128]{2,1,0:T(8,128)(2,1)S(1)}, bf16[32,32,256]{2,1,0:T(8,128)(2,1)S(1)}, bf16[32,...) custom-call(bf16[4,256,128]{2,1,0:T(8,128)(2,1)S(1)} %pad.36.do_src, ...), custom_call_target="tpu_custom_call" | custom-call | tf_op jit(solution)/shard_map/attention_backward/pallas_call | solution.py:370
  320.3 1.4 copy-done
  321.7 1.0 copy-done.4
  322.8 0.6 copy-done.8
  323.9 0.7 reshape.618
  327.1 0.8 copy.143
  328.0 0.8 copy.146
  329.0 0.7 copy.192
  329.7 1.8 copy.145
  331.6 1.2 multiply_reduce_fusion.3
  332.8 1.3 multiply_reduce_fusion
  334.1 1.0 copy-done.31
  335.0 1.4 convolution_convert_fusion.2
  339.1 0.7 add_convert_fusion.1.refs_3_
  339.8 35.5 %exchange8.1 = (bf16[4,64,1024]{2,1,0:T(8,128)(2,1)}, bf16[32,32,512]{2,1,0:T(8,128)(2,1)}, f32[32,8,128]{2,1,0:T(8,128)}, bf16[4,64,1024]{2,1,0:T(8,128)(2,1)}) custom-call(bf16[4,64,1024]{2,1,0:T(8,128)(2,1)} %bitcast.194, bf16[32,32,512]{2,1,0:T(8,128)(2,1)} %bitcast.193, f32[32,8,128]{2,1,0:T(8,128)} %copy-done.46, ...), custom_call_target="tpu_custom_call" | custom-call | tf_op jit(solution)/shard_map/exchange8/pallas_call | solution.py:128
  375.4 1.2 convert_reduce_fusion.7
  376.8 1.7 add_convert_fusion.refs_0_
  379.2 9.9 %exchange9.1 = (bf16[4,64,1024]{2,1,0:T(8,128)(2,1)}, f32[4,8,128]{2,1,0:T(8,128)}) custom-call(bf16[64,1024]{1,0:T(8,128)(2,1)} %add_convert_fusion.refs_0_, f32[8,128]{1,0:T(8,128)} %reduce_sum.242.refs_1_), custom_call_target="tpu_custom_call" | custom-call | tf_op jit(solution)/shard_map/exchange9/pallas_call | solution.py:128
  389.1 2.3 bitcast_convert_fusion
  391.4 1.4 convert_reduce_fusion.3
  394.0 0.7 convert_reduce_fusion.6
  395.1 0.8 pad_maximum_fusion.5
  395.9 0.8 pad_maximum_fusion.6
  396.9 0.8 pad_maximum_fusion.7
  398.8 0.8 copy.203
  (250 shorter events, 17.5 us)
Async XLA Ops:
  2.4 33.9 %copy-start.73 = (f32[2,128]{1,0:T(2,128)}, f32[2,128]{1,0:T(2,128)S(1)}, u32[]{:S(2)}) copy-start(f32[2,128]{1,0:T(2,128)S(1)} %get-tuple-element.176) | copy-start | bytes 3076
  33.4 3.0 copy-start.34
  35.1 1.3 copy-start.50
  36.8 3.9 copy-start.40
  37.1 3.3 copy-start.38
  38.3 1.7 copy-start.64
  40.5 1.2 copy-start.54
  40.5 1.2 copy-start.55
  40.7 1.2 copy-start.56
  40.7 1.3 copy-start.3
  40.8 1.3 copy-start.18
  41.0 1.0 copy-start.70
  132.4 1.0 copy-start.6
  134.1 1.4 copy-start.19
  135.6 1.1 copy-start.21
  138.6 14.3 %copy-start.42 = (bf16[2,2,2,128,64]{3,1,4,2,0:T(2,128)(2,1)}, bf16[2,2,2,128,64]{3,1,4,2,0:T(2,128)(2,1)S(1)}, u32[]{:S(2)}) copy-start(bf16[2,2,2,128,64]{3,1,4,2,0:T(2,128)(2,1)S(1)} %copy.134) | copy-start | bytes 393220
  138.6 14.3 %copy-start.29 = (bf16[2,128,1024]{2,1,0:T(8,128)(2,1)S(1)}, bf16[2,128,1024]{2,1,0:T(8,128)(2,1)}, u32[]{:S(2)}) copy-start(bf16[2,128,1024]{2,1,0:T(8,128)(2,1)} %param.23) | copy-start | bytes 1572868
  154.0 21.2 %copy-start.20 = (bf16[32,32,1152]{2,1,0:T(8,128)(2,1)S(1)}, bf16[32,32,1152]{2,1,0:T(8,128)(2,1)}, u32[]{:S(2)}) copy-start(bf16[32,32,1152]{2,1,0:T(8,128)(2,1)} %copy-done.19) | copy-start | bytes 7077892
  175.2 2.8 copy-start.22
  175.2 2.8 copy-start.25
  180.2 2.5 copy-start.79
  180.2 2.5 copy-start.80
  182.7 17.8 %copy-start.27 = (f32[64,1024]{1,0:T(8,128)S(1)}, f32[64,1024]{1,0:T(8,128)}, u32[]{:S(2)}) copy-start(f32[64,1024]{1,0:T(8,128)} %get-tuple-element.136) | copy-start | bytes 786436
  182.7 17.8 %copy-start.52 = (f32[1024]{0:T(1024)S(1)}, f32[1024]{0:T(1024)}, u32[]{:S(2)}) copy-start(f32[1024]{0:T(1024)} %reshape.607) | copy-start | bytes 12292
  182.8 17.8 %copy-start.68 = (f32[64]{0:T(128)S(1)}, f32[64]{0:T(128)}, u32[]{:S(2)}) copy-start(f32[64]{0:T(128)} %copy-done.67) | copy-start | bytes 772
  211.2 1.9 copy-start.33
  211.2 1.9 copy-start.43
  212.6 1.2 copy-start.44
  213.9 4.3 %copy-start.26 = (bf16[2,256,1024]{2,1,0:T(8,128)(2,1)S(1)}, bf16[2,256,1024]{2,1,0:T(8,128)(2,1)}, u32[]{:S(2)}) copy-start(bf16[2,256,1024]{2,1,0:T(8,128)(2,1)} %copy-done.24) | copy-start | bytes 3145732
  213.9 4.3 %copy-start.78 = (bf16[512,576]{0,1:T(8,128)(2,1)S(1)}, bf16[512,576]{0,1:T(8,128)(2,1)}, u32[]{:S(2)}) copy-start(bf16[512,576]{0,1:T(8,128)(2,1)} %get-tuple-element.139) | copy-start | bytes 1769476
  220.1 1.8 copy-start.23
  221.9 2.3 copy-start.2
  221.9 2.3 copy-start.7
  221.9 2.3 copy-start.11
  320.2 1.4 copy-start
  322.7 2.1 copy-start.48
  322.7 2.2 copy-start.60
  322.7 2.2 copy-start.71
  324.8 1.0 copy-start.41
  325.1 1.3 copy-start.13
  325.4 1.4 copy-start.39
  325.4 1.4 copy-start.58
  325.4 1.4 copy-start.65
  327.9 3.5 copy-start.66
  328.9 3.9 copy-start.30
  328.9 3.9 copy-start.35
  328.9 3.9 copy-start.45
  328.9 3.9 copy-start.72
  332.8 2.3 copy-start.51
  334.1 2.5 copy-start.61
  335.0 3.1 copy-start.77
  335.0 3.9 copy-start.5
  336.5 2.6 copy-start.28
  339.8 36.8 %copy-start.32 = (f32[256,1024]{1,0:T(8,128)S(1)}, f32[256,1024]{1,0:T(8,128)}, u32[]{:S(2)}) copy-start(f32[256,1024]{1,0:T(8,128)} %copy-done.31) | copy-start | bytes 3145732
  339.8 36.9 %copy-start.74 = (f32[2,128]{1,0:T(2,128)S(1)}, f32[2,128]{1,0:T(2,128)}, u32[]{:S(2)}) copy-start(f32[2,128]{1,0:T(2,128)} %copy-done.73) | copy-start | bytes 3076
  339.8 37.0 %copy-start.37 = (f32[64,1024]{1,0:T(8,128)S(1)}, f32[64,1024]{1,0:T(8,128)}, u32[]{:S(2)}) copy-start(f32[64,1024]{1,0:T(8,128)} %copy-done.36) | copy-start | bytes 786436
  339.8 37.0 %copy-start.53 = (f32[1024]{0:T(1024)S(1)}, f32[1024]{0:T(1024)}, u32[]{:S(2)}) copy-start(f32[1024]{0:T(1024)} %reshape.607) | copy-start | bytes 12292
  339.8 37.0 %copy-start.69 = (f32[64]{0:T(128)S(1)}, f32[64]{0:T(128)}, u32[]{:S(2)}) copy-start(f32[64]{0:T(128)} %copy-done.67) | copy-start | bytes 772
  339.8 37.0 %copy-start.76 = (f32[64]{0:T(128)S(1)}, f32[64]{0:T(128)}, u32[]{:S(2)}) copy-start(f32[64]{0:T(128)} %copy-done.75) | copy-start | bytes 772
  375.3 3.2 copy-start.49
  389.1 4.9 %copy-start.9 = (bf16[32,32,256]{2,1,0:T(8,128)(2,1)S(1)}, bf16[32,32,256]{2,1,0:T(8,128)(2,1)}, u32[]{:S(2)}) copy-start(bf16[32,32,256]{2,1,0:T(8,128)(2,1)} %copy-done.8) | copy-start | bytes 1572868
  389.1 5.6 %copy-start.1 = (bf16[32,32,1152]{2,1,0:T(8,128)(2,1)S(1)}, bf16[32,32,1152]{2,1,0:T(8,128)(2,1)}, u32[]{:S(2)}) copy-start(bf16[32,32,1152]{2,1,0:T(8,128)(2,1)} %copy-done) | copy-start | bytes 7077892
  395.1 2.5 copy-start.63
  395.1 3.6 copy-start.47
  (17 other events, 13.6 us)

commit v2 on v1

--- a/solution.py
+++ b/solution.py
@@ -64,7 +64,7 @@
 
     @pl.loop(1, n)
     def _(i):
-        p = lax.rem(me + i, n)
+        p = lax.rem(me + 5 * i, n)
         pltpu.make_async_remote_copy(
             src_ref=choose(src, p),
             dst_ref=dst.at[me],
@@ -242,16 +242,16 @@
     return token >= key
 
 
-FORWARD_PLAN = (("ctx", "same"), ("ctx", "half"), ("ctx", "half"), ("pair", "same"))
+FORWARD_PLAN = (("ctx", "same"), ("pair", "same"))
 
 
 def forward_body(
-    q_src, kv_src, wo, gu, dn, cot,
-    att, q_buf, kv_buf, o_buf, log_buf, wo_all, gu_all, dn_all, cot_all,
+    q_src, kv_src, wo, cot,
+    att, q_buf, kv_buf, o_buf, log_buf, wo_all, cot_all,
     acc, den, q_send, q_recv, o_send, o_recv, kv_send, kv_recv, *rest,
 ):
     c, t, slot, low, to = places()
-    background = list(zip(FORWARD_PLAN, (wo, gu, dn, cot), (wo_all, gu_all, dn_all, cot_all)))
+    background = list(zip(FORWARD_PLAN, (wo, cot), (wo_all, cot_all)))
     greet(["ctx"])
     to_workers(q_src, q_buf, q_send, q_recv, "start")
     begin("ctx", "plane", kv_src, kv_buf, kv_send, kv_recv)
@@ -288,7 +288,7 @@
         finish(kind, pick, src, dst, rest[2 * k], rest[2 * k + 1])
 
 
-def forward(q_src, kv_src, wo, gu, dn, cot):
+def forward(q_src, kv_src, wo, cot):
     stack = jax.ShapeDtypeStruct((SLOTS, 2 * BLOCK, BLOCK), BF16)
     kinds = [kind for kind, _ in FORWARD_PLAN]
     return pl.pallas_call(
@@ -300,9 +300,9 @@
             stack,
             jax.ShapeDtypeStruct((SLOTS, 2 * BLOCK, BLOCK), F32),
         ]
-        + [landing(k, p, a) for (k, p), a in zip(FORWARD_PLAN, (wo, gu, dn, cot))],
-        in_specs=[ANY] * 6,
-        out_specs=[ANY] + [VMEM] * 4 + [ANY] * 4,
+        + [landing(k, p, a) for (k, p), a in zip(FORWARD_PLAN, (wo, cot))],
+        in_specs=[ANY] * 4,
+        out_specs=[ANY] + [VMEM] * 4 + [ANY] * 2,
         scratch_shapes=[
             pltpu.VMEM((2 * BLOCK, BLOCK), F32),
             pltpu.VMEM((2 * BLOCK, BLOCK), F32),
@@ -313,7 +313,7 @@
             collective_id=2, has_side_effects=True, vmem_limit_bytes=24 * 2**20
         ),
         name="attention_forward",
-    )(q_src, kv_src, wo, gu, dn, cot)
+    )(q_src, kv_src, wo, cot)
 
 
 BACKWARD_PLAN = (("ctx", "own"), ("ctx", "own"), ("ctx", "own"), ("rows", "own"))
@@ -459,8 +459,15 @@
     weight_rows = jnp.concatenate([w_query, key_weight, w_value], axis=1)
     gains = jnp.zeros((16, 128), BF16)
     gains = gains.at[0:2, 0:32].set(norm_gains).at[2:4, 0:2].set(head_gains)
-    weights_all, gains_all = exchange(
-        1, ["ctx"], [("ctx", "same", weight_rows), ("ctx", "same", gains)]
+    ffn_rows = jnp.concatenate([halves(w_gate), halves(w_up), halves(w_down)], axis=2)
+    weights_all, gains_all, ffn_pair = exchange(
+        1,
+        ["ctx"],
+        [("ctx", "same", weight_rows), ("ctx", "same", gains), ("pair", "own", ffn_rows)],
+    )
+    planes = [[2 * g + h for g in range(NCTX // 2)] for h in range(2)]
+    ffn_full = lax.all_gather(
+        ffn_pair.reshape(2 * 32, 3 * unit_half), "ctx", axis_index_groups=planes, tiled=True
     )
     qkv_full = weights_all.reshape(width, weight_rows.shape[1])
     gain_attn = gains_all[:, 0, :32].reshape(width).astype(F32)
@@ -485,15 +492,13 @@
     kv_src = jnp.concatenate([key_rot, values], axis=-1).transpose(2, 0, 1, 3)
     kv_src = kv_src.reshape(PAIRS, tokens, 2 * HEAD_SIZE)
 
-    gu_src = jnp.concatenate([halves(w_gate), halves(w_up)], axis=2)
-    dn_src = halves(w_down)
-    att, q_buf, kv_buf, o_buf, log_buf, wo_all, gu_all, dn_all, cot_all = forward(
-        q_src, kv_src, w_out, gu_src, dn_src, cotangent.reshape(rows, width)
+    att, q_buf, kv_buf, o_buf, log_buf, wo_all, cot_all = forward(
+        q_src, kv_src, w_out, cotangent.reshape(rows, width)
     )
     attended = from_pairs(att[..., HEAD_SIZE:], seqs, 2).reshape(rows, 256)
     out_full = wo_all.reshape(width, 256)
-    gu_full = gu_all.reshape(width, 2 * unit_half)
-    dn_full = dn_all.reshape(width, unit_half)
+    gu_full = ffn_full[:, : 2 * unit_half]
+    dn_full = ffn_full[:, 2 * unit_half :]
     cot_rows = cot_all.reshape(2 * rows, width)
 
     attn_part = last_dims(attended, out_full).astype(BF16)

time: 401 us -> 369 us (0.920)
  Pallas kernels: 307 us -> 262 us
  between operations: 2.03 us -> 15.2 us
  other arithmetic: 34.1 us -> 28.7 us
    pallas_call x1, Pallas kernels: 90.3 us -> 47.9 us  [forward(): pl.pallas_call(forward_body, out_shape=[stack, stack, jax.ShapeDtypeStruc...]
    unnamed x169 -> x131, local copies, waits for them, and re-layouts: 16.6 us -> 12.8 us
  transfers between devices with their start and end apart: 0 -> 1, of which waited for: 0 -> 0; matrix products, arithmetic and copies ran while one was open for 0% -> 4% of each run, Pallas kernels for 0% -> 20%
where the time goes in v2:
time: 369 us; the launch traced here: 367 us
  Pallas kernels  262 us (71%)
  local copies, waits for them, and re-layouts  35.3 us (10%)
  other arithmetic  28.7 us (8%)
  matrix products  25.4 us (7%)
  between operations  15.2 us (4%)
    pallas_call x7, Pallas kernels, exchange(): pl.pallas_call(functools.partial(exchange_body, plan, kinds), out_shape=[...  122 us
    pallas_call x1, Pallas kernels, backward(): pl.pallas_call(backward_body, out_shape=[jax.ShapeDtypeStruct((SLOTS, 2 *...  92.9 us
    pallas_call x1, Pallas kernels, forward(): pl.pallas_call(forward_body, out_shape=[stack, stack, jax.ShapeDtypeStruc...  47.9 us
    unnamed x131, local copies, waits for them, and re-layouts  12.8 us
    dot_general x4, matrix products, first_dims(): lax.dot_general(a, b, (((0,), (0,)), ((), ())), preferred_element_type=F32)  10.4 us
    dot_general x4, matrix products, last_dims(): lax.dot_general(a, b, (((1,), (1,)), ((), ())), preferred_element_type=F32)  7.47 us
  transfers between devices with their start and end apart: 1, of which 0 were waited for; matrix products, arithmetic and copies ran while one was open for 4% of the time, Pallas kernels for 20%

profile of v2, /device:TPU:0, one launch (start us, length us, event | category | flops | bytes accessed | tf_op | source)
XLA Modules:
  0.0 367.0 jit_solution(798227201344224217)
XLA Ops:
  7.2 0.9 slice_bitcast_fusion.11
  8.2 0.9 slice_bitcast_fusion.9
  9.1 0.9 slice_bitcast_fusion.7
  10.7 1.4 pad_maximum_fusion.14.refs_0_
  12.1 0.8 concatenate.63.refs_2_
  12.9 1.5 scatter.21.refs_1_
  15.0 26.8 %exchange1.1 = (bf16[32,32,512]{2,1,0:T(8,128)(2,1)}, bf16[32,16,128]{2,1,0:T(8,128)(2,1)}, bf16[2,32,1728]{2,1,0:T(8,128)(2,1)}) custom-call(bf16[32,512]{1,0:T(8,128)(2,1)} %pad_maximum_fusion.14.refs_0_, bf16[16,128]{1,0:T(8,128)(2,1)} %copy-done.46, bf16[2,32,1728]{2,1,0:T(8,128)(2,1)} %concatenate.63.refs_2_), custom_call_target="tpu_custom_call" | custom-call | tf_op jit(solution)/shard_map/exchange1/pallas_call | solution.py:128
  41.9 1.1 convert_reduce_fusion.9
  44.5 0.7 copy-done.29
  45.5 1.1 convert_reduce_fusion.10
  46.9 0.8 broadcast_multiply_fusion.1
  49.4 47.9 %attention_forward.1 = (bf16[4,256,128]{2,1,0:T(8,128)(2,1)S(1)}, bf16[4,256,128]{2,1,0:T(8,128)(2,1)S(1)}, bf16[32,128,128]{2,1,0:T(8,128)(2,1)S(1)}, bf16[4,25...) custom-call(bf16[4,256,128]{2,1,0:T(8,128)(2,1)S(1)} %pad.35.q_src, ...), custom_call_target="tpu_custom_call" | custom-call | tf_op jit(solution)/shard_map/attention_forward/pallas_call | solution.py:294
  97.3 1.0 copy-done.8
  98.3 0.8 copy-done.10
  100.1 1.1 convolution_convert_fusion.5
  101.2 7.6 %exchange3.1 = bf16[4,64,1024]{2,1,0:T(8,128)(2,1)} custom-call(bf16[4,64,1024]{2,1,0:T(8,128)(2,1)} %bitcast.187), custom_call_target="tpu_custom_call" | custom-call | tf_op jit(solution)/shard_map/exchange3/pallas_call | solution.py:128
  108.9 1.1 convert_reduce_fusion.8
  110.3 0.7 multiply_convert_fusion.7.refs_0_
  111.1 16.9 %exchange4.1 = bf16[8,64,1024]{2,1,0:T(8,128)(2,1)} custom-call(bf16[64,1024]{1,0:T(8,128)(2,1)} %multiply_convert_fusion.7.refs_0_), custom_call_target="tpu_custom_call" | custom-call | tf_op jit(solution)/shard_map/exchange4/pallas_call | solution.py:128
  128.1 0.8 copy.152
  129.6 0.8 copy.146
  131.7 3.6 fusion.2
  135.3 2.1 multiply_convert_fusion.2
  137.4 2.5 fusion.4
  140.0 15.8 %exchange5.1 = bf16[8,64,1024]{2,1,0:T(8,128)(2,1)} custom-call(bf16[8,64,1024]{2,1,0:T(8,128)(2,1)} %bitcast.195), custom_call_target="tpu_custom_call" | custom-call | tf_op jit(solution)/shard_map/exchange5/pallas_call | solution.py:128
  155.8 1.4 convert_reduce_fusion.5
  157.2 0.7 multiply_reduce_fusion.4
  157.9 0.8 fusion.24.refs_0_
  158.7 7.3 %exchange7.1 = bf16[4,64,1024]{2,1,0:T(8,128)(2,1)} custom-call(bf16[64,1024]{1,0:T(8,128)(2,1)} %fusion.24.refs_0_), custom_call_target="tpu_custom_call" | custom-call | tf_op jit(solution)/shard_map/exchange7/pallas_call | solution.py:128
  166.1 1.3 convolution_convert_fusion.6
  167.4 1.4 convolution_convert_fusion.4
  168.8 4.7 %convolution_convert_fusion = bf16[1024,1152]{1,0:T(8,128)(2,1)} fusion(bf16[512,1024]{1,0:T(8,128)(2,1)} %bitcast.194, bf16[512,576]{0,1:T(8,128)(2,1)} %copy-done.61, bf16[512,576]{0,1:T(8,128)(2,1)} %copy-done.60), kind=kOutput, calls=%fused_computation.1 | convolution fusion | flops 1211498496 | bytes 4587520 | tf_op jit(solution)/shard_map/dot_general | solution.py:234
  174.0 2.9 convolution_convert_fusion.1
  176.9 1.7 copy.139
  178.6 2.5 convolution_convert_fusion.3
  181.2 0.9 copy-done.13
  182.1 0.9 copy-done.15
  183.1 92.9 %attention_backward.1 = (bf16[4,256,128]{2,1,0:T(8,128)(2,1)S(1)}, bf16[32,128,128]{2,1,0:T(8,128)(2,1)S(1)}, bf16[32,32,256]{2,1,0:T(8,128)(2,1)S(1)}, bf16[32,...) custom-call(bf16[4,256,128]{2,1,0:T(8,128)(2,1)S(1)} %pad.36.do_src, ...), custom_call_target="tpu_custom_call" | custom-call | tf_op jit(solution)/shard_map/attention_backward/pallas_call | solution.py:370
  276.0 1.4 copy-done
  277.4 1.1 copy-done.3
  278.5 1.0 copy-done.6
  280.0 0.7 reshape.614
  281.2 0.8 copy.149
  282.0 0.8 copy.151
  283.6 0.8 copy.143
  284.5 0.8 copy.145
  285.4 1.1 multiply_reduce_fusion.9
  286.5 1.2 multiply_reduce_fusion.3
  287.7 1.3 multiply_reduce_fusion
  289.0 1.0 copy-done.23
  290.0 1.4 convolution_convert_fusion.2
  295.3 36.6 %exchange8.1 = (bf16[4,64,1024]{2,1,0:T(8,128)(2,1)}, bf16[32,32,512]{2,1,0:T(8,128)(2,1)}, f32[32,8,128]{2,1,0:T(8,128)}, bf16[4,64,1024]{2,1,0:T(8,128)(2,1)}) custom-call(bf16[4,64,1024]{2,1,0:T(8,128)(2,1)} %bitcast.185, bf16[32,32,512]{2,1,0:T(8,128)(2,1)} %bitcast.184, f32[32,8,128]{2,1,0:T(8,128)} %copy-done.33, ...), custom_call_target="tpu_custom_call" | custom-call | tf_op jit(solution)/shard_map/exchange8/pallas_call | solution.py:128
  331.9 1.4 convert_reduce_fusion.3
  334.6 1.1 convert_reduce_fusion.7
  336.5 1.3 multiply_reduce_fusion.2
  338.9 2.0 add_convert_fusion.refs_0_
  340.9 10.6 %exchange9.1 = (bf16[4,64,1024]{2,1,0:T(8,128)(2,1)}, f32[4,8,128]{2,1,0:T(8,128)}) custom-call(bf16[64,1024]{1,0:T(8,128)(2,1)} %add_convert_fusion.refs_0_, f32[8,128]{1,0:T(8,128)} %reduce_sum.242.refs_1_), custom_call_target="tpu_custom_call" | custom-call | tf_op jit(solution)/shard_map/exchange9/pallas_call | solution.py:128
  351.5 0.7 reduce_sum.247
  353.4 2.1 bitcast_convert_fusion
  355.5 0.7 convert_reduce_fusion.6
  357.1 0.8 pad_maximum_fusion.5
  357.8 0.8 pad_maximum_fusion.6
  358.6 0.8 pad_maximum_fusion.7
  359.3 0.8 copy.203
  (217 shorter events, 19.5 us)
Async XLA Ops:
  7.2 35.8 %copy-start.21 = (bf16[2,128,1024]{2,1,0:T(8,128)(2,1)S(1)}, bf16[2,128,1024]{2,1,0:T(8,128)(2,1)}, u32[]{:S(2)}) copy-start(bf16[2,128,1024]{2,1,0:T(8,128)(2,1)} %param.23) | copy-start | bytes 1572868
  7.2 124.5 %all-gather.2.cloned.1.call-start = ((), (), s32[]{:S(2)}) async-start(), calls=%async_computation | async-start | bytes 3899392 | tf_op jit(solution)/shard_map/all_gather | solution.py:469
  14.4 0.6 copy-start.46
  41.8 2.1 copy-start.24
  43.0 1.0 copy-start.37
  44.4 0.8 copy-start.29
  45.5 3.5 copy-start.27
  46.7 83.7 %copy-start.47 = (f32[64]{0:T(128)}, f32[64]{0:T(128)S(1)}, u32[]{:S(2)}) copy-start(f32[64]{0:T(128)S(1)} %reshape.601) | copy-start | bytes 772
  46.9 82.6 %copy-start.41 = (f32[2,128,4]{1,0,2:T(2,128)}, f32[2,128,4]{1,0,2:T(2,128)S(1)}, u32[]{:S(2)}) copy-start(f32[2,128,4]{1,0,2:T(2,128)S(1)} %add_rsqrt_fusion) | copy-start | bytes 12292
  47.6 1.7 copy-start.5
  47.6 1.7 copy-start.16
  48.7 80.1 %copy-start.51 = (f32[64]{0:T(128)}, f32[64]{0:T(128)S(1)}, u32[]{:S(2)}) copy-start(f32[64]{0:T(128)S(1)} %reshape.602) | copy-start | bytes 772
  48.8 79.2 %copy-start.43 = (f32[2,128,2]{1,0,2:T(2,128)}, f32[2,128,2]{1,0,2:T(2,128)S(1)}, u32[]{:S(2)}) copy-start(f32[2,128,2]{1,0,2:T(2,128)S(1)} %add_rsqrt_fusion.1) | copy-start | bytes 6148
  97.3 1.0 copy-start.8
  98.3 0.8 copy-start.10
  99.1 0.7 copy-start.12
  99.1 0.8 copy-start.14
  99.1 36.2 %copy-start.17 = (bf16[2,256,1024]{2,1,0:T(8,128)(2,1)}, bf16[2,256,1024]{2,1,0:T(8,128)(2,1)S(1)}, u32[]{:S(2)}) copy-start(bf16[2,256,1024]{2,1,0:T(8,128)(2,1)S(1)} %get-tuple-element.109) | copy-start | bytes 3145732
  108.9 49.0 %copy-start.39 = (f32[1024]{0:T(1024)}, f32[1024]{0:T(1024)S(1)}, u32[]{:S(2)}) copy-start(f32[1024]{0:T(1024)S(1)} %reshape.603) | copy-start | bytes 12292
  110.3 47.6 %copy-start.19 = (f32[64,1024]{1,0:T(8,128)}, f32[64,1024]{1,0:T(8,128)S(1)}, u32[]{:S(2)}) copy-start(f32[64,1024]{1,0:T(8,128)S(1)} %get-tuple-element.134) | copy-start | bytes 786436
  110.3 47.6 %copy-start.49 = (f32[64]{0:T(128)}, f32[64]{0:T(128)S(1)}, u32[]{:S(2)}) copy-start(f32[64]{0:T(128)S(1)} %add_rsqrt_fusion.3) | copy-start | bytes 772
  131.7 3.6 copy-start.58
  137.4 2.5 copy-start.60
  137.4 2.5 copy-start.61
  157.2 11.6 %copy-start.26 = (f32[64,1024]{1,0:T(8,128)}, f32[64,1024]{1,0:T(8,128)S(1)}, u32[]{:S(2)}) copy-start(f32[64,1024]{1,0:T(8,128)S(1)} %convert_reduce_fusion.5) | copy-start | bytes 786436
  157.9 15.6 %copy-start.55 = (f32[64]{0:T(128)}, f32[64]{0:T(128)S(1)}, u32[]{:S(2)}) copy-start(f32[64]{0:T(128)S(1)} %broadcast_multiply_fusion.5) | copy-start | bytes 772
  168.8 5.1 %copy-start.18 = (bf16[2,256,1024]{2,1,0:T(8,128)(2,1)S(1)}, bf16[2,256,1024]{2,1,0:T(8,128)(2,1)}, u32[]{:S(2)}) copy-start(bf16[2,256,1024]{2,1,0:T(8,128)(2,1)} %copy-done.17) | copy-start | bytes 3145732
  174.0 4.6 %copy-start.59 = (bf16[512,576]{0,1:T(8,128)(2,1)S(1)}, bf16[512,576]{0,1:T(8,128)(2,1)}, u32[]{:S(2)}) copy-start(bf16[512,576]{0,1:T(8,128)(2,1)} %get-tuple-element.137) | copy-start | bytes 1769476
  178.6 2.5 copy-start.2
  178.6 2.5 copy-start.9
  178.6 2.5 copy-start.11
  181.2 1.0 copy-start.13
  182.1 0.9 copy-start.15
  276.0 1.4 copy-start
  277.4 1.1 copy-start.3
  278.5 1.0 copy-start.6
  279.5 1.4 copy-start.35
  279.5 1.5 copy-start.44
  279.5 1.5 copy-start.52
  280.0 3.2 copy-start.28
  280.0 3.2 copy-start.42
  280.0 3.2 copy-start.48
  282.9 2.5 copy-start.30
  282.9 2.5 copy-start.57
  283.0 3.5 copy-start.54
  283.5 4.2 %copy-start.22 = (bf16[2,128,1024]{2,1,0:T(8,128)(2,1)S(1)}, bf16[2,128,1024]{2,1,0:T(8,128)(2,1)}, u32[]{:S(2)}) copy-start(bf16[2,128,1024]{2,1,0:T(8,128)(2,1)} %param.23) | copy-start | bytes 1572868
  283.5 4.1 %copy-start.25 = (bf16[32,32,512]{2,1,0:T(8,128)(2,1)S(1)}, bf16[32,32,512]{2,1,0:T(8,128)(2,1)}, u32[]{:S(2)}) copy-start(bf16[32,32,512]{2,1,0:T(8,128)(2,1)} %get-tuple-element.106) | copy-start | bytes 3145732
  283.5 4.1 %copy-start.32 = (bf16[256,128]{1,0:T(8,128)(2,1)S(1)}, bf16[256,128]{1,0:T(8,128)(2,1)}, u32[]{:S(2)}) copy-start(bf16[256,128]{1,0:T(8,128)(2,1)} %reshape.614) | copy-start | bytes 196612
  283.5 4.1 %copy-start.53 = (f32[256]{0:T(256)S(1)}, f32[256]{0:T(256)}, u32[]{:S(2)}) copy-start(f32[256]{0:T(256)} %get-tuple-element.173) | copy-start | bytes 3076
  286.5 3.5 copy-start.38
  287.7 3.8 %copy-start.45 = (f32[1024]{0:T(1024)S(1)}, f32[1024]{0:T(1024)}, u32[]{:S(2)}) copy-start(f32[1024]{0:T(1024)} %get-tuple-element.127) | copy-start | bytes 12292
  289.0 1.0 copy-start.23
  289.0 3.0 copy-start.7
  289.0 3.2 copy-start.20
  294.6 0.7 copy-start.33
  295.3 43.6 %copy-start.40 = (f32[1024]{0:T(1024)S(1)}, f32[1024]{0:T(1024)}, u32[]{:S(2)}) copy-start(f32[1024]{0:T(1024)} %copy-done.39) | copy-start | bytes 12292
  295.3 43.6 %copy-start.50 = (f32[64]{0:T(128)S(1)}, f32[64]{0:T(128)}, u32[]{:S(2)}) copy-start(f32[64]{0:T(128)} %copy-done.49) | copy-start | bytes 772
  295.3 43.6 %copy-start.56 = (f32[64]{0:T(128)S(1)}, f32[64]{0:T(128)}, u32[]{:S(2)}) copy-start(f32[64]{0:T(128)} %copy-done.55) | copy-start | bytes 772
  331.9 6.3 %copy-start.36 = (f32[32,8,128]{2,1,0:T(8,128)S(1)}, f32[32,8,128]{2,1,0:T(8,128)}, u32[]{:S(2)}) copy-start(f32[32,8,128]{2,1,0:T(8,128)} %get-tuple-element.120) | copy-start | bytes 393220
  335.7 0.7 copy-start.31
  336.5 19.8 %copy-start.1 = (bf16[32,32,1152]{2,1,0:T(8,128)(2,1)S(1)}, bf16[32,32,1152]{2,1,0:T(8,128)(2,1)}, u32[]{:S(2)}) copy-start(bf16[32,32,1152]{2,1,0:T(8,128)(2,1)} %copy-done) | copy-start | bytes 7077892
  355.5 1.3 copy-start.4
  356.5 2.8 copy-start.34
Sparse Core Ops, SparseCore 0:
  42.0 63.5 all-gather.1

commit v3 on v2

--- a/solution.py
+++ b/solution.py
@@ -316,16 +316,15 @@
     )(q_src, kv_src, wo, cot)
 
 
-BACKWARD_PLAN = (("ctx", "own"), ("ctx", "own"), ("ctx", "own"), ("rows", "own"))
+BACKWARD_PLAN = (("rows", "own"),)
 
 
 def backward_body(
-    do_src, q_buf, kv_buf, o_buf, log_buf, wo, gu, dn, ffn,
-    dq_all, dkv_all, wo_all, gu_all, dn_all, ffn_all,
+    do_src, q_buf, kv_buf, o_buf, log_buf, ffn, dq_all, dkv_all, ffn_all,
     do_buf, dq_buf, dkv_buf, acc, dkv, do_send, do_recv, dq_send, dq_recv, kv_send, kv_recv, *rest,
 ):
     c, t, slot, low, to = places()
-    background = list(zip(BACKWARD_PLAN, (wo, gu, dn, ffn), (wo_all, gu_all, dn_all, ffn_all)))
+    background = list(zip(BACKWARD_PLAN, (ffn,), (ffn_all,)))
     greet(["ctx", "rows"])
     to_workers(do_src, do_buf, do_send, do_recv, "start")
     for k, ((kind, pick), src, dst) in enumerate(background):
@@ -365,7 +364,7 @@
         finish(kind, pick, src, dst, rest[2 * k], rest[2 * k + 1])
 
 
-def backward(do_src, q_buf, kv_buf, o_buf, log_buf, wo, gu, dn, ffn):
+def backward(do_src, q_buf, kv_buf, o_buf, log_buf, ffn):
     kinds = [kind for kind, _ in BACKWARD_PLAN]
     return pl.pallas_call(
         backward_body,
@@ -373,9 +372,9 @@
             jax.ShapeDtypeStruct((SLOTS, 2 * BLOCK, BLOCK), BF16),
             jax.ShapeDtypeStruct((NCTX, BLOCK, BLOCK), BF16),
         ]
-        + [landing(k, p, a) for (k, p), a in zip(BACKWARD_PLAN, (wo, gu, dn, ffn))],
-        in_specs=[ANY] + [VMEM] * 4 + [ANY] * 4,
-        out_specs=[ANY] * 6,
+        + [landing(k, p, a) for (k, p), a in zip(BACKWARD_PLAN, (ffn,))],
+        in_specs=[ANY] + [VMEM] * 4 + [ANY],
+        out_specs=[ANY] * 3,
         scratch_shapes=[
             pltpu.VMEM((SLOTS, 2 * BLOCK, BLOCK), BF16),
             pltpu.VMEM((SLOTS, 2 * BLOCK, BLOCK), BF16),
@@ -389,7 +388,140 @@
             collective_id=6, has_side_effects=True, vmem_limit_bytes=24 * 2**20
         ),
         name="attention_backward",
-    )(do_src, q_buf, kv_buf, o_buf, log_buf, wo, gu, dn, ffn)
+    )(do_src, q_buf, kv_buf, o_buf, log_buf, ffn)
+
+
+def row_scale(rows):
+    return lax.rsqrt(jnp.mean(rows * rows, axis=1, keepdims=True) + EPSILON)
+
+
+def row_back(grads, normed, scale, gain):
+    scaled = grads * gain
+    return scale * (scaled - normed * jnp.mean(scaled * normed, axis=1, keepdims=True))
+
+
+def summed(ref):
+    total = ref[0].astype(F32)
+    for k in range(1, ref.shape[0]):
+        total += ref[k].astype(F32)
+    return total
+
+
+def norm_body(
+    parts, inputs, gain, residual, hidden_all, landed, hidden, send0, recv0, send1, recv1
+):
+    greet(["rows"])
+    begin("tp", "own", parts, landed, send0, recv0)
+    finish("tp", "own", parts, landed, send0, recv0)
+    total = inputs[...] + summed(landed)
+    residual[...] = total
+    hidden[...] = (total * row_scale(total) * gain[...]).astype(BF16)
+    begin("rows", "same", hidden, hidden_all, send1, recv1)
+    finish("rows", "same", hidden, hidden_all, send1, recv1)
+
+
+def norm_step(parts, inputs, gain):
+    own, width = inputs.shape
+    return pl.pallas_call(
+        norm_body,
+        out_shape=[
+            jax.ShapeDtypeStruct((own, width), F32),
+            jax.ShapeDtypeStruct((8, own, width), BF16),
+        ],
+        in_specs=[VMEM] * 3,
+        out_specs=[VMEM, ANY],
+        scratch_shapes=[pltpu.VMEM((4, own, width), BF16), pltpu.VMEM((own, width), BF16)]
+        + sems(["tp", "rows"]),
+        compiler_params=pltpu.CompilerParams(collective_id=3, has_side_effects=True),
+        name="norm_step",
+    )(parts, inputs, gain)
+
+
+def norm_back_body(
+    parts, residual, cot, gain, grad_residual, gain_part, grad_all,
+    landed, grad_bf, send0, recv0, send1, recv1,
+):
+    greet(["rows"])
+    begin("rows", "own", parts, landed, send0, recv0)
+    rows = residual[...]
+    scale = row_scale(rows)
+    normed = rows * scale
+    finish("rows", "own", parts, landed, send0, recv0)
+    grads = summed(landed)
+    result = cot[...].astype(F32) + row_back(grads, normed, scale, gain[...])
+    grad_bf[...] = result.astype(BF16)
+    begin("tp", "same", grad_bf, grad_all, send1, recv1)
+    grad_residual[...] = result
+    gain_part[...] = jnp.sum(grads * normed, axis=0, keepdims=True)
+    finish("tp", "same", grad_bf, grad_all, send1, recv1)
+
+
+def norm_back_step(parts, residual, cot, gain):
+    own, width = residual.shape
+    return pl.pallas_call(
+        norm_back_body,
+        out_shape=[
+            jax.ShapeDtypeStruct((own, width), F32),
+            jax.ShapeDtypeStruct((1, width), F32),
+            jax.ShapeDtypeStruct((4, own, width), BF16),
+        ],
+        in_specs=[VMEM] * 4,
+        out_specs=[VMEM, VMEM, ANY],
+        scratch_shapes=[pltpu.VMEM((8, own, width), BF16), pltpu.VMEM((own, width), BF16)]
+        + sems(["rows", "tp"]),
+        compiler_params=pltpu.CompilerParams(collective_id=5, has_side_effects=True),
+        name="norm_back_step",
+    )(parts, residual, cot, gain)
+
+
+def last_body(
+    parts, qkv, gains, output, grad_residual, inputs, gain,
+    qkv_all, output_all, input_all, gain_tp,
+    landed, gain_all, input_bf, gain_sum, *sem,
+):
+    greet(["ctx", "tp"])
+    begin("tp", "own", parts, landed, sem[0], sem[1])
+    begin("ctx", "own", gains, gain_all, sem[2], sem[3])
+    begin("ctx", "own", qkv, qkv_all, sem[4], sem[5])
+    begin("tp", "same", output, output_all, sem[6], sem[7])
+    rows = inputs[...]
+    scale = row_scale(rows)
+    normed = rows * scale
+    finish("tp", "own", parts, landed, sem[0], sem[1])
+    result = grad_residual[...] + row_back(summed(landed), normed, scale, gain[...])
+    input_bf[...] = result.astype(BF16)
+    begin("tp", "same", input_bf, input_all, sem[8], sem[9])
+    finish("ctx", "own", gains, gain_all, sem[2], sem[3])
+    gain_sum[...] = summed(gain_all)
+    begin("tp", "same", gain_sum, gain_tp, sem[10], sem[11])
+    finish("tp", "same", output, output_all, sem[6], sem[7])
+    finish("tp", "same", input_bf, input_all, sem[8], sem[9])
+    finish("tp", "same", gain_sum, gain_tp, sem[10], sem[11])
+    finish("ctx", "own", qkv, qkv_all, sem[4], sem[5])
+
+
+def last_step(parts, qkv, gains, output, grad_residual, inputs, gain):
+    own, width = inputs.shape
+    return pl.pallas_call(
+        last_body,
+        out_shape=[
+            jax.ShapeDtypeStruct(qkv.shape, BF16),
+            jax.ShapeDtypeStruct((4, own, width), BF16),
+            jax.ShapeDtypeStruct((4, own, width), BF16),
+            jax.ShapeDtypeStruct((4, *gains.shape[1:]), F32),
+        ],
+        in_specs=[VMEM, ANY, VMEM, VMEM, VMEM, VMEM, VMEM],
+        out_specs=[ANY] * 4,
+        scratch_shapes=[
+            pltpu.VMEM((4, own, width), BF16),
+            pltpu.VMEM(gains.shape, F32),
+            pltpu.VMEM((own, width), BF16),
+            pltpu.VMEM(gains.shape[1:], F32),
+        ]
+        + sems(["tp", "ctx", "ctx", "tp", "tp", "tp"]),
+        compiler_params=pltpu.CompilerParams(collective_id=8, has_side_effects=True),
+        name="last_step",
+    )(parts, qkv, gains, output, grad_residual, inputs, gain)
 
 
 def rms_scale(rows):
@@ -415,11 +547,6 @@
 def head_back(grads, hatted, scale, gain):
     scaled = grads * gain
     return scale * (scaled - hatted * jnp.mean(scaled * hatted, axis=-1, keepdims=True))
-
-
-def row_back(grads, normed, scale, gain):
-    scaled = grads * gain
-    return scale * (scaled - normed * jnp.mean(scaled * normed, axis=-1, keepdims=True))
 
 
 def to_pairs(rows, heads, left):
@@ -502,12 +629,10 @@
     cot_rows = cot_all.reshape(2 * rows, width)
 
     attn_part = last_dims(attended, out_full).astype(BF16)
-    (attn_parts,) = exchange(3, ["tp"], [("tp", "own", attn_part.reshape(4, own, width))])
-    residual = mine(inputs) + jnp.sum(attn_parts.astype(F32), axis=0)
-    scale_ffn = rms_scale(residual)
-    normed_ffn = residual * scale_ffn
-    hidden_own = (normed_ffn * gain_ffn).astype(BF16)
-    (hidden_all,) = exchange(4, ["rows"], [("rows", "same", hidden_own)])
+    inputs_own = mine(inputs)
+    residual, hidden_all = norm_step(
+        attn_part.reshape(4, own, width), inputs_own, gain_ffn.reshape(1, width)
+    )
     hidden_ffn = hidden_all.reshape(2 * rows, width)
 
     gu_raw = jnp.dot(hidden_ffn, gu_full, preferred_element_type=F32)
@@ -520,12 +645,10 @@
     grad_up_in = grad_units * activated
     grad_gu_in = jnp.concatenate([grad_gate_in, grad_up_in], axis=1).astype(BF16)
     ffn_back = last_dims(grad_gu_in, gu_full).astype(BF16)
-    (back_parts,) = exchange(5, ["rows"], [("rows", "own", ffn_back.reshape(8, own, width))])
-    grad_hidden_ffn = jnp.sum(back_parts.astype(F32), axis=0)
-    ffn_gain_part = jnp.sum(grad_hidden_ffn * normed_ffn, axis=0)
-    cot_own = mine(cotangent.reshape(rows, width)).astype(F32)
-    grad_residual = cot_own + row_back(grad_hidden_ffn, normed_ffn, scale_ffn, gain_ffn)
-    (residual_all,) = exchange(7, ["tp"], [("tp", "same", grad_residual.astype(BF16))])
+    cot_own = mine(cotangent.reshape(rows, width))
+    grad_residual, ffn_gain_part, residual_all = norm_back_step(
+        ffn_back.reshape(8, own, width), residual, cot_own, gain_ffn.reshape(1, width)
+    )
     residual_bf = residual_all.reshape(rows, width)
 
     grad_attended = jnp.dot(residual_bf, out_full, preferred_element_type=F32).astype(BF16)
@@ -534,12 +657,14 @@
     grad_gu = first_dims(hidden_ffn, grad_gu_in).astype(BF16)
     grad_dn = first_dims(cot_rows, hidden_units).astype(BF16)
     ffn_part = last_dims(hidden_units, dn_full).astype(BF16)
-    dq_all, dkv_all, wo_parts, gu_parts, dn_parts, ffn_parts = backward(
-        do_src, q_buf, kv_buf, o_buf, log_buf,
-        grad_out.reshape(NCTX, 32, 256),
-        grad_gu.reshape(NCTX, 32, 2 * unit_half),
-        grad_dn.reshape(NCTX, 32, unit_half),
-        ffn_part.reshape(8, own, width),
+    grads_own = lax.psum_scatter(
+        jnp.concatenate([grad_gu, grad_out, grad_dn], axis=1),
+        "ctx",
+        axis_index_groups=planes,
+        tiled=True,
+    )
+    dq_all, dkv_all, ffn_parts = backward(
+        do_src, q_buf, kv_buf, o_buf, log_buf, ffn_part.reshape(8, own, width)
     )
 
     output_own = (residual + jnp.sum(ffn_parts.astype(F32), axis=0)).astype(BF16)
@@ -562,33 +687,28 @@
     gain_parts = gain_parts.at[:, 1, :32].set(ffn_gain_part.reshape(NCTX, 32))
     gain_parts = gain_parts.at[:, 2, :2].set(query_gain_part.reshape(NCTX, 2))
     gain_parts = gain_parts.at[:, 3, :2].set(key_gain_part.reshape(NCTX, 2))
-    attn_parts, qkv_parts, gain_all, output_all = exchange(
-        8,
-        ["ctx", "tp"],
-        [
-            ("tp", "own", attn_back.astype(BF16).reshape(4, own, width)),
-            ("ctx", "own", grad_qkv.reshape(NCTX, 32, 512)),
-            ("ctx", "own", gain_parts),
-            ("tp", "same", output_own),
-        ],
-    )
-    grad_hidden_attn = jnp.sum(attn_parts.astype(F32), axis=0)
-    input_own = grad_residual + row_back(
-        grad_hidden_attn, mine(normed_attn), mine(scale_attn), gain_attn
-    )
-    input_all, gain_tp = exchange(
-        9,
-        ["tp"],
-        [("tp", "same", input_own.astype(BF16)), ("tp", "same", jnp.sum(gain_all, axis=0))],
-    )
+    qkv_parts, output_all, input_all, gain_tp = last_step(
+        attn_back.astype(BF16).reshape(4, own, width),
+        grad_qkv.reshape(NCTX, 32, 512),
+        gain_parts,
+        output_own,
+        grad_residual,
+        inputs_own,
+        gain_attn.reshape(1, width),
+    )
+    (pair_grads,) = exchange(9, ["pair"], [("pair", "own", grads_own.reshape(2, 32, -1))])
+    pair_grads = pair_grads.astype(F32)
     gain_sum = jnp.sum(gain_tp, axis=0)
     qkv_grad = jnp.sum(qkv_parts.astype(F32), axis=0)
-    out_grad = jnp.sum(wo_parts.astype(F32), axis=0)
-    gu_grad = jnp.sum(gu_parts.reshape(16, 2, 32, 2 * unit_half).astype(F32), axis=0)
-    dn_grad = jnp.sum(dn_parts.reshape(16, 2, 32, unit_half).astype(F32), axis=0)
-    gate_grad = jnp.concatenate([gu_grad[0, :, :unit_half], gu_grad[1, :, :unit_half]], axis=1)
-    up_grad = jnp.concatenate([gu_grad[0, :, unit_half:], gu_grad[1, :, unit_half:]], axis=1)
-    down_grad = jnp.concatenate([dn_grad[0], dn_grad[1]], axis=1)
+    gu, end = 2 * unit_half, 2 * unit_half + 256
+    out_grad = jnp.sum(pair_grads[:, :, gu:end], axis=0)
+
+    def joined(first, last):
+        return jnp.concatenate([pair_grads[0, :, first:last], pair_grads[1, :, first:last]], axis=1)
+
+    gate_grad = joined(0, unit_half)
+    up_grad = joined(unit_half, gu)
+    down_grad = joined(end, end + unit_half)
     return (
         output_all.reshape(seqs, tokens, width),
         input_all.astype(F32).reshape(seqs, tokens, width),

time: 369 us -> 327 us (0.89)
  Pallas kernels: 262 us -> 228 us
  other arithmetic: 28.7 us -> 23.3 us
    pallas_call x7 -> x2, Pallas kernels: 122 us -> 34.2 us  [exchange(): pl.pallas_call(functools.partial(exchange_body, plan, kinds), out_shape=[...]
    pallas_call x0 -> x3, Pallas kernels: none -> 87.4 us  [the longest x1 38.4 us: last_step(): pl.pallas_call(last_body, out_shape=[jax.ShapeDtypeStruct(qkv.shape, BF16...]
    pallas_call x1, Pallas kernels: 92.9 us -> 59.1 us  [backward(): pl.pallas_call(backward_body, out_shape=[jax.ShapeDtypeStruct((SLOTS, 2 *...]
    reduce_sum x9 -> x1, other arithmetic: 7.51 us -> 0.62 us  [local(): out_grad = jnp.sum(pair_grads[:, :, gu:end], axis=0)]
    unnamed x131 -> x101, local copies, waits for them, and re-layouts: 12.8 us -> 7.91 us
    concatenate x3 -> x4, other arithmetic: 2.25 us -> 6.03 us  [the longest x1 3.78 us: local(): jnp.concatenate([grad_gu, grad_out, grad_dn], axis=1)]
  transfers between devices with their start and end apart: 1 -> 2, of which waited for: 0 -> 0; matrix products, arithmetic and copies ran while one was open for 4% -> 12% of each run, Pallas kernels for 20% -> 52%
where the time goes in v3:
time: 327 us; the launch traced here: 325 us
  Pallas kernels  228 us (70%)
  local copies, waits for them, and re-layouts  32.3 us (10%)
  matrix products  26.3 us (8%)
  other arithmetic  23.3 us (7%)
  between operations  15 us (5%)
    pallas_call x1, Pallas kernels, backward(): pl.pallas_call(backward_body, out_shape=[jax.ShapeDtypeStruct((SLOTS, 2 *...  59.1 us
    pallas_call x1, Pallas kernels, forward(): pl.pallas_call(forward_body, out_shape=[stack, stack, jax.ShapeDtypeStruc...  47.5 us
    pallas_call x1, Pallas kernels, last_step(): pl.pallas_call(last_body, out_shape=[jax.ShapeDtypeStruct(qkv.shape, BF16...  38.4 us
    pallas_call x2, Pallas kernels, exchange(): pl.pallas_call(functools.partial(exchange_body, plan, kinds), out_shape=[...  34.2 us
    pallas_call x1, Pallas kernels, norm_step(): pl.pallas_call(norm_body, out_shape=[jax.ShapeDtypeStruct((own, width), F...  24.8 us
    pallas_call x1, Pallas kernels, norm_back_step(): pl.pallas_call(norm_back_body, out_shape=[jax.ShapeDtypeStruct((own, widt...  24.2 us
    dot_general x4, matrix products, first_dims(): lax.dot_general(a, b, (((0,), (0,)), ((), ())), preferred_element_type=F32)  9.54 us
    dot_general x4, matrix products, last_dims(): lax.dot_general(a, b, (((1,), (1,)), ((), ())), preferred_element_type=F32)  8.93 us
  transfers between devices with their start and end apart: 2, of which 0 were waited for; matrix products, arithmetic and copies ran while one was open for 12% of the time, Pallas kernels for 52%

profile of v3, /device:TPU:0, one launch (start us, length us, event | category | flops | bytes accessed | tf_op | source)
XLA Modules:
  0.0 325.2 jit_solution(309224773263726877)
XLA Ops:
  7.2 0.9 slice_bitcast_fusion.11
  8.2 0.9 slice_bitcast_fusion.9
  9.1 0.9 slice_bitcast_fusion.7
  10.0 0.7 scatter.20
  10.7 1.4 pad_maximum_fusion.15.refs_0_
  12.1 0.8 concatenate.66.refs_2_
  12.9 1.5 scatter.21.refs_1_
  14.4 0.6 copy-done.34
  15.0 26.8 %exchange1.1 = (bf16[32,32,512]{2,1,0:T(8,128)(2,1)}, bf16[32,16,128]{2,1,0:T(8,128)(2,1)}, bf16[2,32,1728]{2,1,0:T(8,128)(2,1)}) custom-call(bf16[32,512]{1,0:T(8,128)(2,1)} %pad_maximum_fusion.15.refs_0_, bf16[16,128]{1,0:T(8,128)(2,1)} %copy-done.34, bf16[2,32,1728]{2,1,0:T(8,128)(2,1)} %concatenate.66.refs_2_), custom_call_target="tpu_custom_call" | custom-call | tf_op jit(solution)/shard_map/exchange1/pallas_call | solution.py:128
  41.9 1.6 convert_reduce_fusion.3
  45.1 0.8 copy-done.10
  46.2 1.0 convert_reduce_fusion.4
  47.5 0.8 broadcast_multiply_fusion
  49.8 0.6 copy-done.32
  51.0 47.5 %attention_forward.1 = (bf16[4,256,128]{2,1,0:T(8,128)(2,1)S(1)}, bf16[4,256,128]{2,1,0:T(8,128)(2,1)S(1)}, bf16[32,128,128]{2,1,0:T(8,128)(2,1)S(1)}, bf16[4,25...) custom-call(bf16[4,256,128]{2,1,0:T(8,128)(2,1)S(1)} %pad.35.q_src, ...), custom_call_target="tpu_custom_call" | custom-call | tf_op jit(solution)/shard_map/attention_forward/pallas_call | solution.py:294
  98.6 1.0 copy-done.4
  100.4 1.4 reshape.574.gain
  101.8 1.2 bitcast_convert_fusion.1
  102.9 1.0 copy-done.6
  104.0 0.7 constant_dynamic-slice_fusion.1.inputs
  104.7 1.1 convolution_convert_fusion.5
  105.8 24.8 %norm_step.1 = (f32[64,1024]{1,0:T(8,128)}, bf16[8,64,1024]{2,1,0:T(8,128)(2,1)}) custom-call(bf16[4,64,1024]{2,1,0:T(8,128)(2,1)} %bitcast.168, f32[64,1024]{1,0:T(8,128)} %constant_dynamic-slice_fusion.1.inputs, f32[1,1024]{1,0:T(1,128)} %reshape.574.gain), custom_call_target="tpu_custom_call" | custom-call | tf_op jit(solution)/shard_map/norm_step/pallas_call | solution.py:425
  130.7 0.7 constant_dynamic-slice_fusion.cot
  131.4 3.5 %fusion.2 = f32[512,1152]{0,1:T(8,128)S(1)} fusion(bf16[512,1024]{1,0:T(8,128)(2,1)} %bitcast.204, bf16[1024,1728]{1,0:T(8,128)(2,1)} %all-gather.2.cloned.1.call-done), kind=kOutput, calls=%fused_computation.7 | convolution fusion | flops 1207959552 | bytes 5767168 | tf_op jit(solution)/shard_map/dot_general | solution.py:638
  134.9 3.6 %multiply_convert_fusion.2 = (bf16[512,576]{0,1:T(8,128)(2,1)}, bf16[512,576]{0,1:T(8,128)(2,1)}, bf16[512,576]{0,1:T(8,128)(2,1)S(1)}) fusion(f32[512,1152]{0,1:T(8,128)S(1)} %fusion.2, bf16[512,1024]{1,0:T(8,128)(2,1)S(1)} %bitcast.162, bf16[1024,1728]{1,0:T(8,128)(2,1)} %all-gather.2.cloned.1.call-done), kind=kOutput, calls=%fused_computation.18 | convolution fusion | flops 608403456 | bytes 6488064 | tf_op jit(solution)/shard_map/dot_general | solution.py:643
  138.5 0.8 copy-done.44
  139.4 1.9 convolution_convert_fusion.1
  141.2 2.4 copy.198
  143.6 4.8 %convolution_convert_fusion = bf16[1024,1152]{1,0:T(8,128)(2,1)} fusion(bf16[512,1024]{1,0:T(8,128)(2,1)} %bitcast.205, bf16[512,576]{0,1:T(8,128)(2,1)} %get-tuple-element.132, bf16[512,576]{0,1:T(8,128)(2,1)} %get-tuple-element.131), kind=kOutput, calls=%fused_computation.1 | convolution fusion | flops 1211498496 | bytes 4587520 | tf_op jit(solution)/shard_map/dot_general | solution.py:234
  148.4 2.5 fusion.4
  150.9 24.2 %norm_back_step.1 = (f32[64,1024]{1,0:T(8,128)}, f32[1,1024]{1,0:T(1,128)}, bf16[4,64,1024]{2,1,0:T(8,128)(2,1)}) custom-call(bf16[8,64,1024]{2,1,0:T(8,128)(2,1)} %bitcast.176, f32[64,1024]{1,0:T(8,128)} %get-tuple-element.112.residual, bf16[64,1024]{1,0:T(8,128)(2,1)} %constant_dynamic-slice_fusion.cot, f32[1,1024]{1,0:T(1,128)} %reshape.574.gain), custom_call_target="tpu_custom_call" | custom-call | tf_op jit(solution)/shard_map/norm_back_step/pallas_call | solution.py:461
  175.1 1.4 convolution_convert_fusion.4
  176.5 3.8 %pad_maximum_fusion = bf16[1024,1984]{1,0:T(8,128)(2,1)} fusion(bf16[1024,576]{1,0:T(8,128)(2,1)} %copy.198, bf16[1024,256]{1,0:T(8,128)(2,1)S(1)} %convolution_convert_fusion.4, bf16[1024,1152]{1,0:T(8,128)(2,1)} %convolution_convert_fusion), kind=kLoop, calls=%fused_computation | loop fusion | flops 12189696 | bytes 8126464 | tf_op jit(solution)/shard_map/concatenate | solution.py:661
  180.3 0.6 copy-done.33
  181.1 0.6 mul.409
  181.8 0.8 copy.183
  182.7 0.6 mul.392
  183.3 0.8 slice_convert_fusion.2
  184.2 0.7 reshape.578.gain
  185.6 2.6 convolution_convert_fusion.3
  188.2 59.1 %attention_backward.1 = (bf16[4,256,128]{2,1,0:T(8,128)(2,1)S(1)}, bf16[32,128,128]{2,1,0:T(8,128)(2,1)S(1)}, bf16[8,64,1024]{2,1,0:T(8,128)(2,1)S(1)}) custom-call(bf16[4,256,128]{2,1,0:T(8,128)(2,1)S(1)} %pad.36.do_src, bf16[4,256,128]{2,1,0:T(8,128)(2,1)S(1)} %get-tuple-element.114.q_buf, bf16[32,128,128]{2,1,0:T(8,128)(2,1)S(1)} %get-tuple-element.115.kv_buf, ...), custom_call_target="tpu_custom_call" | custom-call | tf_op jit(solution)/shard_map/attention_backward/pallas_call | solution.py:369
  247.9 0.7 reshape.584
  249.0 0.8 copy.186
  249.9 0.8 copy.188
  252.5 2.7 multiply_reduce_fusion
  255.8 0.7 reduce.38
  257.0 0.6 scatter.25
  257.6 0.6 scatter.26
  258.2 0.6 scatter.29.gains
  258.9 0.7 add_convert_fusion.output
  259.6 1.5 convolution_convert_fusion.2
  261.2 38.4 %last_step.1 = (bf16[32,32,512]{2,1,0:T(8,128)(2,1)}, bf16[4,64,1024]{2,1,0:T(8,128)(2,1)}, bf16[4,64,1024]{2,1,0:T(8,128)(2,1)}, f32[4,8,128]{2,1,0:T(8,128)}) custom-call(bf16[4,64,1024]{2,1,0:T(8,128)(2,1)} %bitcast.195, bf16[32,32,512]{2,1,0:T(8,128)(2,1)} %bitcast.164, f32[32,8,128]{2,1,0:T(8,128)} %copy-done.18, ...), custom_call_target="tpu_custom_call" | custom-call | tf_op jit(solution)/shard_map/last_step/pallas_call | solution.py:505
  299.5 0.7 reduce_sum.147
  301.4 1.4 convert_reduce_fusion.1
  302.8 0.6 slice.328
  303.4 0.6 fusion.26
  304.0 2.2 bitcast_convert_fusion
  306.2 7.4 %exchange9.1 = bf16[2,32,1984]{2,1,0:T(8,128)(2,1)} custom-call(bf16[2,32,1984]{2,1,0:T(8,128)(2,1)} %bitcast.197), custom_call_target="tpu_custom_call" | custom-call | tf_op jit(solution)/shard_map/exchange9/pallas_call | solution.py:128
  313.6 1.0 convert_element_type.183
  314.6 0.6 slice_reduce_fusion
  315.3 0.8 pad_maximum_fusion.6
  316.1 0.8 pad_maximum_fusion.7
  316.8 0.8 pad_maximum_fusion.8
  317.6 0.8 copy.243
  (179 shorter events, 11.3 us)
Async XLA Ops:
  7.2 36.5 %copy-start.8 = (bf16[2,128,1024]{2,1,0:T(8,128)(2,1)S(1)}, bf16[2,128,1024]{2,1,0:T(8,128)(2,1)}, u32[]{:S(2)}) copy-start(bf16[2,128,1024]{2,1,0:T(8,128)(2,1)} %param.23) | copy-start | bytes 1572868
  7.2 124.2 %all-gather.2.cloned.1.call-start = ((), (), s32[]{:S(2)}) async-start(), calls=%async_computation.1 | async-start | bytes 3899392 | tf_op jit(solution)/shard_map/all_gather | solution.py:596
  14.4 0.6 copy-start.34
  41.8 2.8 copy-start.15
  41.9 264.4 %reduce-scatter.2.cloned.1.call-start = ((), (), s32[]{:S(2)}) async-start(), calls=%async_computation.2 | async-start | bytes 4456448 | tf_op jit(solution)/shard_map/reduce_scatter | solution.py:660
  43.6 1.0 copy-start.30
  45.0 0.8 copy-start.10
  47.3 1.1 copy-start.35
  47.5 0.9 copy-start.28
  48.2 2.7 copy-start.22
  48.2 2.8 copy-start
  48.2 2.8 copy-start.3
  49.2 1.8 copy-start.13
  49.3 0.5 copy-start.37
  49.8 0.6 copy-start.32
  98.6 1.0 copy-start.4
  99.5 0.7 copy-start.1
  102.9 1.0 copy-start.6
  131.4 3.5 %copy-start.5 = (bf16[2,256,1024]{2,1,0:T(8,128)(2,1)S(1)}, bf16[2,256,1024]{2,1,0:T(8,128)(2,1)}, u32[]{:S(2)}) copy-start(bf16[2,256,1024]{2,1,0:T(8,128)(2,1)} %copy-done.4) | copy-start | bytes 3145732
  138.5 0.8 copy-start.44
  143.6 4.8 %copy-start.43 = (bf16[1024,1728]{1,0:T(8,128)(2,1)S(1)}, bf16[1024,1728]{1,0:T(8,128)(2,1)}, u32[]{:S(2)}) copy-start(bf16[1024,1728]{1,0:T(8,128)(2,1)} %all-gather.2.cloned.1.call-done) | copy-start | bytes 10616836
  143.6 4.8 %copy-start.45 = (bf16[512,576]{0,1:T(8,128)(2,1)S(1)}, bf16[512,576]{0,1:T(8,128)(2,1)}, u32[]{:S(2)}) copy-start(bf16[512,576]{0,1:T(8,128)(2,1)} %get-tuple-element.131) | copy-start | bytes 1769476
  143.6 4.8 %copy-start.46 = (bf16[512,576]{0,1:T(8,128)(2,1)S(1)}, bf16[512,576]{0,1:T(8,128)(2,1)}, u32[]{:S(2)}) copy-start(bf16[512,576]{0,1:T(8,128)(2,1)} %get-tuple-element.132) | copy-start | bytes 1769476
  180.3 0.7 copy-start.33
  180.3 0.8 copy-start.38
  180.3 1.4 copy-start.29
  180.3 2.4 copy-start.36
  180.3 4.5 %copy-start.12 = (bf16[4,64,1024]{2,1,0:T(8,128)(2,1)S(1)}, bf16[4,64,1024]{2,1,0:T(8,128)(2,1)}, u32[]{:S(2)}) copy-start(bf16[4,64,1024]{2,1,0:T(8,128)(2,1)} %get-tuple-element.113) | copy-start | bytes 1572868
  185.6 2.6 copy-start.2
  247.3 1.4 copy-start.23
  247.3 1.4 copy-start.27
  247.3 1.5 copy-start.14
  250.7 1.1 copy-start.11
  250.8 1.1 copy-start.20
  250.8 1.1 copy-start.21
  250.8 1.1 copy-start.42
  250.8 1.2 copy-start.17
  250.8 1.2 copy-start.40
  251.4 1.1 copy-start.9
  251.4 1.1 copy-start.39
  252.0 3.2 copy-start.25
  252.0 3.8 %copy-start.41 = (f32[1,1024]{1,0:T(1,128)S(1)}, f32[1,1024]{1,0:T(1,128)}, u32[]{:S(2)}) copy-start(f32[1,1024]{1,0:T(1,128)} %get-tuple-element.120) | copy-start | bytes 12292
  252.5 6.4 %copy-start.16 = (f32[64,1024]{1,0:T(8,128)S(1)}, f32[64,1024]{1,0:T(8,128)}, u32[]{:S(2)}) copy-start(f32[64,1024]{1,0:T(8,128)} %get-tuple-element.112.residual) | copy-start | bytes 786436
  252.5 7.1 %copy-start.7 = (f32[256,1024]{1,0:T(8,128)S(1)}, f32[256,1024]{1,0:T(8,128)}, u32[]{:S(2)}) copy-start(f32[256,1024]{1,0:T(8,128)} %copy-done.6) | copy-start | bytes 3145732
  252.5 7.1 %copy-start.24 = (bf16[256,128]{1,0:T(8,128)(2,1)S(1)}, bf16[256,128]{1,0:T(8,128)(2,1)}, u32[]{:S(2)}) copy-start(bf16[256,128]{1,0:T(8,128)(2,1)} %reshape.584) | copy-start | bytes 196612
  252.5 7.1 %copy-start.31 = (f32[1024]{0:T(1024)S(1)}, f32[1024]{0:T(1024)}, u32[]{:S(2)}) copy-start(f32[1024]{0:T(1024)} %copy-done.30) | copy-start | bytes 12292
  255.2 4.5 %copy-start.26 = (bf16[256,128]{1,0:T(8,128)(2,1)S(1)}, bf16[256,128]{1,0:T(8,128)(2,1)}, u32[]{:S(2)}) copy-start(bf16[256,128]{1,0:T(8,128)(2,1)} %copy-done.25) | copy-start | bytes 196612
  258.7 2.4 copy-start.18
  304.0 13.6 %copy-start.19 = (bf16[4,64,1024]{2,1,0:T(8,128)(2,1)S(1)}, bf16[4,64,1024]{2,1,0:T(8,128)(2,1)}, u32[]{:S(2)}) copy-start(bf16[4,64,1024]{2,1,0:T(8,128)(2,1)} %get-tuple-element.123) | copy-start | bytes 1572868
Sparse Core Ops, SparseCore 0:
  42.0 64.0 all-gather.1
  180.5 100.3 reduce-scatter.1

commit v4 on v3

--- a/solution.py
+++ b/solution.py
@@ -31,6 +31,15 @@
         return 4, t, lambda p: (c, p)
     if kind == "pair":
         return 2, h, lambda p: (c - h + p, t)
+    z, x, core = c // 8, lax.rem(c // 2, 4), lax.rem(t, 2)
+    if kind == "z":
+        return 4, z, lambda p: (c + (p - z) * 8, t)
+    if kind == "x":
+        return 4, x, lambda p: (c + (p - x) * 2, t)
+    if kind == "core":
+        return 2, core, lambda p: (c, t - core + p)
+    if kind == "ring":
+        return 4, h * 2 + t // 2, lambda p: (c - h + p // 2, lax.rem(p, 2) * 2 + core)
     return 8, h * 4 + t, lambda p: (c - h + p // 4, lax.rem(p, 4))
 
 
@@ -98,7 +107,110 @@
     pltpu.make_async_copy(choose(src, me), dst.at[me], recv.at[me]).wait()
 
 
-SIZES = {"ctx": NCTX, "tp": 4, "pair": 2, "rows": 8}
+def push(kind, src_of, dst_of, send, recv, local=False):
+    n, me, dev = group(kind)
+
+    @pl.loop(1, n)
+    def _(i):
+        p = lax.rem(me + i, n)
+        pltpu.make_async_remote_copy(
+            src_ref=src_of(p),
+            dst_ref=dst_of(me),
+            send_sem=send.at[p],
+            recv_sem=recv.at[me],
+            device_id=dev(p),
+            device_id_type=MESH,
+        ).start()
+
+    if local:
+        pltpu.make_async_copy(src_of(me), dst_of(me), recv.at[me]).start()
+
+
+def settle(kind, src_of, dst_of, send, recv, local=False):
+    n, me, dev = group(kind)
+
+    @pl.loop(1, n)
+    def _(i):
+        p = lax.rem(me + i, n)
+        copy = pltpu.make_async_remote_copy(
+            src_ref=src_of(p),
+            dst_ref=dst_of(p),
+            send_sem=send.at[p],
+            recv_sem=recv.at[p],
+            device_id=dev(p),
+            device_id_type=MESH,
+        )
+        copy.wait_send()
+        copy.wait_recv()
+
+    if local:
+        pltpu.make_async_copy(src_of(me), dst_of(me), recv.at[me]).wait()
+
+
+def stage(*moves):
+    for move in moves:
+        push(*move)
+    for move in moves:
+        settle(*move)
+
+
+class Sems:
+    def __init__(self, refs):
+        self.refs = list(refs)
+
+    def two(self):
+        return self.refs.pop(0), self.refs.pop(0)
+
+
+def position():
+    c = lax.axis_index("ctx")
+    return c // 8, lax.rem(c // 2, 4), lax.rem(c, 2)
+
+
+SIZES = {"ctx": NCTX, "tp": 4, "pair": 2, "rows": 8, "z": 4, "x": 4, "core": 2, "ring": 4}
+
+
+def gather_body(w, gains, ffn, w_all, gains_all, ffn_pair, *sem):
+    z, x, h = position()
+    take = Sems(sem)
+    greet(["z", "x", "pair"])
+    swap = ("pair", lambda p: ffn.at[p], lambda q: ffn_pair.at[q], *take.two(), True)
+    first = [
+        ("pair", lambda p: w, lambda q: w_all.at[z, x, q], *take.two(), True),
+        ("pair", lambda p: gains, lambda q: gains_all.at[z, x, q], *take.two(), True),
+    ]
+    for move in first:
+        push(*move)
+    push(*swap)
+    for move in first:
+        settle(*move)
+    stage(
+        ("x", lambda p: w_all.at[z, x, :, 0], lambda q: w_all.at[z, q, :, 0], *take.two()),
+        ("z", lambda p: w_all.at[z, x, :, 1], lambda q: w_all.at[q, x, :, 1], *take.two()),
+        ("x", lambda p: gains_all.at[z, x], lambda q: gains_all.at[z, q], *take.two()),
+    )
+    stage(
+        ("z", lambda p: w_all.at[z, :, :, 0], lambda q: w_all.at[q, :, :, 0], *take.two()),
+        ("x", lambda p: w_all.at[:, x, :, 1], lambda q: w_all.at[:, q, :, 1], *take.two()),
+        ("z", lambda p: gains_all.at[z], lambda q: gains_all.at[q], *take.two()),
+    )
+    settle(*swap)
+
+
+def gather(w, gains, ffn):
+    return pl.pallas_call(
+        gather_body,
+        out_shape=[
+            jax.ShapeDtypeStruct((4, 4, 2, *w.shape), BF16),
+            jax.ShapeDtypeStruct((4, 4, 2, *gains.shape), BF16),
+            jax.ShapeDtypeStruct(ffn.shape, BF16),
+        ],
+        in_specs=[ANY] * 3,
+        out_specs=[VMEM, VMEM, ANY],
+        scratch_shapes=sems(["pair"] * 3 + ["x", "z", "x", "z", "x", "z"]),
+        compiler_params=pltpu.CompilerParams(collective_id=1, has_side_effects=True),
+        name="gather",
+    )(w, gains, ffn)
 
 
 def piece_shape(pick, array):
@@ -145,6 +257,31 @@
 
 def block_of(low, j):
     return j * WORKERS + (low if j % 2 == 0 else WORKERS - 1 - low)
+
+
+def greet_attention(kinds):
+    c, t, slot, low, to = places()
+    barrier = pltpu.get_barrier_semaphore()
+    total = 0
+    others = [p * WORKERS + to for p in range(PAIRS)] + [block_of(low, j) for j in range(SLOTS)]
+    for other in others:
+
+        @pl.when(other != c)
+        def _():
+            pl.semaphore_signal(barrier, inc=1, device_id=(other, t), device_id_type=MESH)
+
+        total = total + jnp.where(other != c, 1, 0)
+    for kind in kinds:
+        n, me, dev = group(kind)
+
+        @pl.loop(1, n)
+        def _(i):
+            pl.semaphore_signal(
+                barrier, inc=1, device_id=dev(lax.rem(me + i, n)), device_id_type=MESH
+            )
+
+        total = total + (n - 1)
+    pl.semaphore_wait(barrier, total)
 
 
 def to_workers(src, dst, send, recv, act):
@@ -242,24 +379,43 @@
     return token >= key
 
 
-FORWARD_PLAN = (("ctx", "same"), ("pair", "same"))
-
-
 def forward_body(
-    q_src, kv_src, wo, cot,
-    att, q_buf, kv_buf, o_buf, log_buf, wo_all, cot_all,
-    acc, den, q_send, q_recv, o_send, o_recv, kv_send, kv_recv, *rest,
+    q_src, kv_src, wo, cot, att, q_buf, kv_buf, o_buf, log_buf, wo_all, cot_all,
+    acc, den, q_send, q_recv, o_send, o_recv, *sem,
 ):
     c, t, slot, low, to = places()
-    background = list(zip(FORWARD_PLAN, (wo, cot), (wo_all, cot_all)))
-    greet(["ctx"])
+    z, x, h = position()
+    take = Sems(sem)
+    greet_attention(["z", "x", "pair"])
+    near = ("z", lambda p: kv_src.at[p], lambda q: kv_buf.at[q, x, h], *take.two(), True)
+    out_first = ("pair", lambda p: wo, lambda q: wo_all.at[z, x, q], *take.two(), True)
+    push(*near)
     to_workers(q_src, q_buf, q_send, q_recv, "start")
-    begin("ctx", "plane", kv_src, kv_buf, kv_send, kv_recv)
-    for k, ((kind, pick), src, dst) in enumerate(background):
-        begin(kind, pick, src, dst, rest[2 * k], rest[2 * k + 1])
+    push(*out_first)
+    settle(*near)
+    stage(
+        ("x", lambda p: kv_buf.at[:, x, h, 0], lambda q: kv_buf.at[:, q, h, 0], *take.two()),
+        ("pair", lambda p: kv_buf.at[:, x, h, 1], lambda q: kv_buf.at[:, x, q, 1], *take.two()),
+    )
+    stage(
+        ("pair", lambda p: kv_buf.at[:, :, h, 0], lambda q: kv_buf.at[:, :, q, 0], *take.two()),
+        ("x", lambda p: kv_buf.at[:, x, :, 1], lambda q: kv_buf.at[:, q, :, 1], *take.two()),
+    )
+    settle(*out_first)
+    out_second = [
+        ("x", lambda p: wo_all.at[z, x, :, 0], lambda q: wo_all.at[z, q, :, 0], *take.two()),
+        ("z", lambda p: wo_all.at[z, x, :, 1], lambda q: wo_all.at[q, x, :, 1], *take.two()),
+    ]
+    out_third = [
+        ("z", lambda p: wo_all.at[z, :, :, 0], lambda q: wo_all.at[q, :, :, 0], *take.two()),
+        ("x", lambda p: wo_all.at[:, x, :, 1], lambda q: wo_all.at[:, q, :, 1], *take.two()),
+    ]
+    swap = ("pair", lambda p: cot, lambda q: cot_all.at[q], *take.two(), True)
+    for move in out_second:
+        push(*move)
+    push(*swap)
     to_workers(q_src, q_buf, q_send, q_recv, "wait")
     from_owners(q_src, q_buf, q_send, q_recv)
-    finish("ctx", "plane", kv_src, kv_buf, kv_send, kv_recv)
     lanes = lax.broadcasted_iota(jnp.int32, (2 * BLOCK, BLOCK), 1)
     for j in range(SLOTS):
         b = block_of(low, j)
@@ -268,7 +424,7 @@
 
         def chunk(i, masked):
             q = q_buf[j]
-            kv = kv_buf[pl.ds(2 * i, 2)].reshape(2 * BLOCK, BLOCK)
+            kv = kv_buf[i // 4, lax.rem(i, 4)].reshape(2 * BLOCK, BLOCK)
             powered = jnp.exp(last_dims(q, kv))
             if masked:
                 powered = jnp.where(causal_mask(b, i), powered, 0.0)
@@ -281,34 +437,40 @@
         o_buf[j] = jnp.where(lanes >= HEAD_SIZE, acc[...] / total, 0.0).astype(BF16)
         log_buf[j] = jnp.broadcast_to(jnp.log(total), (2 * BLOCK, BLOCK))
         to_owner(o_buf, att, o_send, o_recv, j, "start")
+        if j == 1:
+            for move in out_second:
+                settle(*move)
+            for move in out_third:
+                push(*move)
     for j in range(SLOTS):
         to_owner(o_buf, att, o_send, o_recv, j, "wait")
     from_workers(o_buf, att, o_send, o_recv)
-    for k, ((kind, pick), src, dst) in enumerate(background):
-        finish(kind, pick, src, dst, rest[2 * k], rest[2 * k + 1])
+    for move in out_third:
+        settle(*move)
+    settle(*swap)
 
 
 def forward(q_src, kv_src, wo, cot):
     stack = jax.ShapeDtypeStruct((SLOTS, 2 * BLOCK, BLOCK), BF16)
-    kinds = [kind for kind, _ in FORWARD_PLAN]
     return pl.pallas_call(
         forward_body,
         out_shape=[
             stack,
             stack,
-            jax.ShapeDtypeStruct((NCTX, BLOCK, BLOCK), BF16),
+            jax.ShapeDtypeStruct((4, 4, 2, 2, BLOCK // 2, BLOCK), BF16),
             stack,
             jax.ShapeDtypeStruct((SLOTS, 2 * BLOCK, BLOCK), F32),
-        ]
-        + [landing(k, p, a) for (k, p), a in zip(FORWARD_PLAN, (wo, cot))],
+            jax.ShapeDtypeStruct((4, 4, 2, *wo.shape), BF16),
+            jax.ShapeDtypeStruct((2, *cot.shape), BF16),
+        ],
         in_specs=[ANY] * 4,
-        out_specs=[ANY] + [VMEM] * 4 + [ANY] * 2,
+        out_specs=[ANY] + [VMEM] * 5 + [ANY],
         scratch_shapes=[
             pltpu.VMEM((2 * BLOCK, BLOCK), F32),
             pltpu.VMEM((2 * BLOCK, BLOCK), F32),
         ]
         + [pltpu.SemaphoreType.DMA((SLOTS,))] * 4
-        + sems(["ctx"] + kinds),
+        + sems(["z", "pair", "x", "pair", "pair", "x", "x", "z", "z", "x", "pair"]),
         compiler_params=pltpu.CompilerParams(
             collective_id=2, has_side_effects=True, vmem_limit_bytes=24 * 2**20
         ),
@@ -316,19 +478,18 @@
     )(q_src, kv_src, wo, cot)
 
 
-BACKWARD_PLAN = (("rows", "own"),)
-
-
 def backward_body(
     do_src, q_buf, kv_buf, o_buf, log_buf, ffn, dq_all, dkv_all, ffn_all,
-    do_buf, dq_buf, dkv_buf, acc, dkv, do_send, do_recv, dq_send, dq_recv, kv_send, kv_recv, *rest,
+    do_buf, dq_buf, dkv_buf, acc, dkv, one_a, one_b, sum_a, sum_b, two_a, two_b, sum_all,
+    do_send, do_recv, dq_send, dq_recv, *sem,
 ):
     c, t, slot, low, to = places()
-    background = list(zip(BACKWARD_PLAN, (ffn,), (ffn_all,)))
-    greet(["ctx", "rows"])
+    z, x, h = position()
+    take = Sems(sem)
+    greet_attention(["z", "x", "rows"])
     to_workers(do_src, do_buf, do_send, do_recv, "start")
-    for k, ((kind, pick), src, dst) in enumerate(background):
-        begin(kind, pick, src, dst, rest[2 * k], rest[2 * k + 1])
+    ffn_sems = take.two()
+    begin("rows", "own", ffn, ffn_all, *ffn_sems)
     dkv[...] = jnp.zeros_like(dkv)
     to_workers(do_src, do_buf, do_send, do_recv, "wait")
     from_owners(do_src, do_buf, do_send, do_recv)
@@ -339,7 +500,7 @@
 
         def chunk(i, masked):
             q, do = q_buf[j], do_buf[j]
-            kv = kv_buf[pl.ds(2 * i, 2)].reshape(2 * BLOCK, BLOCK)
+            kv = kv_buf[i // 4, lax.rem(i, 4)].reshape(2 * BLOCK, BLOCK)
             logs = log_buf[j]
             scores = last_dims(q, kv)
             probs = jnp.exp(scores - jnp.concatenate([logs, logs], axis=1))
@@ -348,42 +509,59 @@
             grads = (probs * (last_dims(do, kv) - delta)).astype(BF16)
             acc[...] += jnp.dot(grads, kv, preferred_element_type=F32)
             update = first_dims(grads, q) + first_dims(probs.astype(BF16), do)
-            dkv[pl.ds(2 * i, 2)] += update.reshape(2, BLOCK, BLOCK)
+            dkv[i // 4, lax.rem(i, 4)] += update.reshape(2, 2, BLOCK // 2, BLOCK)
 
         pl.loop(0, b // 2)(lambda i: chunk(i, False))
         chunk(b // 2, True)
         dq_buf[j] = (acc[...] * (HEAD_SIZE**-0.5)).astype(BF16)
         to_owner(dq_buf, dq_all, dq_send, dq_recv, j, "start")
     dkv_buf[...] = dkv[...].astype(BF16)
-    begin("ctx", "own", dkv_buf, dkv_all, kv_send, kv_recv)
+    stage(
+        ("x", lambda p: dkv_buf.at[:, p, :, 0], lambda q: one_a.at[q], *take.two(), True),
+        ("pair", lambda p: dkv_buf.at[:, :, p, 1], lambda q: one_b.at[q], *take.two(), True),
+    )
+    sum_a[...] = summed(one_a).astype(BF16)
+    sum_b[...] = summed(one_b).astype(BF16)
+    stage(
+        ("pair", lambda p: sum_a.at[:, p], lambda q: two_a.at[q], *take.two(), True),
+        ("x", lambda p: sum_b.at[:, p], lambda q: two_b.at[q], *take.two(), True),
+    )
+    sum_all[:, 0] = summed(two_a).astype(BF16)
+    sum_all[:, 1] = summed(two_b).astype(BF16)
+    stage(("z", lambda p: sum_all.at[p], lambda q: dkv_all.at[q], *take.two(), True))
     for j in range(SLOTS):
         to_owner(dq_buf, dq_all, dq_send, dq_recv, j, "wait")
     from_workers(dq_buf, dq_all, dq_send, dq_recv)
-    finish("ctx", "own", dkv_buf, dkv_all, kv_send, kv_recv)
-    for k, ((kind, pick), src, dst) in enumerate(background):
-        finish(kind, pick, src, dst, rest[2 * k], rest[2 * k + 1])
+    finish("rows", "own", ffn, ffn_all, *ffn_sems)
 
 
 def backward(do_src, q_buf, kv_buf, o_buf, log_buf, ffn):
-    kinds = [kind for kind, _ in BACKWARD_PLAN]
+    half = BLOCK // 2
     return pl.pallas_call(
         backward_body,
         out_shape=[
             jax.ShapeDtypeStruct((SLOTS, 2 * BLOCK, BLOCK), BF16),
-            jax.ShapeDtypeStruct((NCTX, BLOCK, BLOCK), BF16),
-        ]
-        + [landing(k, p, a) for (k, p), a in zip(BACKWARD_PLAN, (ffn,))],
+            jax.ShapeDtypeStruct((PAIRS, 2, half, BLOCK), BF16),
+            landing("rows", "own", ffn),
+        ],
         in_specs=[ANY] + [VMEM] * 4 + [ANY],
         out_specs=[ANY] * 3,
         scratch_shapes=[
             pltpu.VMEM((SLOTS, 2 * BLOCK, BLOCK), BF16),
             pltpu.VMEM((SLOTS, 2 * BLOCK, BLOCK), BF16),
-            pltpu.VMEM((NCTX, BLOCK, BLOCK), BF16),
+            pltpu.VMEM((4, 4, 2, 2, half, BLOCK), BF16),
             pltpu.VMEM((2 * BLOCK, BLOCK), F32),
-            pltpu.VMEM((NCTX, BLOCK, BLOCK), F32),
+            pltpu.VMEM((4, 4, 2, 2, half, BLOCK), F32),
+            pltpu.VMEM((4, 4, 2, half, BLOCK), BF16),
+            pltpu.VMEM((2, 4, 4, half, BLOCK), BF16),
+            pltpu.VMEM((4, 2, half, BLOCK), BF16),
+            pltpu.VMEM((4, 4, half, BLOCK), BF16),
+            pltpu.VMEM((2, 4, half, BLOCK), BF16),
+            pltpu.VMEM((4, 4, half, BLOCK), BF16),
+            pltpu.VMEM((4, 2, half, BLOCK), BF16),
         ]
         + [pltpu.SemaphoreType.DMA((SLOTS,))] * 4
-        + sems(["ctx"] + kinds),
+        + sems(["rows", "x", "pair", "pair", "x", "z"]),
         compiler_params=pltpu.CompilerParams(
             collective_id=6, has_side_effects=True, vmem_limit_bytes=24 * 2**20
         ),
@@ -408,16 +586,18 @@
 
 
 def norm_body(
-    parts, inputs, gain, residual, hidden_all, landed, hidden, send0, recv0, send1, recv1
+    parts, inputs, gain, residual, hidden_all, landed, hidden,
+    send0, recv0, send1, recv1, send2, recv2,
 ):
-    greet(["rows"])
+    greet(["tp", "ring"])
     begin("tp", "own", parts, landed, send0, recv0)
     finish("tp", "own", parts, landed, send0, recv0)
     total = inputs[...] + summed(landed)
     residual[...] = total
     hidden[...] = (total * row_scale(total) * gain[...]).astype(BF16)
-    begin("rows", "same", hidden, hidden_all, send1, recv1)
-    finish("rows", "same", hidden, hidden_all, send1, recv1)
+    core = lax.rem(lax.axis_index("tp"), 2)
+    stage(("ring", lambda p: hidden, lambda q: hidden_all.at[q, core], send1, recv1, True))
+    stage(("core", lambda p: hidden_all.at[:, core], lambda q: hidden_all.at[:, q], send2, recv2))
 
 
 def norm_step(parts, inputs, gain):
@@ -426,12 +606,12 @@
         norm_body,
         out_shape=[
             jax.ShapeDtypeStruct((own, width), F32),
-            jax.ShapeDtypeStruct((8, own, width), BF16),
+            jax.ShapeDtypeStruct((4, 2, own, width), BF16),
         ],
         in_specs=[VMEM] * 3,
-        out_specs=[VMEM, ANY],
+        out_specs=[VMEM, VMEM],
         scratch_shapes=[pltpu.VMEM((4, own, width), BF16), pltpu.VMEM((own, width), BF16)]
-        + sems(["tp", "rows"]),
+        + sems(["tp", "ring", "core"]),
         compiler_params=pltpu.CompilerParams(collective_id=3, has_side_effects=True),
         name="norm_step",
     )(parts, inputs, gain)
@@ -439,14 +619,17 @@
 
 def norm_back_body(
     parts, residual, cot, gain, grad_residual, gain_part, grad_all,
-    landed, grad_bf, send0, recv0, send1, recv1,
+    halved, chip, landed, grad_bf, send0, recv0, send1, recv1, send2, recv2,
 ):
-    greet(["rows"])
-    begin("rows", "own", parts, landed, send0, recv0)
+    greet(["tp", "ring"])
+    both = ("core", lambda p: parts.at[:, p], lambda q: halved.at[q], send2, recv2, True)
+    push(*both)
     rows = residual[...]
     scale = row_scale(rows)
     normed = rows * scale
-    finish("rows", "own", parts, landed, send0, recv0)
+    settle(*both)
+    chip[...] = summed(halved).astype(BF16)
+    stage(("ring", lambda p: chip.at[p], lambda q: landed.at[q], send0, recv0, True))
     grads = summed(landed)
     result = cot[...].astype(F32) + row_back(grads, normed, scale, gain[...])
     grad_bf[...] = result.astype(BF16)
@@ -467,8 +650,13 @@
         ],
         in_specs=[VMEM] * 4,
         out_specs=[VMEM, VMEM, ANY],
-        scratch_shapes=[pltpu.VMEM((8, own, width), BF16), pltpu.VMEM((own, width), BF16)]
-        + sems(["rows", "tp"]),
+        scratch_shapes=[
+            pltpu.VMEM((2, 4, own, width), BF16),
+            pltpu.VMEM((4, own, width), BF16),
+            pltpu.VMEM((4, own, width), BF16),
+            pltpu.VMEM((own, width), BF16),
+        ]
+        + sems(["ring", "tp", "core"]),
         compiler_params=pltpu.CompilerParams(collective_id=5, has_side_effects=True),
         name="norm_back_step",
     )(parts, residual, cot, gain)
@@ -476,50 +664,84 @@
 
 def last_body(
     parts, qkv, gains, output, grad_residual, inputs, gain,
-    qkv_all, output_all, input_all, gain_tp,
-    landed, gain_all, input_bf, gain_sum, *sem,
+    qkv_grad, output_all, input_all, gain_tp,
+    landed, input_bf, one_a, one_b, one_g, sum_a, sum_b, sum_g, two_a, two_b, two_g,
+    part_a, part_b, part_g, three_a, three_b, three_g, gain_sum, *sem,
 ):
-    greet(["ctx", "tp"])
-    begin("tp", "own", parts, landed, sem[0], sem[1])
-    begin("ctx", "own", gains, gain_all, sem[2], sem[3])
-    begin("ctx", "own", qkv, qkv_all, sem[4], sem[5])
-    begin("tp", "same", output, output_all, sem[6], sem[7])
+    take = Sems(sem)
+    greet(["z", "x", "pair", "tp"])
+    rows_sums, rows_output, rows_input, gains_out = [take.two() for _ in range(4)]
+    begin("tp", "own", parts, landed, *rows_sums)
+    first = [
+        ("x", lambda p: qkv.at[:, p, :, 0], lambda q: one_a.at[q], *take.two(), True),
+        ("z", lambda p: qkv.at[p, :, :, 1], lambda q: one_b.at[q], *take.two(), True),
+        ("x", lambda p: gains.at[:, p], lambda q: one_g.at[q], *take.two(), True),
+    ]
+    for move in first:
+        push(*move)
     rows = inputs[...]
     scale = row_scale(rows)
     normed = rows * scale
-    finish("tp", "own", parts, landed, sem[0], sem[1])
+    finish("tp", "own", parts, landed, *rows_sums)
     result = grad_residual[...] + row_back(summed(landed), normed, scale, gain[...])
     input_bf[...] = result.astype(BF16)
-    begin("tp", "same", input_bf, input_all, sem[8], sem[9])
-    finish("ctx", "own", gains, gain_all, sem[2], sem[3])
-    gain_sum[...] = summed(gain_all)
-    begin("tp", "same", gain_sum, gain_tp, sem[10], sem[11])
-    finish("tp", "same", output, output_all, sem[6], sem[7])
-    finish("tp", "same", input_bf, input_all, sem[8], sem[9])
-    finish("tp", "same", gain_sum, gain_tp, sem[10], sem[11])
-    finish("ctx", "own", qkv, qkv_all, sem[4], sem[5])
+    begin("tp", "same", input_bf, input_all, *rows_input)
+    begin("tp", "same", output, output_all, *rows_output)
+    for move in first:
+        settle(*move)
+    sum_a[...] = summed(one_a).astype(BF16)
+    sum_b[...] = summed(one_b).astype(BF16)
+    sum_g[...] = summed(one_g)
+    stage(
+        ("z", lambda p: sum_a.at[p], lambda q: two_a.at[q], *take.two(), True),
+        ("x", lambda p: sum_b.at[p], lambda q: two_b.at[q], *take.two(), True),
+        ("z", lambda p: sum_g.at[p], lambda q: two_g.at[q], *take.two(), True),
+    )
+    part_a[...] = summed(two_a).astype(BF16)
+    part_b[...] = summed(two_b).astype(BF16)
+    part_g[...] = summed(two_g)
+    stage(
+        ("pair", lambda p: part_a.at[p], lambda q: three_a.at[q], *take.two(), True),
+        ("pair", lambda p: part_b.at[p], lambda q: three_b.at[q], *take.two(), True),
+        ("pair", lambda p: part_g.at[p], lambda q: three_g.at[q], *take.two(), True),
+    )
+    gain_sum[...] = summed(three_g)
+    begin("tp", "same", gain_sum, gain_tp, *gains_out)
+    qkv_grad[0] = summed(three_a)
+    qkv_grad[1] = summed(three_b)
+    finish("tp", "same", output, output_all, *rows_output)
+    finish("tp", "same", input_bf, input_all, *rows_input)
+    finish("tp", "same", gain_sum, gain_tp, *gains_out)
 
 
 def last_step(parts, qkv, gains, output, grad_residual, inputs, gain):
     own, width = inputs.shape
+    piece, small = qkv.shape[4:], gains.shape[3:]
+
+    def scratch(*shape):
+        return [pltpu.VMEM((*shape, *piece), BF16)] * 2 + [pltpu.VMEM((*shape, *small), F32)]
+
     return pl.pallas_call(
         last_body,
         out_shape=[
-            jax.ShapeDtypeStruct(qkv.shape, BF16),
+            jax.ShapeDtypeStruct((2, *piece), F32),
             jax.ShapeDtypeStruct((4, own, width), BF16),
             jax.ShapeDtypeStruct((4, own, width), BF16),
-            jax.ShapeDtypeStruct((4, *gains.shape[1:]), F32),
+            jax.ShapeDtypeStruct((4, *small), F32),
         ],
-        in_specs=[VMEM, ANY, VMEM, VMEM, VMEM, VMEM, VMEM],
-        out_specs=[ANY] * 4,
-        scratch_shapes=[
-            pltpu.VMEM((4, own, width), BF16),
-            pltpu.VMEM(gains.shape, F32),
-            pltpu.VMEM((own, width), BF16),
-            pltpu.VMEM(gains.shape[1:], F32),
-        ]
-        + sems(["tp", "ctx", "ctx", "tp", "tp", "tp"]),
-        compiler_params=pltpu.CompilerParams(collective_id=8, has_side_effects=True),
+        in_specs=[VMEM] * 7,
+        out_specs=[VMEM] + [ANY] * 3,
+        scratch_shapes=[pltpu.VMEM((4, own, width), BF16), pltpu.VMEM((own, width), BF16)]
+        + scratch(4, 4, 2)
+        + scratch(4, 2)
+        + scratch(4, 2)
+        + scratch(2)
+        + scratch(2)
+        + [pltpu.VMEM(small, F32)]
+        + sems(["tp"] * 4 + ["x", "z", "x", "z", "x", "z"] + ["pair"] * 3),
+        compiler_params=pltpu.CompilerParams(
+            collective_id=8, has_side_effects=True, vmem_limit_bytes=24 * 2**20
+        ),
         name="last_step",
     )(parts, qkv, gains, output, grad_residual, inputs, gain)
 
@@ -587,11 +809,10 @@
     gains = jnp.zeros((16, 128), BF16)
     gains = gains.at[0:2, 0:32].set(norm_gains).at[2:4, 0:2].set(head_gains)
     ffn_rows = jnp.concatenate([halves(w_gate), halves(w_up), halves(w_down)], axis=2)
-    weights_all, gains_all, ffn_pair = exchange(
-        1,
-        ["ctx"],
-        [("ctx", "same", weight_rows), ("ctx", "same", gains), ("pair", "own", ffn_rows)],
-    )
+    weights_all, gains_all, ffn_pair = gather(
+        weight_rows.reshape(2, 16, weight_rows.shape[1]), gains, ffn_rows
+    )
+    gains_all = gains_all.reshape(NCTX, 16, 128)
     planes = [[2 * g + h for g in range(NCTX // 2)] for h in range(2)]
     ffn_full = lax.all_gather(
         ffn_pair.reshape(2 * 32, 3 * unit_half), "ctx", axis_index_groups=planes, tiled=True
@@ -617,10 +838,10 @@
     key_rot = rotary(key_hat * gain_key, cosine, sine, 1.0).astype(BF16)
     q_src = to_pairs(query_rot * jnp.asarray(HEAD_SIZE**-0.5, BF16), 2, True)
     kv_src = jnp.concatenate([key_rot, values], axis=-1).transpose(2, 0, 1, 3)
-    kv_src = kv_src.reshape(PAIRS, tokens, 2 * HEAD_SIZE)
+    kv_src = kv_src.reshape(PAIRS, 2, tokens // 2, 2 * HEAD_SIZE)
 
     att, q_buf, kv_buf, o_buf, log_buf, wo_all, cot_all = forward(
-        q_src, kv_src, w_out, cotangent.reshape(rows, width)
+        q_src, kv_src, w_out.reshape(2, 16, 256), cotangent.reshape(rows, width)
     )
     attended = from_pairs(att[..., HEAD_SIZE:], seqs, 2).reshape(rows, 256)
     out_full = wo_all.reshape(width, 256)
@@ -647,7 +868,7 @@
     ffn_back = last_dims(grad_gu_in, gu_full).astype(BF16)
     cot_own = mine(cotangent.reshape(rows, width))
     grad_residual, ffn_gain_part, residual_all = norm_back_step(
-        ffn_back.reshape(8, own, width), residual, cot_own, gain_ffn.reshape(1, width)
+        ffn_back.reshape(4, 2, own, width), residual, cot_own, gain_ffn.reshape(1, width)
     )
     residual_bf = residual_all.reshape(rows, width)
 
@@ -669,7 +890,7 @@
 
     output_own = (residual + jnp.sum(ffn_parts.astype(F32), axis=0)).astype(BF16)
     grad_query_rot = from_pairs(dq_all[..., :HEAD_SIZE].astype(F32), seqs, 2)
-    dkv = jnp.sum(dkv_all.reshape(PAIRS, WORKERS, tokens, 2 * HEAD_SIZE).astype(F32), axis=1)
+    dkv = dkv_all.reshape(PAIRS, tokens, 2 * HEAD_SIZE).astype(F32)
     key_grad = from_pairs(dkv[..., :HEAD_SIZE], seqs, 1)
     value_in = from_pairs(dkv[..., HEAD_SIZE:], seqs, 1).astype(BF16).reshape(rows, 128)
     gq = rotary(grad_query_rot, cosine, sine, -1.0)
@@ -687,10 +908,10 @@
     gain_parts = gain_parts.at[:, 1, :32].set(ffn_gain_part.reshape(NCTX, 32))
     gain_parts = gain_parts.at[:, 2, :2].set(query_gain_part.reshape(NCTX, 2))
     gain_parts = gain_parts.at[:, 3, :2].set(key_gain_part.reshape(NCTX, 2))
-    qkv_parts, output_all, input_all, gain_tp = last_step(
+    qkv_grad, output_all, input_all, gain_tp = last_step(
         attn_back.astype(BF16).reshape(4, own, width),
-        grad_qkv.reshape(NCTX, 32, 512),
-        gain_parts,
+        grad_qkv.reshape(4, 4, 2, 2, 16, 512),
+        gain_parts.reshape(4, 4, 2, 8, 128),
         output_own,
         grad_residual,
         inputs_own,
@@ -699,7 +920,7 @@
     (pair_grads,) = exchange(9, ["pair"], [("pair", "own", grads_own.reshape(2, 32, -1))])
     pair_grads = pair_grads.astype(F32)
     gain_sum = jnp.sum(gain_tp, axis=0)
-    qkv_grad = jnp.sum(qkv_parts.astype(F32), axis=0)
+    qkv_grad = qkv_grad.reshape(32, 512)
     gu, end = 2 * unit_half, 2 * unit_half + 256
     out_grad = jnp.sum(pair_grads[:, :, gu:end], axis=0)
 

time: 327 us -> 305 us (0.933)
  Pallas kernels: 228 us -> 204 us
  local copies, waits for them, and re-layouts: 32.3 us -> 37.9 us
    pallas_call x2 -> x1, Pallas kernels: 34.2 us -> 7.74 us  [exchange(): pl.pallas_call(functools.partial(exchange_body, plan, kinds), out_shape=[...]
    pallas_call x1 -> x2, Pallas kernels: 38.4 us -> 49.7 us  [the longest x1 25.8 us: last_step(): pl.pallas_call(last_body, out_shape=[jax.ShapeDtypeStruct((2, *piece), F3...]
    pallas_call x1, Pallas kernels: 24.8 us -> 19.9 us  [norm_step(): pl.pallas_call(norm_body, out_shape=[jax.ShapeDtypeStruct((own, width), F...]
    pallas_call x1, Pallas kernels: 47.5 us -> 42.9 us  [forward(): pl.pallas_call(forward_body, out_shape=[stack, stack, jax.ShapeDtypeStruc...]
    pallas_call x1, Pallas kernels: 59.1 us -> 63.3 us  [backward(): pl.pallas_call(backward_body, out_shape=[jax.ShapeDtypeStruct((SLOTS, 2 *...]
    pallas_call x1, Pallas kernels: 24.2 us -> 20.2 us  [norm_back_step(): pl.pallas_call(norm_back_body, out_shape=[jax.ShapeDtypeStruct((own, widt...]
    unnamed x101 -> x105, local copies, waits for them, and re-layouts: 7.91 us -> 6.2 us
  transfers between devices with their start and end apart: 2 -> 2, of which waited for: 0 -> 0; matrix products, arithmetic and copies ran while one was open for 12% -> 14% of each run, Pallas kernels for 52% -> 50%
where the time goes in v4:
time: 305 us; the launch traced here: 304 us
  Pallas kernels  204 us (67%)
  local copies, waits for them, and re-layouts  37.9 us (12%)
  matrix products  25.9 us (8%)
  other arithmetic  20.6 us (7%)
  between operations  15.2 us (5%)
    pallas_call x1, Pallas kernels, backward(): pl.pallas_call(backward_body, out_shape=[jax.ShapeDtypeStruct((SLOTS, 2 *...  63.3 us
    pallas_call x1, Pallas kernels, forward(): pl.pallas_call(forward_body, out_shape=[stack, stack, jax.ShapeDtypeStruc...  42.9 us
    pallas_call x1, Pallas kernels, last_step(): pl.pallas_call(last_body, out_shape=[jax.ShapeDtypeStruct((2, *piece), F3...  25.8 us
    pallas_call x1, Pallas kernels, gather(): pl.pallas_call(gather_body, out_shape=[jax.ShapeDtypeStruct((4, 4, 2, *w....  23.9 us
    pallas_call x1, Pallas kernels, norm_back_step(): pl.pallas_call(norm_back_body, out_shape=[jax.ShapeDtypeStruct((own, widt...  20.2 us
    pallas_call x1, Pallas kernels, norm_step(): pl.pallas_call(norm_body, out_shape=[jax.ShapeDtypeStruct((own, width), F...  19.9 us
    dot_general x4, matrix products, first_dims(): lax.dot_general(a, b, (((0,), (0,)), ((), ())), preferred_element_type=F32)  8.59 us
    dot_general x4, matrix products, last_dims(): lax.dot_general(a, b, (((1,), (1,)), ((), ())), preferred_element_type=F32)  8.19 us
  transfers between devices with their start and end apart: 2, of which 0 were waited for; matrix products, arithmetic and copies ran while one was open for 14% of the time, Pallas kernels for 50%

profile of v4, /device:TPU:0, one launch (start us, length us, event | category | flops | bytes accessed | tf_op | source)
XLA Modules:
  0.0 303.5 jit_solution(6223629212399557791)
XLA Ops:
  7.2 0.9 slice_bitcast_fusion.11
  8.2 0.9 slice_bitcast_fusion.9
  9.1 0.9 slice_bitcast_fusion.7
  10.0 0.7 scatter.20
  10.7 1.4 pad_maximum_fusion.15
  12.1 0.8 concatenate.66.ffn
  12.9 1.5 scatter.21.gains
  15.0 23.9 %gather.1 = (bf16[4,4,2,2,16,512]{5,4,3,2,1,0:T(8,128)(2,1)}, bf16[4,4,2,16,128]{4,3,2,1,0:T(8,128)(2,1)}, bf16[2,32,1728]{2,1,0:T(8,128)(2,1)}) custom-call(bf16[2,16,512]{2,1,0:T(8,128)(2,1)} %bitcast.221, bf16[16,128]{1,0:T(8,128)(2,1)} %copy-done.33, bf16[2,32,1728]{2,1,0:T(8,128)(2,1)} %concatenate.66.ffn), custom_call_target="tpu_custom_call" | custom-call | tf_op jit(solution)/shard_map/gather/pallas_call | solution.py:201
  39.0 1.5 fusion.26
  41.6 1.7 fusion.29
  43.3 0.7 copy-done.11
  44.4 1.0 fusion.27
  45.7 0.8 broadcast_multiply_fusion
  49.2 42.9 %attention_forward.1 = (bf16[4,256,128]{2,1,0:T(8,128)(2,1)S(1)}, bf16[4,256,128]{2,1,0:T(8,128)(2,1)S(1)}, bf16[4,4,2,2,64,128]{5,4,3,2,1,0:T(8,128)(2,1)S(1)},...) custom-call(bf16[4,256,128]{2,1,0:T(8,128)(2,1)S(1)} %pad.35.q_src, ...), custom_call_target="tpu_custom_call" | custom-call | tf_op jit(solution)/shard_map/attention_forward/pallas_call | solution.py:455
  92.2 1.0 copy-done.4
  93.4 0.7 copy_convert_fusion
  94.1 0.7 reshape.599.gain
  94.8 1.1 bitcast_convert_fusion.1
  96.0 1.0 copy-done.6
  97.0 0.7 constant_dynamic-slice_fusion.1.inputs
  97.7 1.1 convolution_convert_fusion.5
  98.8 19.9 %norm_step.1 = (f32[64,1024]{1,0:T(8,128)}, bf16[4,2,64,1024]{3,2,1,0:T(8,128)(2,1)}) custom-call(bf16[4,64,1024]{2,1,0:T(8,128)(2,1)} %bitcast.191, f32[64,1024]{1,0:T(8,128)} %constant_dynamic-slice_fusion.1.inputs, f32[1,1024]{1,0:T(1,128)} %reshape.599.gain), custom_call_target="tpu_custom_call" | custom-call | tf_op jit(solution)/shard_map/norm_step/pallas_call | solution.py:605
  118.8 0.7 constant_dynamic-slice_fusion.cot
  119.5 3.5 %fusion.2 = f32[512,1152]{0,1:T(8,128)S(1)} fusion(bf16[512,1024]{1,0:T(8,128)(2,1)} %bitcast.227, bf16[1024,1728]{1,0:T(8,128)(2,1)} %all-gather.2.cloned.1.call-done), kind=kOutput, calls=%fused_computation.5 | convolution fusion | flops 1207959552 | bytes 5767168 | tf_op jit(solution)/shard_map/dot_general | solution.py:859
  123.0 3.6 %multiply_convert_fusion.2 = (bf16[512,576]{0,1:T(8,128)(2,1)}, bf16[512,576]{0,1:T(8,128)(2,1)}, bf16[512,576]{0,1:T(8,128)(2,1)S(1)}) fusion(f32[512,1152]{0,1:T(8,128)S(1)} %fusion.2, bf16[512,1024]{1,0:T(8,128)(2,1)S(1)} %bitcast.186, bf16[1024,1728]{1,0:T(8,128)(2,1)} %all-gather.2.cloned.1.call-done), kind=kOutput, calls=%fused_computation.16 | convolution fusion | flops 608403456 | bytes 6488064 | tf_op jit(solution)/shard_map/dot_general | solution.py:864
  126.6 1.9 convolution_convert_fusion.1
  128.5 2.4 copy.191
  130.9 4.8 %convolution_convert_fusion = bf16[1024,1152]{1,0:T(8,128)(2,1)} fusion(bf16[512,1024]{1,0:T(8,128)(2,1)} %bitcast.228, bf16[512,576]{0,1:T(8,128)(2,1)} %get-tuple-element.128, bf16[512,576]{0,1:T(8,128)(2,1)} %get-tuple-element.127), kind=kOutput, calls=%fused_computation.1 | convolution fusion | flops 1211498496 | bytes 4587520 | tf_op jit(solution)/shard_map/dot_general | solution.py:371
  135.7 2.5 fusion.4
  138.2 20.2 %norm_back_step.1 = (f32[64,1024]{1,0:T(8,128)}, f32[1,1024]{1,0:T(1,128)}, bf16[4,64,1024]{2,1,0:T(8,128)(2,1)}) custom-call(bf16[4,2,64,1024]{3,2,1,0:T(8,128)(2,1)} %bitcast.198, f32[64,1024]{1,0:T(8,128)} %get-tuple-element.112.residual, bf16[64,1024]{1,0:T(8,128)(2,1)} %constant_dynamic-slice_fusion.cot, f32[1,1024]{1,0:T(1,128)} %reshape.599.gain), custom_call_target="tpu_custom_call" | custom-call | tf_op jit(solution)/shard_map/norm_back_step/pallas_call | solution.py:644
  158.5 1.4 convolution_convert_fusion.4
  159.9 3.8 %pad_maximum_fusion = bf16[1024,1984]{1,0:T(8,128)(2,1)} fusion(bf16[1024,576]{1,0:T(8,128)(2,1)} %copy.191, bf16[1024,256]{1,0:T(8,128)(2,1)S(1)} %convolution_convert_fusion.4, bf16[1024,1152]{1,0:T(8,128)(2,1)} %convolution_convert_fusion), kind=kLoop, calls=%fused_computation | loop fusion | flops 12189696 | bytes 8126464 | tf_op jit(solution)/shard_map/concatenate | solution.py:882
  163.7 0.7 copy-done.25
  164.5 0.8 copy.181
  166.0 0.8 copy.175
  166.8 0.6 mul.392
  168.2 2.5 convolution_convert_fusion.3
  170.8 63.3 %attention_backward.1 = (bf16[4,256,128]{2,1,0:T(8,128)(2,1)S(1)}, bf16[4,2,64,128]{3,2,1,0:T(8,128)(2,1)S(1)}, bf16[8,64,1024]{2,1,0:T(8,128)(2,1)S(1)}) custom-call(bf16[4,256,128]{2,1,0:T(8,128)(2,1)S(1)} %pad.36.do_src, bf16[4,256,128]{2,1,0:T(8,128)(2,1)S(1)} %get-tuple-element.114.q_buf, bf16[4,4,2,2,64,128]{5,4,3,2,1,0:T(8,128)(2,1)S(1)} %get-tuple-element.115.kv_buf, ...), custom_call_target="tpu_custom_call" | custom-call | tf_op jit(solution)/shard_map/attention_backward/pallas_call | solution.py:540
  234.6 0.7 reshape.613
  235.6 1.1 pad_maximum_fusion.9
  238.8 0.7 multiply_reduce_fusion.2
  239.5 2.0 multiply_reduce_fusion
  241.5 0.7 reshape.586
  242.7 0.7 reduce.20
  243.3 0.7 reshape.587
  244.1 0.7 scatter.24
  245.4 1.4 reshape.588
  246.7 1.3 reduce_sum.123
  248.0 0.7 reduce_sum.124
  248.7 0.7 reshape.589
  249.4 1.2 scatter.25
  250.6 1.2 scatter.26
  251.9 1.2 scatter.29
  253.3 1.0 add_convert_fusion.output
  254.9 25.8 %last_step.1 = (f32[2,16,512]{2,1,0:T(8,128)S(1)}, bf16[4,64,1024]{2,1,0:T(8,128)(2,1)S(1)}, bf16[4,64,1024]{2,1,0:T(8,128)(2,1)S(1)}, f32[4,8,128]{2,1,0:T(8,128)S(1)}) custom-call(bf16[4,64,1024]{2,1,0:T(8,128)(2,1)S(1)} %bitcast.181, bf16[4,4,2,2,16,512]{5,4,3,2,1,0:T(8,128)(2,1)S(1)} %bitcast.170, f32[4,4,2,8,128]{4,3,2,1,0:T(8,128)S(1)} %bitcast.177, ...), custom_call_target="tpu_custom_call" | custom-call | tf_op jit(solution)/shard_map/last_step/pallas_call | solution.py:724
  281.9 0.6 slice.333
  283.1 1.1 bitcast_convert_fusion
  284.2 7.7 %exchange9.1 = bf16[2,32,1984]{2,1,0:T(8,128)(2,1)} custom-call(bf16[2,32,1984]{2,1,0:T(8,128)(2,1)} %bitcast.217), custom_call_target="tpu_custom_call" | custom-call | tf_op jit(solution)/shard_map/exchange9/pallas_call | solution.py:240
  291.9 1.0 convert_element_type.176
  292.9 0.6 slice_reduce_fusion
  293.7 0.8 pad_maximum_fusion.6
  294.4 0.8 pad_maximum_fusion.7
  295.2 0.8 pad_maximum_fusion.8
  295.9 0.8 copy.246
  (183 shorter events, 13.1 us)
Async XLA Ops:
  7.2 33.4 %copy-start.8 = (bf16[2,128,1024]{2,1,0:T(8,128)(2,1)S(1)}, bf16[2,128,1024]{2,1,0:T(8,128)(2,1)}, u32[]{:S(2)}) copy-start(bf16[2,128,1024]{2,1,0:T(8,128)(2,1)} %param.23) | copy-start | bytes 1572868
  7.2 112.3 %all-gather.2.cloned.1.call-start = ((), (), s32[]{:S(2)}) async-start(), calls=%async_computation.1 | async-start | bytes 3899392 | tf_op jit(solution)/shard_map/all_gather | solution.py:817
  14.4 0.6 copy-start.33
  38.9 245.3 %reduce-scatter.2.cloned.1.call-start = ((), (), s32[]{:S(2)}) async-start(), calls=%async_computation.2 | async-start | bytes 4456448 | tf_op jit(solution)/shard_map/reduce_scatter | solution.py:881
  40.5 3.7 %copy-start.24 = (f32[32,1,32]{2,0,1:T(8,128)}, f32[32,1,32]{2,0,1:T(8,128)S(1)}, u32[]{:S(2)}) copy-start(f32[32,1,32]{2,0,1:T(8,128)S(1)} %copy_convert_fusion.3) | copy-start | bytes 12292
  40.6 3.6 %copy-start.29 = (f32[1024]{0:T(1024)}, f32[1024]{0:T(1024)S(1)}, u32[]{:S(2)}) copy-start(f32[1024]{0:T(1024)S(1)} %reshape.596) | copy-start | bytes 12292
  43.2 0.8 copy-start.11
  44.3 4.8 %copy-start.9 = (f32[2,128,4,64]{1,0,3,2:T(2,128)}, f32[2,128,4,64]{1,0,3,2:T(2,128)S(1)}, u32[]{:S(2)}) copy-start(f32[2,128,4,64]{1,0,3,2:T(2,128)S(1)} %reshape.560) | copy-start | bytes 786436
  45.5 1.1 copy-start.34
  45.5 3.7 %copy-start.1 = (bf16[2,128,1024]{2,1,0:T(8,128)(2,1)S(1)}, bf16[2,128,1024]{2,1,0:T(8,128)(2,1)}, u32[]{:S(2)}) copy-start(bf16[2,128,1024]{2,1,0:T(8,128)(2,1)} %param.24) | copy-start | bytes 1572868
  45.5 3.7 %copy-start.3 = (bf16[32,256]{1,0:T(8,128)(2,1)S(1)}, bf16[32,256]{1,0:T(8,128)(2,1)}, u32[]{:S(2)}) copy-start(bf16[32,256]{1,0:T(8,128)(2,1)} %param.28) | copy-start | bytes 49156
  45.7 0.9 copy-start.26
  46.4 2.8 copy-start.17
  47.4 1.8 copy-start.14
  47.5 0.5 copy-start.37
  48.1 0.6 copy-start.31
  92.2 1.0 copy-start.4
  96.0 1.0 copy-start.6
  119.4 3.5 %copy-start.5 = (bf16[2,256,1024]{2,1,0:T(8,128)(2,1)S(1)}, bf16[2,256,1024]{2,1,0:T(8,128)(2,1)}, u32[]{:S(2)}) copy-start(bf16[2,256,1024]{2,1,0:T(8,128)(2,1)} %copy-done.4) | copy-start | bytes 3145732
  126.6 4.3 %copy-start.45 = (bf16[512,576]{0,1:T(8,128)(2,1)}, bf16[512,576]{0,1:T(8,128)(2,1)S(1)}, u32[]{:S(2)}) copy-start(bf16[512,576]{0,1:T(8,128)(2,1)S(1)} %get-tuple-element.129) | copy-start | bytes 1769476
  130.9 4.8 %copy-start.44 = (bf16[1024,1728]{1,0:T(8,128)(2,1)S(1)}, bf16[1024,1728]{1,0:T(8,128)(2,1)}, u32[]{:S(2)}) copy-start(bf16[1024,1728]{1,0:T(8,128)(2,1)} %all-gather.2.cloned.1.call-done) | copy-start | bytes 10616836
  130.9 4.8 %copy-start.46 = (bf16[512,576]{0,1:T(8,128)(2,1)S(1)}, bf16[512,576]{0,1:T(8,128)(2,1)}, u32[]{:S(2)}) copy-start(bf16[512,576]{0,1:T(8,128)(2,1)} %get-tuple-element.127) | copy-start | bytes 1769476
  130.9 4.8 %copy-start.47 = (bf16[512,576]{0,1:T(8,128)(2,1)S(1)}, bf16[512,576]{0,1:T(8,128)(2,1)}, u32[]{:S(2)}) copy-start(bf16[512,576]{0,1:T(8,128)(2,1)} %get-tuple-element.128) | copy-start | bytes 1769476
  163.6 0.7 copy-start.25
  163.7 0.8 copy-start.32
  163.7 1.6 copy-start.38
  163.7 2.2 copy-start.27
  163.7 3.1 %copy-start.35 = (f32[64]{0:T(128)S(1)}, f32[64]{0:T(128)}, u32[]{:S(2)}) copy-start(f32[64]{0:T(128)} %copy-done.34) | copy-start | bytes 772
  163.7 3.8 %copy-start.13 = (bf16[4,64,1024]{2,1,0:T(8,128)(2,1)S(1)}, bf16[4,64,1024]{2,1,0:T(8,128)(2,1)}, u32[]{:S(2)}) copy-start(bf16[4,64,1024]{2,1,0:T(8,128)(2,1)} %get-tuple-element.113) | copy-start | bytes 1572868
  170.8 64.7 %copy-start.18 = (f32[128,32]{0,1:T(8,128)S(1)}, f32[128,32]{0,1:T(8,128)}, u32[]{:S(2)}) copy-start(f32[128,32]{0,1:T(8,128)} %copy-done.17) | copy-start | bytes 49156
  170.8 64.7 %copy-start.22 = (f32[128,32]{0,1:T(8,128)S(1)}, f32[128,32]{0,1:T(8,128)}, u32[]{:S(2)}) copy-start(f32[128,32]{0,1:T(8,128)} %get-tuple-element.172) | copy-start | bytes 49156
  234.2 3.0 copy-start.23
  234.3 3.1 %copy-start.10 = (f32[2,128,4,64]{1,0,3,2:T(2,128)S(1)}, f32[2,128,4,64]{1,0,3,2:T(2,128)}, u32[]{:S(2)}) copy-start(f32[2,128,4,64]{1,0,3,2:T(2,128)} %copy-done.9) | copy-start | bytes 786436
  234.3 3.1 %copy-start.28 = (f32[2,128,4]{1,0,2:T(2,128)S(1)}, f32[2,128,4]{1,0,2:T(2,128)}, u32[]{:S(2)}) copy-start(f32[2,128,4]{1,0,2:T(2,128)} %copy-done.26) | copy-start | bytes 12292
  234.3 3.1 %copy-start.36 = (f32[64]{0:T(128)S(1)}, f32[64]{0:T(128)}, u32[]{:S(2)}) copy-start(f32[64]{0:T(128)} %copy-done.34) | copy-start | bytes 772
  237.0 1.2 copy-start.12
  237.0 1.2 copy-start.16
  237.0 1.2 copy-start.43
  237.1 1.6 copy-start.15
  237.1 1.6 copy-start.40
  237.4 2.0 copy-start.39
  238.2 4.5 %copy-start.42 = (f32[1,1024]{1,0:T(1,128)S(1)}, f32[1,1024]{1,0:T(1,128)}, u32[]{:S(2)}) copy-start(f32[1,1024]{1,0:T(1,128)} %get-tuple-element.120) | copy-start | bytes 12292
  238.8 0.7 copy-start.20
  239.4 4.6 %copy-start.41 = (f32[256]{0:T(256)S(1)}, f32[256]{0:T(256)}, u32[]{:S(2)}) copy-start(f32[256]{0:T(256)} %get-tuple-element.130) | copy-start | bytes 3076
  239.4 14.8 %copy-start.7 = (f32[256,1024]{1,0:T(8,128)S(1)}, f32[256,1024]{1,0:T(8,128)}, u32[]{:S(2)}) copy-start(f32[256,1024]{1,0:T(8,128)} %copy-done.6) | copy-start | bytes 3145732
  239.5 14.8 %copy-start.19 = (bf16[256,128]{1,0:T(8,128)(2,1)S(1)}, bf16[256,128]{1,0:T(8,128)(2,1)}, u32[]{:S(2)}) copy-start(bf16[256,128]{1,0:T(8,128)(2,1)} %reshape.613) | copy-start | bytes 196612
  239.5 14.8 %copy-start.30 = (f32[1024]{0:T(1024)S(1)}, f32[1024]{0:T(1024)}, u32[]{:S(2)}) copy-start(f32[1024]{0:T(1024)} %copy-done.29) | copy-start | bytes 12292
  241.4 12.8 %copy-start.21 = (bf16[256,128]{1,0:T(8,128)(2,1)S(1)}, bf16[256,128]{1,0:T(8,128)(2,1)}, u32[]{:S(2)}) copy-start(bf16[256,128]{1,0:T(8,128)(2,1)} %copy-done.20) | copy-start | bytes 196612
  241.5 13.4 %copy-start = (f32[64,1024]{1,0:T(8,128)S(1)}, f32[64,1024]{1,0:T(8,128)}, u32[]{:S(2)}) copy-start(f32[64,1024]{1,0:T(8,128)} %constant_dynamic-slice_fusion.1.inputs) | copy-start | bytes 786436
  241.5 13.4 %copy-start.2 = (f32[64,1024]{1,0:T(8,128)S(1)}, f32[64,1024]{1,0:T(8,128)}, u32[]{:S(2)}) copy-start(f32[64,1024]{1,0:T(8,128)} %get-tuple-element.122.grad_residual) | copy-start | bytes 786436
Sparse Core Ops, SparseCore 0:
  39.0 54.0 all-gather.1
  163.8 89.1 reduce-scatter.1

commit v5 on v4

--- a/solution.py
+++ b/solution.py
@@ -585,93 +585,144 @@
     return total
 
 
-def norm_body(
-    parts, inputs, gain, residual, hidden_all, landed, hidden,
-    send0, recv0, send1, recv1, send2, recv2,
+UNITS = 640
+
+
+def feed_body(
+    parts, inputs, gain, w, cot, cot_own,
+    residual, grad_residual, gain_part, grad_all, grads, ffn_part,
+    landed, hidden, hidden_all, grad_units, units, grad_in, back, halved, chip, ringed, grad_bf, *sem,
 ):
+    take = Sems(sem)
+    core = lax.rem(lax.axis_index("tp"), 2)
     greet(["tp", "ring"])
-    begin("tp", "own", parts, landed, send0, recv0)
-    finish("tp", "own", parts, landed, send0, recv0)
-    total = inputs[...] + summed(landed)
-    residual[...] = total
-    hidden[...] = (total * row_scale(total) * gain[...]).astype(BF16)
-    core = lax.rem(lax.axis_index("tp"), 2)
-    stage(("ring", lambda p: hidden, lambda q: hidden_all.at[q, core], send1, recv1, True))
-    stage(("core", lambda p: hidden_all.at[:, core], lambda q: hidden_all.at[:, q], send2, recv2))
-
-
-def norm_step(parts, inputs, gain):
-    own, width = inputs.shape
-    return pl.pallas_call(
-        norm_body,
-        out_shape=[
-            jax.ShapeDtypeStruct((own, width), F32),
-            jax.ShapeDtypeStruct((4, 2, own, width), BF16),
-        ],
-        in_specs=[VMEM] * 3,
-        out_specs=[VMEM, VMEM],
-        scratch_shapes=[pltpu.VMEM((4, own, width), BF16), pltpu.VMEM((own, width), BF16)]
-        + sems(["tp", "ring", "core"]),
-        compiler_params=pltpu.CompilerParams(collective_id=3, has_side_effects=True),
-        name="norm_step",
-    )(parts, inputs, gain)
-
-
-def norm_back_body(
-    parts, residual, cot, gain, grad_residual, gain_part, grad_all,
-    halved, chip, landed, grad_bf, send0, recv0, send1, recv1, send2, recv2,
-):
-    greet(["tp", "ring"])
-    both = ("core", lambda p: parts.at[:, p], lambda q: halved.at[q], send2, recv2, True)
+    share = ("tp", lambda p: parts.at[p], lambda q: landed.at[q], *take.two(), True)
+    push(*share)
+
+    @pl.loop(0, 4)
+    def _(m):
+        at = pl.ds(pl.multiple_of(m * 128, 128), 128)
+        grad_units[at] = jnp.dot(cot[at], w[:, 2 * UNITS :], preferred_element_type=F32)
+
+    settle(*share)
+    rows = inputs[...] + summed(landed)
+    residual[...] = rows
+    scale = row_scale(rows)
+    hidden[...] = (rows * scale * gain[...]).astype(BF16)
+    stage(("ring", lambda p: hidden, lambda q: hidden_all.at[q, core], *take.two(), True))
+    stage(("core", lambda p: hidden_all.at[:, core], lambda q: hidden_all.at[:, q], *take.two()))
+
+    @pl.loop(0, 2)
+    def _(m):
+        at = pl.ds(pl.multiple_of(m * 256, 256), 256)
+        some = hidden_all[pl.ds(2 * m, 2)].reshape(256, hidden.shape[1])
+        gate = jnp.dot(some, w[:, :UNITS], preferred_element_type=F32)
+        up = jnp.dot(some, w[:, UNITS : 2 * UNITS], preferred_element_type=F32)
+        sigmoid = jax.nn.sigmoid(gate)
+        activated = gate * sigmoid
+        units[at] = (activated * up).astype(BF16)
+        grad = grad_units[at]
+        grad_in[at, :UNITS] = (grad * up * sigmoid * (1.0 + gate * (1.0 - sigmoid))).astype(BF16)
+        grad_in[at, UNITS:] = (grad * activated).astype(BF16)
+        step = last_dims(grad_in[at], w[:, : 2 * UNITS]).astype(BF16)
+        back[pl.ds(2 * m, 2)] = step.reshape(2, *back.shape[1:])
+
+    both = ("core", lambda p: back.at[:, p], lambda q: halved.at[q], *take.two(), True)
     push(*both)
+
+    @pl.loop(0, 2)
+    def _(m):
+        at = pl.ds(pl.multiple_of(m * 256, 256), 256)
+        step = last_dims(units[at], w[:, 2 * UNITS :]).astype(BF16)
+        ffn_part[pl.ds(4 * m, 4)] = step.reshape(4, *ffn_part.shape[1:])
+
+    settle(*both)
+    chip[...] = summed(halved).astype(BF16)
+    ring = ("ring", lambda p: chip.at[p], lambda q: ringed.at[q], *take.two(), True)
+    push(*ring)
+
+    @pl.loop(0, 4)
+    def _(m):
+        at = pl.ds(pl.multiple_of(m * 256, 256), 256)
+        some = hidden_all[:, :, :, at].reshape(512, 256)
+        grads[at, : 2 * UNITS] = first_dims(some, grad_in[...]).astype(BF16)
+
+    settle(*ring)
+    total = summed(ringed)
     rows = residual[...]
     scale = row_scale(rows)
     normed = rows * scale
-    settle(*both)
-    chip[...] = summed(halved).astype(BF16)
-    stage(("ring", lambda p: chip.at[p], lambda q: landed.at[q], send0, recv0, True))
-    grads = summed(landed)
-    result = cot[...].astype(F32) + row_back(grads, normed, scale, gain[...])
+    result = cot_own[...].astype(F32) + row_back(total, normed, scale, gain[...])
     grad_bf[...] = result.astype(BF16)
-    begin("tp", "same", grad_bf, grad_all, send1, recv1)
+    last = ("tp", lambda p: grad_bf, lambda q: grad_all.at[q], *take.two(), True)
+    push(*last)
     grad_residual[...] = result
-    gain_part[...] = jnp.sum(grads * normed, axis=0, keepdims=True)
-    finish("tp", "same", grad_bf, grad_all, send1, recv1)
-
-
-def norm_back_step(parts, residual, cot, gain):
-    own, width = residual.shape
+    gain_part[...] = jnp.sum(total * normed, axis=0, keepdims=True)
+
+    @pl.loop(0, 4)
+    def _(m):
+        at = pl.ds(pl.multiple_of(m * 256, 256), 256)
+        grads[at, 2 * UNITS :] = first_dims(cot[:, at], units[...]).astype(BF16)
+
+    settle(*last)
+
+
+def feed_step(parts, inputs, gain, w, cot, cot_own):
+    own, width = inputs.shape
+    rows = cot.shape[0]
     return pl.pallas_call(
-        norm_back_body,
+        feed_body,
         out_shape=[
+            jax.ShapeDtypeStruct((own, width), F32),
             jax.ShapeDtypeStruct((own, width), F32),
             jax.ShapeDtypeStruct((1, width), F32),
             jax.ShapeDtypeStruct((4, own, width), BF16),
+            jax.ShapeDtypeStruct(w.shape, BF16),
+            jax.ShapeDtypeStruct((8, own, width), BF16),
         ],
-        in_specs=[VMEM] * 4,
-        out_specs=[VMEM, VMEM, ANY],
+        in_specs=[VMEM] * 6,
+        out_specs=[VMEM] * 6,
         scratch_shapes=[
+            pltpu.VMEM((4, own, width), BF16),
+            pltpu.VMEM((own, width), BF16),
+            pltpu.VMEM((4, 2, own, width), BF16),
+            pltpu.VMEM((rows, UNITS), F32),
+            pltpu.VMEM((rows, UNITS), BF16),
+            pltpu.VMEM((rows, 2 * UNITS), BF16),
+            pltpu.VMEM((4, 2, own, width), BF16),
             pltpu.VMEM((2, 4, own, width), BF16),
             pltpu.VMEM((4, own, width), BF16),
             pltpu.VMEM((4, own, width), BF16),
             pltpu.VMEM((own, width), BF16),
         ]
-        + sems(["ring", "tp", "core"]),
-        compiler_params=pltpu.CompilerParams(collective_id=5, has_side_effects=True),
-        name="norm_back_step",
-    )(parts, residual, cot, gain)
+        + sems(["tp", "ring", "core", "core", "ring", "tp"]),
+        compiler_params=pltpu.CompilerParams(
+            collective_id=3, has_side_effects=True, vmem_limit_bytes=40 * 2**20
+        ),
+        name="feed_forward",
+    )(parts, inputs, gain, w, cot, cot_own)
 
 
 def last_body(
-    parts, qkv, gains, output, grad_residual, inputs, gain,
-    qkv_grad, output_all, input_all, gain_tp,
-    landed, input_bf, one_a, one_b, one_g, sum_a, sum_b, sum_g, two_a, two_b, two_g,
+    parts, hidden, grad_in, res_rows, attended, ffn, gains, output, grad_residual, inputs, gain,
+    qkv_grad, ffn_all, output_all, input_all, gain_tp,
+    qkv, landed, input_bf, one_a, one_b, one_g, sum_a, sum_b, sum_g, two_a, two_b, two_g,
     part_a, part_b, part_g, three_a, three_b, three_g, gain_sum, *sem,
 ):
     take = Sems(sem)
     greet(["z", "x", "pair", "tp"])
     rows_sums, rows_output, rows_input, gains_out = [take.two() for _ in range(4)]
     begin("tp", "own", parts, landed, *rows_sums)
+
+    @pl.loop(0, 4)
+    def _(m):
+        at = pl.ds(pl.multiple_of(m * 256, 256), 256)
+        wide = grad_in.shape[1]
+        step = first_dims(hidden[:, at], grad_in[...]).astype(BF16)
+        qkv[m, :, :, :, :, :wide] = step.reshape(4, 2, 2, 16, wide)
+        step = first_dims(res_rows[:, at], attended[...]).astype(BF16)
+        qkv[m, :, :, :, :, wide:] = step.reshape(4, 2, 2, 16, attended.shape[1])
+
     first = [
         ("x", lambda p: qkv.at[:, p, :, 0], lambda q: one_a.at[q], *take.two(), True),
         ("z", lambda p: qkv.at[p, :, :, 1], lambda q: one_b.at[q], *take.two(), True),
@@ -687,6 +738,8 @@
     input_bf[...] = result.astype(BF16)
     begin("tp", "same", input_bf, input_all, *rows_input)
     begin("tp", "same", output, output_all, *rows_output)
+    swap = ("pair", lambda p: ffn.at[p], lambda q: ffn_all.at[q], *take.two(), True)
+    push(*swap)
     for move in first:
         settle(*move)
     sum_a[...] = summed(one_a).astype(BF16)
@@ -712,11 +765,14 @@
     finish("tp", "same", output, output_all, *rows_output)
     finish("tp", "same", input_bf, input_all, *rows_input)
     finish("tp", "same", gain_sum, gain_tp, *gains_out)
-
-
-def last_step(parts, qkv, gains, output, grad_residual, inputs, gain):
+    settle(*swap)
+
+
+def last_step(
+    parts, hidden, grad_in, res_rows, attended, ffn, gains, output, grad_residual, inputs, gain
+):
     own, width = inputs.shape
-    piece, small = qkv.shape[4:], gains.shape[3:]
+    piece, small = (16, grad_in.shape[1] + attended.shape[1]), gains.shape[3:]
 
     def scratch(*shape):
         return [pltpu.VMEM((*shape, *piece), BF16)] * 2 + [pltpu.VMEM((*shape, *small), F32)]
@@ -725,25 +781,27 @@
         last_body,
         out_shape=[
             jax.ShapeDtypeStruct((2, *piece), F32),
+            jax.ShapeDtypeStruct(ffn.shape, BF16),
             jax.ShapeDtypeStruct((4, own, width), BF16),
             jax.ShapeDtypeStruct((4, own, width), BF16),
             jax.ShapeDtypeStruct((4, *small), F32),
         ],
-        in_specs=[VMEM] * 7,
-        out_specs=[VMEM] + [ANY] * 3,
-        scratch_shapes=[pltpu.VMEM((4, own, width), BF16), pltpu.VMEM((own, width), BF16)]
+        in_specs=[VMEM] * 5 + [ANY] + [VMEM] * 5,
+        out_specs=[VMEM] + [ANY] * 4,
+        scratch_shapes=[pltpu.VMEM((4, 4, 2, 2, *piece), BF16)]
+        + [pltpu.VMEM((4, own, width), BF16), pltpu.VMEM((own, width), BF16)]
         + scratch(4, 4, 2)
         + scratch(4, 2)
         + scratch(4, 2)
         + scratch(2)
         + scratch(2)
         + [pltpu.VMEM(small, F32)]
-        + sems(["tp"] * 4 + ["x", "z", "x", "z", "x", "z"] + ["pair"] * 3),
+        + sems(["tp"] * 4 + ["x", "z", "x", "pair", "z", "x", "z"] + ["pair"] * 3),
         compiler_params=pltpu.CompilerParams(
             collective_id=8, has_side_effects=True, vmem_limit_bytes=24 * 2**20
         ),
         name="last_step",
-    )(parts, qkv, gains, output, grad_residual, inputs, gain)
+    )(parts, hidden, grad_in, res_rows, attended, ffn, gains, output, grad_residual, inputs, gain)
 
 
 def rms_scale(rows):
@@ -787,9 +845,11 @@
     return x.reshape(s, tokens, kv * heads, HEAD_SIZE)
 
 
-def halves(w):
-    half = w.shape[1] // 2
-    return jnp.stack([w[:, :half], w[:, half:]])
+def halves(*weights):
+    rows, cols = weights[0].shape
+    w = jnp.stack(weights).reshape(len(weights), rows, 2, cols // 2)
+    w = jnp.pad(w, ((0, 0), (0, 0), (0, 0), (0, UNITS - cols // 2)))
+    return w.transpose(2, 1, 0, 3).reshape(2, rows, len(weights) * UNITS)
 
 
 def local(
@@ -806,16 +866,15 @@
         return lax.dynamic_slice_in_dim(x, t * own, own, 0)
 
     weight_rows = jnp.concatenate([w_query, key_weight, w_value], axis=1)
-    gains = jnp.zeros((16, 128), BF16)
-    gains = gains.at[0:2, 0:32].set(norm_gains).at[2:4, 0:2].set(head_gains)
-    ffn_rows = jnp.concatenate([halves(w_gate), halves(w_up), halves(w_down)], axis=2)
+    gains = jnp.pad(norm_gains, ((0, 14), (0, 96))) + jnp.pad(head_gains, ((2, 12), (0, 126)))
+    ffn_rows = halves(w_gate, w_up, w_down)
     weights_all, gains_all, ffn_pair = gather(
         weight_rows.reshape(2, 16, weight_rows.shape[1]), gains, ffn_rows
     )
     gains_all = gains_all.reshape(NCTX, 16, 128)
     planes = [[2 * g + h for g in range(NCTX // 2)] for h in range(2)]
     ffn_full = lax.all_gather(
-        ffn_pair.reshape(2 * 32, 3 * unit_half), "ctx", axis_index_groups=planes, tiled=True
+        ffn_pair.reshape(2 * 32, 3 * UNITS), "ctx", axis_index_groups=planes, tiled=True
     )
     qkv_full = weights_all.reshape(width, weight_rows.shape[1])
     gain_attn = gains_all[:, 0, :32].reshape(width).astype(F32)
@@ -845,47 +904,25 @@
     )
     attended = from_pairs(att[..., HEAD_SIZE:], seqs, 2).reshape(rows, 256)
     out_full = wo_all.reshape(width, 256)
-    gu_full = ffn_full[:, : 2 * unit_half]
-    dn_full = ffn_full[:, 2 * unit_half :]
     cot_rows = cot_all.reshape(2 * rows, width)
-
     attn_part = last_dims(attended, out_full).astype(BF16)
     inputs_own = mine(inputs)
-    residual, hidden_all = norm_step(
-        attn_part.reshape(4, own, width), inputs_own, gain_ffn.reshape(1, width)
-    )
-    hidden_ffn = hidden_all.reshape(2 * rows, width)
-
-    gu_raw = jnp.dot(hidden_ffn, gu_full, preferred_element_type=F32)
-    gate_raw, up_raw = gu_raw[:, :unit_half], gu_raw[:, unit_half:]
-    sigmoid = jax.nn.sigmoid(gate_raw)
-    activated = gate_raw * sigmoid
-    hidden_units = (activated * up_raw).astype(BF16)
-    grad_units = jnp.dot(cot_rows, dn_full, preferred_element_type=F32)
-    grad_gate_in = grad_units * up_raw * sigmoid * (1.0 + gate_raw * (1.0 - sigmoid))
-    grad_up_in = grad_units * activated
-    grad_gu_in = jnp.concatenate([grad_gate_in, grad_up_in], axis=1).astype(BF16)
-    ffn_back = last_dims(grad_gu_in, gu_full).astype(BF16)
     cot_own = mine(cotangent.reshape(rows, width))
-    grad_residual, ffn_gain_part, residual_all = norm_back_step(
-        ffn_back.reshape(4, 2, own, width), residual, cot_own, gain_ffn.reshape(1, width)
-    )
+    residual, grad_residual, ffn_gain_part, residual_all, ffn_grads, ffn_part = feed_step(
+        attn_part.reshape(4, own, width),
+        inputs_own,
+        gain_ffn.reshape(1, width),
+        ffn_full,
+        cot_rows,
+        cot_own,
+    )
+    grads_own = lax.psum_scatter(ffn_grads, "ctx", axis_index_groups=planes, tiled=True)
     residual_bf = residual_all.reshape(rows, width)
 
     grad_attended = jnp.dot(residual_bf, out_full, preferred_element_type=F32).astype(BF16)
     do_src = to_pairs(grad_attended.reshape(seqs, tokens, 4, HEAD_SIZE), 2, False)
-    grad_out = first_dims(residual_bf, attended).astype(BF16)
-    grad_gu = first_dims(hidden_ffn, grad_gu_in).astype(BF16)
-    grad_dn = first_dims(cot_rows, hidden_units).astype(BF16)
-    ffn_part = last_dims(hidden_units, dn_full).astype(BF16)
-    grads_own = lax.psum_scatter(
-        jnp.concatenate([grad_gu, grad_out, grad_dn], axis=1),
-        "ctx",
-        axis_index_groups=planes,
-        tiled=True,
-    )
     dq_all, dkv_all, ffn_parts = backward(
-        do_src, q_buf, kv_buf, o_buf, log_buf, ffn_part.reshape(8, own, width)
+        do_src, q_buf, kv_buf, o_buf, log_buf, ffn_part
     )
 
     output_own = (residual + jnp.sum(ffn_parts.astype(F32), axis=0)).astype(BF16)
@@ -900,43 +937,44 @@
     query_in = head_back(gq, query_hat, query_scale, gain_query).astype(BF16).reshape(rows, 256)
     key_in = head_back(gk, key_hat, key_scale, gain_key).astype(BF16).reshape(rows, 128)
     grad_in = jnp.concatenate([query_in, key_in, value_in], axis=1)
-    grad_qkv = first_dims(hidden_attn, grad_in).astype(BF16)
     attn_back = last_dims(grad_in, qkv_full)
     attn_gain_part = jnp.sum(attn_back * normed_attn, axis=0)
-    gain_parts = jnp.zeros((NCTX, 8, 128), F32)
-    gain_parts = gain_parts.at[:, 0, :32].set(attn_gain_part.reshape(NCTX, 32))
-    gain_parts = gain_parts.at[:, 1, :32].set(ffn_gain_part.reshape(NCTX, 32))
-    gain_parts = gain_parts.at[:, 2, :2].set(query_gain_part.reshape(NCTX, 2))
-    gain_parts = gain_parts.at[:, 3, :2].set(key_gain_part.reshape(NCTX, 2))
-    qkv_grad, output_all, input_all, gain_tp = last_step(
+
+    def placed(row, part):
+        part = part.reshape(NCTX, 1, -1)
+        return jnp.pad(part, ((0, 0), (row, 7 - row), (0, 128 - part.shape[2])))
+
+    gain_parts = placed(0, attn_gain_part) + placed(1, ffn_gain_part)
+    gain_parts = gain_parts + placed(2, query_gain_part) + placed(3, key_gain_part)
+    qkv_grad, pair_grads, output_all, input_all, gain_tp = last_step(
         attn_back.astype(BF16).reshape(4, own, width),
-        grad_qkv.reshape(4, 4, 2, 2, 16, 512),
+        hidden_attn,
+        grad_in,
+        residual_bf,
+        attended,
+        grads_own.reshape(2, 32, -1),
         gain_parts.reshape(4, 4, 2, 8, 128),
         output_own,
         grad_residual,
         inputs_own,
         gain_attn.reshape(1, width),
     )
-    (pair_grads,) = exchange(9, ["pair"], [("pair", "own", grads_own.reshape(2, 32, -1))])
     pair_grads = pair_grads.astype(F32)
     gain_sum = jnp.sum(gain_tp, axis=0)
-    qkv_grad = qkv_grad.reshape(32, 512)
-    gu, end = 2 * unit_half, 2 * unit_half + 256
-    out_grad = jnp.sum(pair_grads[:, :, gu:end], axis=0)
-
-    def joined(first, last):
+    qkv_grad = qkv_grad.reshape(32, 768)
+
+    def joined(first):
+        last = first + unit_half
         return jnp.concatenate([pair_grads[0, :, first:last], pair_grads[1, :, first:last]], axis=1)
 
-    gate_grad = joined(0, unit_half)
-    up_grad = joined(unit_half, gu)
-    down_grad = joined(end, end + unit_half)
+    gate_grad, up_grad, down_grad = joined(0), joined(UNITS), joined(2 * UNITS)
     return (
         output_all.reshape(seqs, tokens, width),
         input_all.astype(F32).reshape(seqs, tokens, width),
         qkv_grad[:, :256],
         qkv_grad[:, 256:384],
-        qkv_grad[:, 384:],
-        out_grad,
+        qkv_grad[:, 384:512],
+        qkv_grad[:, 512:],
         gate_grad,
         up_grad,
         down_grad,

time: 305 us -> 289 us (0.948)
  matrix products: 25.9 us -> 4.81 us
  Pallas kernels: 204 us -> 195 us
  local copies, waits for them, and re-layouts: 37.9 us -> 45.3 us
  other arithmetic: 20.6 us -> 26.4 us
    dot_general x6 -> x0, matrix products: 15.7 us -> none  [the longest x4 8.59 us: first_dims(): lax.dot_general(a, b, (((0,), (0,)), ((), ())), preferred_element_type=F32)]
    unnamed x105 -> x92, local copies, waits for them, and re-layouts: 6.2 us -> 19 us
    pallas_call x3 -> x1, Pallas kernels: 47.9 us -> 37.6 us  [feed_step(): pl.pallas_call(feed_body, out_shape=[jax.ShapeDtypeStruct((own, width), F...]
    scatter x6 -> x0, local copies, waits for them, and re-layouts: 6.48 us -> none  [the longest x2 2.13 us: local(): gains = gains.at[0:2, 0:32].set(norm_gains).at[2:4, 0:2].set(head_gains)]
    dot_general x4 -> x2, matrix products: 8.19 us -> 2.84 us  [last_dims(): lax.dot_general(a, b, (((1,), (1,)), ((), ())), preferred_element_type=F32)]
    concatenate x1, other arithmetic: 3.79 us -> 0.03 us  [local(): grad_in = jnp.concatenate([query_in, key_in, value_in], axis=1)]
    pallas_call x1, Pallas kernels: 25.8 us -> 29 us  [last_step(): pl.pallas_call(last_body, out_shape=[jax.ShapeDtypeStruct((2, *piece), F3...]
    reshape x0 -> x5, local copies, waits for them, and re-layouts: none -> 3.08 us  [the longest x4 2.17 us: placed(): part = part.reshape(NCTX, 1, -1)]
  transfers between devices with their start and end apart: 2 -> 2, of which waited for: 0 -> 0; matrix products, arithmetic and copies ran while one was open for 14% -> 15% of each run, Pallas kernels for 50% -> 36%
where the time goes in v5:
time: 289 us; the launch traced here: 286 us
  Pallas kernels  195 us (67%)
  local copies, waits for them, and re-layouts  45.3 us (16%)
  other arithmetic  26.4 us (9%)
  between operations  14.9 us (5%)
  matrix products  4.81 us (2%)
    pallas_call x1, Pallas kernels, backward(): pl.pallas_call(backward_body, out_shape=[jax.ShapeDtypeStruct((SLOTS, 2 *...  61.7 us
    pallas_call x1, Pallas kernels, forward(): pl.pallas_call(forward_body, out_shape=[stack, stack, jax.ShapeDtypeStruc...  42.8 us
    pallas_call x1, Pallas kernels, feed_step(): pl.pallas_call(feed_body, out_shape=[jax.ShapeDtypeStruct((own, width), F...  37.6 us
    pallas_call x1, Pallas kernels, last_step(): pl.pallas_call(last_body, out_shape=[jax.ShapeDtypeStruct((2, *piece), F3...  29 us
    pallas_call x1, Pallas kernels, gather(): pl.pallas_call(gather_body, out_shape=[jax.ShapeDtypeStruct((4, 4, 2, *w....  23.9 us
    unnamed x92, local copies, waits for them, and re-layouts  19 us
  transfers between devices with their start and end apart: 2, of which 0 were waited for; matrix products, arithmetic and copies ran while one was open for 15% of the time, Pallas kernels for 36%

profile of v5, /device:TPU:0, one launch (start us, length us, event | category | flops | bytes accessed | tf_op | source)
XLA Modules:
  0.0 286.5 jit_solution(6513727243289409923)
XLA Ops:
  7.2 1.1 stack.14
  8.4 1.0 stack.13
  9.6 1.0 stack.12
  11.4 0.9 reshape.360.ffn
  12.3 1.3 pad_add_fusion.1.gains
  13.6 1.4 pad_maximum_fusion.6
  14.9 23.9 %gather.1 = (bf16[4,4,2,2,16,512]{5,4,3,2,1,0:T(8,128)(2,1)}, bf16[4,4,2,16,128]{4,3,2,1,0:T(8,128)(2,1)}, bf16[2,32,1920]{2,1,0:T(8,128)(2,1)}) custom-call(bf16[2,16,512]{2,1,0:T(8,128)(2,1)} %bitcast.194, bf16[16,128]{1,0:T(8,128)(2,1)} %pad_add_fusion.1.gains, bf16[2,32,1920]{2,1,0:T(8,128)(2,1)} %reshape.360.ffn), custom_call_target="tpu_custom_call" | custom-call | tf_op jit(solution)/shard_map/gather/pallas_call | solution.py:201
  39.0 0.9 fusion.9
  40.6 1.2 multiply_reduce_fusion.1
  42.6 1.7 fusion.13
  44.4 0.7 copy-done.24
  45.4 1.0 fusion.10
  46.7 0.8 broadcast_multiply_fusion
  49.7 42.8 %attention_forward.1 = (bf16[4,256,128]{2,1,0:T(8,128)(2,1)S(1)}, bf16[4,256,128]{2,1,0:T(8,128)(2,1)S(1)}, bf16[4,4,2,2,64,128]{5,4,3,2,1,0:T(8,128)(2,1)S(1)},...) custom-call(bf16[4,256,128]{2,1,0:T(8,128)(2,1)S(1)} %pad.39.q_src, ...), custom_call_target="tpu_custom_call" | custom-call | tf_op jit(solution)/shard_map/attention_forward/pallas_call | solution.py:455
  92.5 1.0 copy-done.2
  94.4 0.8 reshape.398.gain
  95.3 1.1 bitcast_convert_fusion.1
  96.9 2.1 copy-done
  99.0 37.6 %feed_forward.1 = (f32[64,1024]{1,0:T(8,128)S(1)}, f32[64,1024]{1,0:T(8,128)S(1)}, f32[1,1024]{1,0:T(1,128)S(1)}, bf16[4,64,1024]{2,1,0:T(8,128)(2,1)S(1)}, bf16...) custom-call(bf16[4,64,1024]{2,1,0:T(8,128)(2,1)S(1)} %bitcast.146, ...), custom_call_target="tpu_custom_call" | custom-call | tf_op jit(solution)/shard_map/feed_forward/pallas_call | solution.py:673
  136.6 1.9 copy-done.1
  138.5 1.0 copy-done.4
  139.5 0.7 copy-done.8
  140.2 0.7 copy-done.11
  140.9 0.9 copy-done.28
  142.6 0.8 copy.98
  144.1 0.8 copy.92
  144.9 0.7 mul.363
  146.2 1.0 copy.105.attended
  148.1 1.2 copy-done.5
  149.3 0.9 copy-done.14
  150.2 0.9 copy-done.16
  151.2 61.7 %attention_backward.1 = (bf16[4,256,128]{2,1,0:T(8,128)(2,1)S(1)}, bf16[4,2,64,128]{3,2,1,0:T(8,128)(2,1)S(1)}, bf16[8,64,1024]{2,1,0:T(8,128)(2,1)S(1)}) custom-call(bf16[4,256,128]{2,1,0:T(8,128)(2,1)S(1)} %pad.40.do_src, bf16[4,256,128]{2,1,0:T(8,128)(2,1)S(1)} %copy-done.14, bf16[4,4,2,2,64,128]{5,4,3,2,1,0:T(8,128)(2,1)S(1)} %copy-done.3, ...), custom_call_target="tpu_custom_call" | custom-call | tf_op jit(solution)/shard_map/attention_backward/pallas_call | solution.py:540
  213.8 0.7 reshape.412
  214.7 0.8 multiply_subtract_fusion.1
  215.5 1.1 pad_maximum_fusion.5
  216.7 0.8 copy.95
  217.5 0.8 copy.97
  218.2 1.8 convert_bitcast_fusion
  220.0 1.2 copy.88
  221.3 0.9 multiply_subtract_fusion
  222.1 1.6 pad_maximum_fusion
  223.8 0.8 copy.89
  224.6 0.7 broadcast_multiply_fusion.1
  225.4 0.8 copy.91
  226.2 1.8 multiply_reduce_fusion.5
  228.6 0.7 reduce_sum.115
  229.3 0.7 reshape.389
  230.0 2.3 multiply_reduce_fusion.2
  232.4 0.8 reduce_sum.111
  233.2 0.7 reshape.388
  235.1 0.7 reshape.387
  235.8 2.5 multiply_reduce_fusion
  238.3 0.8 pad_add_fusion
  239.5 1.0 copy-done.7
  240.6 0.9 copy-done.9
  241.5 0.9 copy-done.17
  242.4 29.0 %last_step.1 = (f32[2,16,768]{2,1,0:T(8,128)S(1)}, bf16[2,32,1920]{2,1,0:T(8,128)(2,1)S(1)}, bf16[4,64,1024]{2,1,0:T(8,128)(2,1)S(1)}, bf16[4,64,1024]{2,1,0:T(8,128)(2,1)S(1)}, f32[4,8,128]{2,1,0:T(8,128)S(1)}) custom-call(bf16[4,64,1024]{2,1,0:T(8,128)(2,1)S(1)} %bitcast.159, bf16[256,1024]{1,0:T(8,128)(2,1)S(1)} %copy-done.7, ...), custom_call_target="tpu_custom_call" | custom-call | tf_op jit(solution)/shard_map/last_step/pallas_call | solution.py:780
  271.4 0.7 copy-done.18
  274.5 1.1 bitcast_convert_fusion
  275.6 1.0 convert_element_type.160
  276.6 0.8 pad_maximum_fusion.2
  277.4 0.8 pad_maximum_fusion.3
  278.1 0.8 pad_maximum_fusion.4
  278.9 0.8 copy.143
  (155 shorter events, 15.5 us)
Async XLA Ops:
  7.2 35.2 %copy-start.20 = (bf16[2,128,1024]{2,1,0:T(8,128)(2,1)S(1)}, bf16[2,128,1024]{2,1,0:T(8,128)(2,1)}, u32[]{:S(2)}) copy-start(bf16[2,128,1024]{2,1,0:T(8,128)(2,1)} %param.11) | copy-start | bytes 1572868
  7.2 89.7 %all-gather.2.cloned.1.call-start = ((), (), s32[]{:S(2)}) async-start(), calls=%async_computation.1 | async-start | bytes 4177920 | tf_op jit(solution)/shard_map/all_gather | solution.py:876
  38.9 200.6 %reduce-scatter.2.cloned.1.call-start = ((), (), s32[]{:S(2)}) async-start(), calls=%async_computation.2 | async-start | bytes 4177920 | tf_op jit(solution)/shard_map/reduce_scatter | solution.py:919
  40.5 2.1 copy-start.34
  40.6 2.0 copy-start.36
  44.3 0.8 copy-start.24
  44.3 5.4 %copy-start.6 = (bf16[2,128,1024]{2,1,0:T(8,128)(2,1)S(1)}, bf16[2,128,1024]{2,1,0:T(8,128)(2,1)}, u32[]{:S(2)}) copy-start(bf16[2,128,1024]{2,1,0:T(8,128)(2,1)} %param.12) | copy-start | bytes 1572868
  44.3 5.4 %copy-start.19 = (bf16[32,256]{1,0:T(8,128)(2,1)S(1)}, bf16[32,256]{1,0:T(8,128)(2,1)}, u32[]{:S(2)}) copy-start(bf16[32,256]{1,0:T(8,128)(2,1)} %param.16) | copy-start | bytes 49156
  45.4 3.8 %copy-start.22 = (f32[2,128,4,64]{1,0,3,2:T(2,128)}, f32[2,128,4,64]{1,0,3,2:T(2,128)S(1)}, u32[]{:S(2)}) copy-start(f32[2,128,4,64]{1,0,3,2:T(2,128)S(1)} %reshape.363) | copy-start | bytes 786436
  46.5 1.1 copy-start.38
  47.4 2.3 copy-start.31
  48.4 1.3 copy-start.26
  48.6 0.6 copy-start.39
  92.5 1.0 copy-start.2
  93.5 0.7 copy-start.13
  93.5 0.8 copy-start.15
  94.4 2.5 copy-start.27
  96.9 2.1 copy-start
  136.6 1.9 copy-start.1
  138.5 1.0 copy-start.4
  139.5 0.7 copy-start.8
  140.2 0.7 copy-start.11
  140.9 0.9 copy-start.28
  140.9 1.6 copy-start.35
  140.9 2.5 copy-start.40
  140.9 7.1 %copy-start.3 = (bf16[4,4,2,2,64,128]{5,4,3,2,1,0:T(8,128)(2,1)S(1)}, bf16[4,4,2,2,64,128]{5,4,3,2,1,0:T(8,128)(2,1)}, u32[]{:S(2)}) copy-start(bf16[4,4,2,2,64,128]{5,4,3,2,1,0:T(8,128)(2,1)} %copy-done.2) | copy-start | bytes 3145732
  148.1 1.2 copy-start.5
  149.3 0.9 copy-start.14
  150.2 0.9 copy-start.16
  212.9 0.7 copy-start.10
  212.9 9.3 %copy-start.23 = (f32[2,128,4,64]{1,0,3,2:T(2,128)S(1)}, f32[2,128,4,64]{1,0,3,2:T(2,128)}, u32[]{:S(2)}) copy-start(f32[2,128,4,64]{1,0,3,2:T(2,128)} %copy-done.22) | copy-start | bytes 786436
  213.8 12.4 %copy-start.25 = (f32[256,512]{1,0:T(8,128)S(1)}, f32[256,512]{1,0:T(8,128)}, u32[]{:S(2)}) copy-start(f32[256,512]{1,0:T(8,128)} %copy-done.24) | copy-start | bytes 1572868
  217.4 18.4 %copy-start.21 = (bf16[2,128,1024]{2,1,0:T(8,128)(2,1)S(1)}, bf16[2,128,1024]{2,1,0:T(8,128)(2,1)}, u32[]{:S(2)}) copy-start(bf16[2,128,1024]{2,1,0:T(8,128)(2,1)} %param.11) | copy-start | bytes 1572868
  217.4 18.4 %copy-start.37 = (f32[1024]{0:T(1024)S(1)}, f32[1024]{0:T(1024)}, u32[]{:S(2)}) copy-start(f32[1024]{0:T(1024)} %copy-done.36) | copy-start | bytes 12292
  222.1 7.9 %copy-start.29 = (f32[256,256]{1,0:T(8,128)S(1)}, f32[256,256]{1,0:T(8,128)}, u32[]{:S(2)}) copy-start(f32[256,256]{1,0:T(8,128)} %copy.92) | copy-start | bytes 786436
  226.2 13.2 %copy-start.12 = (f32[64,1024]{1,0:T(8,128)S(1)}, f32[64,1024]{1,0:T(8,128)}, u32[]{:S(2)}) copy-start(f32[64,1024]{1,0:T(8,128)} %copy-done.11) | copy-start | bytes 786436
  232.4 6.8 %copy-start.30 = (bf16[256,256]{1,0:T(8,128)(2,1)S(1)}, bf16[256,256]{1,0:T(8,128)(2,1)}, u32[]{:S(2)}) copy-start(bf16[256,256]{1,0:T(8,128)(2,1)} %get-tuple-element.62) | copy-start | bytes 393220
  232.4 6.8 %copy-start.32 = (bf16[256,128]{1,0:T(8,128)(2,1)S(1)}, bf16[256,128]{1,0:T(8,128)(2,1)}, u32[]{:S(2)}) copy-start(bf16[256,128]{1,0:T(8,128)(2,1)} %reshape.412) | copy-start | bytes 196612
  232.4 6.8 %copy-start.33 = (bf16[256,128]{1,0:T(8,128)(2,1)S(1)}, bf16[256,128]{1,0:T(8,128)(2,1)}, u32[]{:S(2)}) copy-start(bf16[256,128]{1,0:T(8,128)(2,1)} %get-tuple-element.64) | copy-start | bytes 196612
  239.5 1.0 copy-start.7
  240.6 0.9 copy-start.9
  241.5 0.9 copy-start.17
  271.4 0.7 copy-start.18
Sparse Core Ops, SparseCore 0:
  39.0 55.3 all-gather.1
  141.1 89.4 reduce-scatter.1

commit v6 on v5

--- a/solution.py
+++ b/solution.py
@@ -170,7 +170,78 @@
 SIZES = {"ctx": NCTX, "tp": 4, "pair": 2, "rows": 8, "z": 4, "x": 4, "core": 2, "ring": 4}
 
 
-def gather_body(w, gains, ffn, w_all, gains_all, ffn_pair, *sem):
+def iota(shape, axis):
+    return lax.broadcasted_iota(jnp.int32, shape, axis)
+
+
+def two_parts(v):
+    high = v.astype(BF16)
+    return high, (v - high.astype(F32)).astype(BF16)
+
+
+def exact_dot(v, pattern):
+    high, low = two_parts(v)
+    return jnp.dot(high, pattern, preferred_element_type=F32) + jnp.dot(
+        low, pattern, preferred_element_type=F32
+    )
+
+
+def head_mean(v):
+    n = v.shape[1]
+    same = lax.div(iota((n, n), 0), HEAD_SIZE) == lax.div(iota((n, n), 1), HEAD_SIZE)
+    return exact_dot(v, jnp.where(same, 1.0 / HEAD_SIZE, 0.0).astype(BF16))
+
+
+def head_scale(v):
+    return lax.rsqrt(head_mean(v * v) + EPSILON)
+
+
+def turned(u, cosine, sine):
+    half, n = HEAD_SIZE // 2, 2 * HEAD_SIZE
+    first = lax.rem(iota(u.shape, 1), HEAD_SIZE) < half
+    other = jnp.where(first, pltpu.roll(u, n - half, 1), pltpu.roll(u, half, 1))
+    return u * cosine + other * sine
+
+
+def crossed(tile):
+    return pltpu.roll(tile, HEAD_SIZE, 1)
+
+
+def left_lanes(tile):
+    return iota(tile.shape, 1) < HEAD_SIZE
+
+
+def spread_gain(pieces, row, per, lanes):
+    pattern = (lax.rem(iota((128, lanes), 1), per) == iota((128, lanes), 0)).astype(F32)
+    wide = jnp.dot(pieces, pattern.astype(BF16), preferred_element_type=F32)
+    r, lane = iota(wide.shape, 0), iota(wide.shape, 1)
+    owner = lax.div(lax.rem(lane, NCTX * per), per)
+    keep = jnp.logical_and(lax.rem(r, 16) == row, lax.div(r, 16) == owner)
+    return jnp.sum(jnp.where(keep, wide, 0.0), axis=0, keepdims=True)
+
+
+def owner_pieces(vector, per):
+    lanes = vector.shape[1]
+    shape = (NCTX, lanes)
+    owner = lax.div(lax.rem(iota(shape, 1), NCTX * per), per)
+    parts = jnp.where(owner == iota(shape, 0), jnp.broadcast_to(vector, shape), 0.0)
+    pattern = (lax.rem(iota((lanes, 128), 0), per) == iota((lanes, 128), 1)).astype(F32)
+    return exact_dot(parts, pattern.astype(BF16))
+
+
+def row_scale(rows):
+    return lax.rsqrt(jnp.mean(rows * rows, axis=1, keepdims=True) + EPSILON)
+
+
+def twice(table):
+    return jnp.concatenate([table[...], table[...]], axis=0)
+
+
+def gather_body(
+    w, gains, ffn, rows_in, cosine, sine,
+    w_all, ffn_pair, hidden, raw, q_src, kv_src, gain_attn, gain_ffn, gain_query, gain_key,
+    gains_all, *sem,
+):
     z, x, h = position()
     take = Sems(sem)
     greet(["z", "x", "pair"])
@@ -194,23 +265,62 @@
         ("x", lambda p: w_all.at[:, x, :, 1], lambda q: w_all.at[:, q, :, 1], *take.two()),
         ("z", lambda p: gains_all.at[z], lambda q: gains_all.at[q], *take.two()),
     )
+    pieces = gains_all[...].reshape(NCTX * 16, 128)
+    gain_attn[...] = spread_gain(pieces, 0, 32, gain_attn.shape[1])
+    gain_ffn[...] = spread_gain(pieces, 1, 32, gain_ffn.shape[1])
+    gain_query[...] = spread_gain(pieces, 2, 2, 128)
+    gain_key[...] = spread_gain(pieces, 3, 2, 128)
+    rows = rows_in[...].astype(F32)
+    hidden[...] = (rows * row_scale(rows) * gain_attn[...]).astype(BF16)
+    weights = w_all[...].reshape(hidden.shape[1], w_all.shape[5])
+    raw[...] = jnp.dot(hidden[...], weights, preferred_element_type=F32)
+    cos, sin = twice(cosine), twice(sine)
+    for k in range(2):
+        tile = raw[:, k * 128 : k * 128 + 128]
+        tile = turned(tile * head_scale(tile) * gain_query[...], cos, sin) * (HEAD_SIZE**-0.5)
+        for a, one in enumerate((tile, crossed(tile))):
+            one = jnp.where(left_lanes(one), one, 0.0).astype(BF16)
+            for s in range(2):
+                q_src[2 * k + s, a * BLOCK : (a + 1) * BLOCK] = one[s * BLOCK : (s + 1) * BLOCK]
+    tile = raw[:, 256:384]
+    keys = turned(tile * head_scale(tile) * gain_key[...], cos, sin)
+    values = raw[:, 384:512]
+    for k in range(2):
+        key, value = (keys, crossed(values)) if k == 0 else (crossed(keys), values)
+        one = jnp.where(left_lanes(key), key, value).astype(BF16)
+        for s in range(2):
+            part = one[s * BLOCK : (s + 1) * BLOCK]
+            kv_src[2 * k + s] = part.reshape(2, BLOCK // 2, 128)
     settle(*swap)
 
 
-def gather(w, gains, ffn):
+def gather(w, gains, ffn, rows_in, cosine, sine):
+    rows, width = rows_in.shape
+    vector = jax.ShapeDtypeStruct((1, width), F32)
+    short = jax.ShapeDtypeStruct((1, 128), F32)
     return pl.pallas_call(
         gather_body,
         out_shape=[
             jax.ShapeDtypeStruct((4, 4, 2, *w.shape), BF16),
-            jax.ShapeDtypeStruct((4, 4, 2, *gains.shape), BF16),
             jax.ShapeDtypeStruct(ffn.shape, BF16),
+            jax.ShapeDtypeStruct((rows, width), BF16),
+            jax.ShapeDtypeStruct((rows, w.shape[2]), F32),
+            jax.ShapeDtypeStruct((PAIRS, 2 * BLOCK, BLOCK), BF16),
+            jax.ShapeDtypeStruct((PAIRS, 2, BLOCK // 2, BLOCK), BF16),
+            vector,
+            vector,
+            short,
+            short,
         ],
-        in_specs=[ANY] * 3,
-        out_specs=[VMEM, VMEM, ANY],
-        scratch_shapes=sems(["pair"] * 3 + ["x", "z", "x", "z", "x", "z"]),
-        compiler_params=pltpu.CompilerParams(collective_id=1, has_side_effects=True),
+        in_specs=[ANY] * 3 + [VMEM] * 3,
+        out_specs=[VMEM, ANY] + [VMEM] * 8,
+        scratch_shapes=[pltpu.VMEM((4, 4, 2, *gains.shape), BF16)]
+        + sems(["pair"] * 3 + ["x", "z", "x", "z", "x", "z"]),
+        compiler_params=pltpu.CompilerParams(
+            collective_id=1, has_side_effects=True, vmem_limit_bytes=24 * 2**20
+        ),
         name="gather",
-    )(w, gains, ffn)
+    )(w, gains, ffn, rows_in, cosine, sine)
 
 
 def piece_shape(pick, array):
@@ -223,29 +333,6 @@
 
 def sems(kinds):
     return [pltpu.SemaphoreType.DMA((SIZES[k],)) for k in kinds for _ in range(2)]
-
-
-def exchange_body(plan, kinds, *refs):
-    n = len(plan)
-    srcs, dsts, rest = refs[:n], refs[n : 2 * n], refs[2 * n :]
-    greet(kinds)
-    for k, (kind, pick) in enumerate(plan):
-        begin(kind, pick, srcs[k], dsts[k], rest[2 * k], rest[2 * k + 1])
-    for k, (kind, pick) in enumerate(plan):
-        finish(kind, pick, srcs[k], dsts[k], rest[2 * k], rest[2 * k + 1])
-
-
-def exchange(number, kinds, items):
-    plan = tuple((kind, pick) for kind, pick, _ in items)
-    return pl.pallas_call(
-        functools.partial(exchange_body, plan, kinds),
-        out_shape=[landing(*item) for item in items],
-        in_specs=[ANY] * len(items),
-        out_specs=[ANY] * len(items),
-        scratch_shapes=sems([kind for kind, _ in plan]),
-        compiler_params=pltpu.CompilerParams(collective_id=number, has_side_effects=True),
-        name=f"exchange{number}",
-    )(*[array for _, _, array in items])
 
 
 def places():
@@ -569,10 +656,6 @@
     )(do_src, q_buf, kv_buf, o_buf, log_buf, ffn)
 
 
-def row_scale(rows):
-    return lax.rsqrt(jnp.mean(rows * rows, axis=1, keepdims=True) + EPSILON)
-
-
 def row_back(grads, normed, scale, gain):
     scaled = grads * gain
     return scale * (scaled - normed * jnp.mean(scaled * normed, axis=1, keepdims=True))
@@ -589,13 +672,23 @@
 
 
 def feed_body(
-    parts, inputs, gain, w, cot, cot_own,
-    residual, grad_residual, gain_part, grad_all, grads, ffn_part,
-    landed, hidden, hidden_all, grad_units, units, grad_in, back, halved, chip, ringed, grad_bf, *sem,
+    att, wo, rows_in, gain, w, cot,
+    attended, do_src, residual, grad_residual, gain_part, grad_all, grads, ffn_part,
+    parts, landed, hidden, hidden_all, grad_units, units, grad_in, back, halved, chip, ringed, grad_bf, *sem,
 ):
     take = Sems(sem)
-    core = lax.rem(lax.axis_index("tp"), 2)
+    t = lax.axis_index("tp")
+    core, h = lax.rem(t, 2), lax.rem(lax.axis_index("ctx"), 2)
+    own = residual.shape[0]
     greet(["tp", "ring"])
+    for k in range(2):
+        for s in range(2):
+            first = crossed(att[2 * k + s, :BLOCK].astype(F32))
+            second = att[2 * k + s, BLOCK:].astype(F32)
+            one = jnp.where(left_lanes(first), first, second).astype(BF16)
+            attended[s * BLOCK : (s + 1) * BLOCK, k * 128 : (k + 1) * 128] = one
+    out_full = wo[...].reshape(wo.size // wo.shape[5], wo.shape[5])
+    parts[...] = last_dims(attended[...], out_full).astype(BF16).reshape(parts.shape)
     share = ("tp", lambda p: parts.at[p], lambda q: landed.at[q], *take.two(), True)
     push(*share)
 
@@ -605,7 +698,8 @@
         grad_units[at] = jnp.dot(cot[at], w[:, 2 * UNITS :], preferred_element_type=F32)
 
     settle(*share)
-    rows = inputs[...] + summed(landed)
+    inputs = rows_in[pl.ds(pl.multiple_of(t * own, own), own)].astype(F32)
+    rows = inputs + summed(landed)
     residual[...] = rows
     scale = row_scale(rows)
     hidden[...] = (rows * scale * gain[...]).astype(BF16)
@@ -652,7 +746,8 @@
     rows = residual[...]
     scale = row_scale(rows)
     normed = rows * scale
-    result = cot_own[...].astype(F32) + row_back(total, normed, scale, gain[...])
+    cot_own = cot[pl.ds(pl.multiple_of((h * 4 + t) * own, own), own)].astype(F32)
+    result = cot_own + row_back(total, normed, scale, gain[...])
     grad_bf[...] = result.astype(BF16)
     last = ("tp", lambda p: grad_bf, lambda q: grad_all.at[q], *take.two(), True)
     push(*last)
@@ -665,14 +760,24 @@
         grads[at, 2 * UNITS :] = first_dims(cot[:, at], units[...]).astype(BF16)
 
     settle(*last)
-
-
-def feed_step(parts, inputs, gain, w, cot, cot_own):
-    own, width = inputs.shape
-    rows = cot.shape[0]
+    grad = jnp.dot(grad_all[...].reshape(4 * own, gain.shape[1]), out_full, preferred_element_type=F32)
+    for k in range(2):
+        for s in range(2):
+            tile = grad[s * BLOCK : (s + 1) * BLOCK, k * 128 : (k + 1) * 128]
+            for a, one in enumerate((crossed(tile), tile)):
+                one = jnp.where(left_lanes(one), 0.0, one).astype(BF16)
+                do_src[2 * k + s, a * BLOCK : (a + 1) * BLOCK] = one
+
+
+def feed_step(att, wo, rows_in, gain, w, cot):
+    rows, width = rows_in.shape
+    own = rows // 4
+    wide = cot.shape[0]
     return pl.pallas_call(
         feed_body,
         out_shape=[
+            jax.ShapeDtypeStruct((rows, wo.shape[5]), BF16),
+            jax.ShapeDtypeStruct(att.shape, BF16),
             jax.ShapeDtypeStruct((own, width), F32),
             jax.ShapeDtypeStruct((own, width), F32),
             jax.ShapeDtypeStruct((1, width), F32),
@@ -681,14 +786,15 @@
             jax.ShapeDtypeStruct((8, own, width), BF16),
         ],
         in_specs=[VMEM] * 6,
-        out_specs=[VMEM] * 6,
+        out_specs=[VMEM] * 8,
         scratch_shapes=[
+            pltpu.VMEM((4, own, width), BF16),
             pltpu.VMEM((4, own, width), BF16),
             pltpu.VMEM((own, width), BF16),
             pltpu.VMEM((4, 2, own, width), BF16),
-            pltpu.VMEM((rows, UNITS), F32),
-            pltpu.VMEM((rows, UNITS), BF16),
-            pltpu.VMEM((rows, 2 * UNITS), BF16),
+            pltpu.VMEM((wide, UNITS), F32),
+            pltpu.VMEM((wide, UNITS), BF16),
+            pltpu.VMEM((wide, 2 * UNITS), BF16),
             pltpu.VMEM((4, 2, own, width), BF16),
             pltpu.VMEM((2, 4, own, width), BF16),
             pltpu.VMEM((4, own, width), BF16),
@@ -700,17 +806,60 @@
             collective_id=3, has_side_effects=True, vmem_limit_bytes=40 * 2**20
         ),
         name="feed_forward",
-    )(parts, inputs, gain, w, cot, cot_own)
+    )(att, wo, rows_in, gain, w, cot)
 
 
 def last_body(
-    parts, hidden, grad_in, res_rows, attended, ffn, gains, output, grad_residual, inputs, gain,
+    dq, dkv, raw, w_all, cosine, sine, gain_query, gain_key,
+    hidden, res_all, attended, ffn, ffn_parts, ffn_gain, residual, grad_residual, rows_in, gain,
     qkv_grad, ffn_all, output_all, input_all, gain_tp,
-    qkv, landed, input_bf, one_a, one_b, one_g, sum_a, sum_b, sum_g, two_a, two_b, two_g,
+    parts, grad_in, gains, output, qkv, landed, input_bf, one_a, one_b, one_g, sum_a, sum_b, sum_g, two_a, two_b, two_g,
     part_a, part_b, part_g, three_a, three_b, three_g, gain_sum, *sem,
 ):
     take = Sems(sem)
     greet(["z", "x", "pair", "tp"])
+    t = lax.axis_index("tp")
+    own, width = residual.shape
+    cos, sin = twice(cosine), -twice(sine)
+
+    def head_back(u, tile, gain_row):
+        turn = turned(u, cos, sin)
+        scale = head_scale(tile)
+        hat = tile * scale
+        scaled = turn * gain_row
+        back = scale * (scaled - hat * head_mean(scaled * hat))
+        return back.astype(BF16), jnp.sum(turn * hat, axis=0, keepdims=True)
+
+    def both(first, second):
+        return jnp.concatenate([first.astype(F32), second.astype(F32)], axis=0)
+
+    query_gain = jnp.zeros((1, 128), F32)
+    for k in range(2):
+        first = both(dq[2 * k, :BLOCK], dq[2 * k + 1, :BLOCK])
+        second = crossed(both(dq[2 * k, BLOCK:], dq[2 * k + 1, BLOCK:]))
+        lanes = slice(k * 128, (k + 1) * 128)
+        back, part = head_back(
+            jnp.where(left_lanes(first), first, second), raw[:, lanes], gain_query[...]
+        )
+        grad_in[:, lanes] = back
+        query_gain = query_gain + part
+    first, second = [
+        both(dkv[2 * k].reshape(BLOCK, 128), dkv[2 * k + 1].reshape(BLOCK, 128)) for k in range(2)
+    ]
+    left = left_lanes(first)
+    back, key_gain = head_back(
+        jnp.where(left, first, crossed(second)), raw[:, 256:384], gain_key[...]
+    )
+    grad_in[:, 256:384] = back
+    grad_in[:, 384:] = jnp.where(left, crossed(first), second).astype(BF16)
+    attn_gain = jnp.zeros((1, width), F32)
+    weights = w_all[...].reshape(width, grad_in.shape[1])
+    for q in range(4):
+        at = slice(q * own, (q + 1) * own)
+        back = last_dims(grad_in[at], weights)
+        parts[q] = back.astype(BF16)
+        rows = rows_in[at].astype(F32)
+        attn_gain = attn_gain + jnp.sum(back * (rows * row_scale(rows)), axis=0, keepdims=True)
     rows_sums, rows_output, rows_input, gains_out = [take.two() for _ in range(4)]
     begin("tp", "own", parts, landed, *rows_sums)
 
@@ -718,11 +867,18 @@
     def _(m):
         at = pl.ds(pl.multiple_of(m * 256, 256), 256)
         wide = grad_in.shape[1]
+        res_rows = res_all[:, :, at].reshape(4 * own, 256)
         step = first_dims(hidden[:, at], grad_in[...]).astype(BF16)
         qkv[m, :, :, :, :, :wide] = step.reshape(4, 2, 2, 16, wide)
-        step = first_dims(res_rows[:, at], attended[...]).astype(BF16)
+        step = first_dims(res_rows, attended[...]).astype(BF16)
         qkv[m, :, :, :, :, wide:] = step.reshape(4, 2, 2, 16, attended.shape[1])
 
+    pieces = jnp.zeros((NCTX, 8, 128), F32)
+    vectors = ((attn_gain, 32), (ffn_gain[...], 32), (query_gain, 2), (key_gain, 2))
+    for row, (vector, per) in enumerate(vectors):
+        piece = jnp.broadcast_to(owner_pieces(vector, per)[:, None, :], pieces.shape)
+        pieces = jnp.where(iota(pieces.shape, 1) == row, piece, pieces)
+    gains[...] = pieces.reshape(gains.shape)
     first = [
         ("x", lambda p: qkv.at[:, p, :, 0], lambda q: one_a.at[q], *take.two(), True),
         ("z", lambda p: qkv.at[p, :, :, 1], lambda q: one_b.at[q], *take.two(), True),
@@ -730,7 +886,8 @@
     ]
     for move in first:
         push(*move)
-    rows = inputs[...]
+    output[...] = (residual[...] + summed(ffn_parts)).astype(BF16)
+    rows = rows_in[pl.ds(pl.multiple_of(t * own, own), own)].astype(F32)
     scale = row_scale(rows)
     normed = rows * scale
     finish("tp", "own", parts, landed, *rows_sums)
@@ -769,10 +926,12 @@
 
 
 def last_step(
-    parts, hidden, grad_in, res_rows, attended, ffn, gains, output, grad_residual, inputs, gain
+    dq, dkv, raw, w_all, cosine, sine, gain_query, gain_key,
+    hidden, res_all, attended, ffn, ffn_parts, ffn_gain, residual, grad_residual, rows_in, gain,
 ):
-    own, width = inputs.shape
-    piece, small = (16, grad_in.shape[1] + attended.shape[1]), gains.shape[3:]
+    own, width = residual.shape
+    cols = w_all.shape[5]
+    piece, small = (16, cols + attended.shape[1]), (8, 128)
 
     def scratch(*shape):
         return [pltpu.VMEM((*shape, *piece), BF16)] * 2 + [pltpu.VMEM((*shape, *small), F32)]
@@ -786,9 +945,15 @@
             jax.ShapeDtypeStruct((4, own, width), BF16),
             jax.ShapeDtypeStruct((4, *small), F32),
         ],
-        in_specs=[VMEM] * 5 + [ANY] + [VMEM] * 5,
+        in_specs=[VMEM] * 11 + [ANY] + [VMEM] * 6,
         out_specs=[VMEM] + [ANY] * 4,
-        scratch_shapes=[pltpu.VMEM((4, 4, 2, 2, *piece), BF16)]
+        scratch_shapes=[
+            pltpu.VMEM((4, own, width), BF16),
+            pltpu.VMEM((4 * own, cols), BF16),
+            pltpu.VMEM((4, 4, 2, *small), F32),
+            pltpu.VMEM((own, width), BF16),
+            pltpu.VMEM((4, 4, 2, 2, *piece), BF16),
+        ]
         + [pltpu.VMEM((4, own, width), BF16), pltpu.VMEM((own, width), BF16)]
         + scratch(4, 4, 2)
         + scratch(4, 2)
@@ -801,48 +966,19 @@
             collective_id=8, has_side_effects=True, vmem_limit_bytes=24 * 2**20
         ),
         name="last_step",
-    )(parts, hidden, grad_in, res_rows, attended, ffn, gains, output, grad_residual, inputs, gain)
-
-
-def rms_scale(rows):
-    return lax.rsqrt(jnp.mean(rows * rows, axis=-1, keepdims=True) + EPSILON)
+    )(
+        dq, dkv, raw, w_all, cosine, sine, gain_query, gain_key,
+        hidden, res_all, attended, ffn, ffn_parts, ffn_gain, residual, grad_residual, rows_in, gain,
+    )
 
 
 def rope_tables(tokens, offset):
     half = HEAD_SIZE // 2
     inverse = ROPE_BASE ** (-(jnp.arange(half, dtype=F32) * 2.0 / HEAD_SIZE))
-    places_ = (offset + jnp.arange(tokens, dtype=jnp.int32)).astype(F32)
-    angles = places_[:, None] * inverse[None, :]
-    return jnp.cos(angles), jnp.sin(angles)
-
-
-def rotary(rows, cosine, sine, direction):
-    half = HEAD_SIZE // 2
-    first, second = rows[..., :half], rows[..., half:]
-    cosine = cosine[:, None, :]
-    sine = sine[:, None, :] * direction
-    return jnp.concatenate([first * cosine - second * sine, second * cosine + first * sine], -1)
-
-
-def head_back(grads, hatted, scale, gain):
-    scaled = grads * gain
-    return scale * (scaled - hatted * jnp.mean(scaled * hatted, axis=-1, keepdims=True))
-
-
-def to_pairs(rows, heads, left):
-    s, tokens = rows.shape[:2]
-    kv = rows.shape[2] // heads
-    x = rows.reshape(s, tokens, kv, heads, HEAD_SIZE).transpose(2, 0, 3, 1, 4)
-    x = x.reshape(kv * s, heads * tokens, HEAD_SIZE)
-    side = (0, HEAD_SIZE) if left else (HEAD_SIZE, 0)
-    return jnp.pad(x, ((0, 0), (0, 0), side))
-
-
-def from_pairs(x, s, heads):
-    kv = x.shape[0] // s
-    tokens = x.shape[1] // heads
-    x = x.reshape(kv, s, heads, tokens, HEAD_SIZE).transpose(1, 3, 0, 2, 4)
-    return x.reshape(s, tokens, kv * heads, HEAD_SIZE)
+    steps = (offset + jnp.arange(tokens, dtype=jnp.int32)).astype(F32)
+    angles = steps[:, None] * jnp.tile(inverse, 4)[None, :]
+    signs = jnp.where(jnp.arange(4 * half) % HEAD_SIZE < half, -1.0, 1.0)
+    return jnp.cos(angles), jnp.sin(angles) * signs[None, :]
 
 
 def halves(*weights):
@@ -856,108 +992,41 @@
     block_input, cotangent, w_query, key_weight, w_value, w_out, w_gate, w_up, w_down,
     norm_gains, head_gains,
 ):
-    c, t = lax.axis_index("ctx"), lax.axis_index("tp")
     seqs, tokens, width = block_input.shape
     rows = seqs * tokens
-    own = rows // 4
     unit_half = w_gate.shape[1] // 2
-
-    def mine(x):
-        return lax.dynamic_slice_in_dim(x, t * own, own, 0)
-
+    rows_in = block_input.reshape(rows, width)
+    cot_rows = cotangent.reshape(rows, width)
+    cosine, sine = rope_tables(tokens, lax.axis_index("ctx") * tokens)
     weight_rows = jnp.concatenate([w_query, key_weight, w_value], axis=1)
     gains = jnp.pad(norm_gains, ((0, 14), (0, 96))) + jnp.pad(head_gains, ((2, 12), (0, 126)))
-    ffn_rows = halves(w_gate, w_up, w_down)
-    weights_all, gains_all, ffn_pair = gather(
-        weight_rows.reshape(2, 16, weight_rows.shape[1]), gains, ffn_rows
-    )
-    gains_all = gains_all.reshape(NCTX, 16, 128)
+    (
+        weights_all, ffn_pair, hidden_attn, raw, q_src, kv_src,
+        gain_attn, gain_ffn, gain_query, gain_key,
+    ) = gather(
+        weight_rows.reshape(2, 16, weight_rows.shape[1]),
+        gains,
+        halves(w_gate, w_up, w_down),
+        rows_in,
+        cosine,
+        sine,
+    )
     planes = [[2 * g + h for g in range(NCTX // 2)] for h in range(2)]
     ffn_full = lax.all_gather(
         ffn_pair.reshape(2 * 32, 3 * UNITS), "ctx", axis_index_groups=planes, tiled=True
     )
-    qkv_full = weights_all.reshape(width, weight_rows.shape[1])
-    gain_attn = gains_all[:, 0, :32].reshape(width).astype(F32)
-    gain_ffn = gains_all[:, 1, :32].reshape(width).astype(F32)
-    gain_query = gains_all[:, 2, :2].reshape(HEAD_SIZE).astype(F32)
-    gain_key = gains_all[:, 3, :2].reshape(HEAD_SIZE).astype(F32)
-
-    inputs = block_input.astype(F32).reshape(rows, width)
-    scale_attn = rms_scale(inputs)
-    normed_attn = inputs * scale_attn
-    hidden_attn = (normed_attn * gain_attn).astype(BF16)
-    raw = jnp.dot(hidden_attn, qkv_full, preferred_element_type=F32)
-    query_raw = raw[:, :256].reshape(seqs, tokens, 4, HEAD_SIZE)
-    key_raw = raw[:, 256:384].reshape(seqs, tokens, 2, HEAD_SIZE)
-    values = raw[:, 384:].astype(BF16).reshape(seqs, tokens, 2, HEAD_SIZE)
-    query_scale, key_scale = rms_scale(query_raw), rms_scale(key_raw)
-    query_hat, key_hat = query_raw * query_scale, key_raw * key_scale
-    cosine, sine = rope_tables(tokens, c * tokens)
-    query_rot = rotary(query_hat * gain_query, cosine, sine, 1.0).astype(BF16)
-    key_rot = rotary(key_hat * gain_key, cosine, sine, 1.0).astype(BF16)
-    q_src = to_pairs(query_rot * jnp.asarray(HEAD_SIZE**-0.5, BF16), 2, True)
-    kv_src = jnp.concatenate([key_rot, values], axis=-1).transpose(2, 0, 1, 3)
-    kv_src = kv_src.reshape(PAIRS, 2, tokens // 2, 2 * HEAD_SIZE)
-
     att, q_buf, kv_buf, o_buf, log_buf, wo_all, cot_all = forward(
-        q_src, kv_src, w_out.reshape(2, 16, 256), cotangent.reshape(rows, width)
-    )
-    attended = from_pairs(att[..., HEAD_SIZE:], seqs, 2).reshape(rows, 256)
-    out_full = wo_all.reshape(width, 256)
-    cot_rows = cot_all.reshape(2 * rows, width)
-    attn_part = last_dims(attended, out_full).astype(BF16)
-    inputs_own = mine(inputs)
-    cot_own = mine(cotangent.reshape(rows, width))
-    residual, grad_residual, ffn_gain_part, residual_all, ffn_grads, ffn_part = feed_step(
-        attn_part.reshape(4, own, width),
-        inputs_own,
-        gain_ffn.reshape(1, width),
-        ffn_full,
-        cot_rows,
-        cot_own,
-    )
+        q_src, kv_src, w_out.reshape(2, 16, 256), cot_rows
+    )
+    (
+        attended, do_src, residual, grad_residual, ffn_gain, residual_all, ffn_grads, ffn_part,
+    ) = feed_step(att, wo_all, rows_in, gain_ffn, ffn_full, cot_all.reshape(2 * rows, width))
     grads_own = lax.psum_scatter(ffn_grads, "ctx", axis_index_groups=planes, tiled=True)
-    residual_bf = residual_all.reshape(rows, width)
-
-    grad_attended = jnp.dot(residual_bf, out_full, preferred_element_type=F32).astype(BF16)
-    do_src = to_pairs(grad_attended.reshape(seqs, tokens, 4, HEAD_SIZE), 2, False)
-    dq_all, dkv_all, ffn_parts = backward(
-        do_src, q_buf, kv_buf, o_buf, log_buf, ffn_part
-    )
-
-    output_own = (residual + jnp.sum(ffn_parts.astype(F32), axis=0)).astype(BF16)
-    grad_query_rot = from_pairs(dq_all[..., :HEAD_SIZE].astype(F32), seqs, 2)
-    dkv = dkv_all.reshape(PAIRS, tokens, 2 * HEAD_SIZE).astype(F32)
-    key_grad = from_pairs(dkv[..., :HEAD_SIZE], seqs, 1)
-    value_in = from_pairs(dkv[..., HEAD_SIZE:], seqs, 1).astype(BF16).reshape(rows, 128)
-    gq = rotary(grad_query_rot, cosine, sine, -1.0)
-    gk = rotary(key_grad, cosine, sine, -1.0)
-    query_gain_part = jnp.sum(gq * query_hat, axis=(0, 1, 2))
-    key_gain_part = jnp.sum(gk * key_hat, axis=(0, 1, 2))
-    query_in = head_back(gq, query_hat, query_scale, gain_query).astype(BF16).reshape(rows, 256)
-    key_in = head_back(gk, key_hat, key_scale, gain_key).astype(BF16).reshape(rows, 128)
-    grad_in = jnp.concatenate([query_in, key_in, value_in], axis=1)
-    attn_back = last_dims(grad_in, qkv_full)
-    attn_gain_part = jnp.sum(attn_back * normed_attn, axis=0)
-
-    def placed(row, part):
-        part = part.reshape(NCTX, 1, -1)
-        return jnp.pad(part, ((0, 0), (row, 7 - row), (0, 128 - part.shape[2])))
-
-    gain_parts = placed(0, attn_gain_part) + placed(1, ffn_gain_part)
-    gain_parts = gain_parts + placed(2, query_gain_part) + placed(3, key_gain_part)
+    dq_all, dkv_all, ffn_parts = backward(do_src, q_buf, kv_buf, o_buf, log_buf, ffn_part)
     qkv_grad, pair_grads, output_all, input_all, gain_tp = last_step(
-        attn_back.astype(BF16).reshape(4, own, width),
-        hidden_attn,
-        grad_in,
-        residual_bf,
-        attended,
-        grads_own.reshape(2, 32, -1),
-        gain_parts.reshape(4, 4, 2, 8, 128),
-        output_own,
-        grad_residual,
-        inputs_own,
-        gain_attn.reshape(1, width),
+        dq_all, dkv_all, raw, weights_all, cosine, sine, gain_query, gain_key,
+        hidden_attn, residual_all, attended, grads_own.reshape(2, 32, -1), ffn_parts, ffn_gain,
+        residual, grad_residual, rows_in, gain_attn,
     )
     pair_grads = pair_grads.astype(F32)
     gain_sum = jnp.sum(gain_tp, axis=0)

time: 289 us -> 289 us (level)
  waiting for transfers between devices: 0.08 us -> 26 us
  other arithmetic: 26.4 us -> 5.1 us
  matrix products: 4.81 us -> 0 us
    reduce_scatter x1, waiting for transfers between devices: 0.02 us -> 21.2 us  [local(): lax.psum_scatter(ffn_grads, 'ctx', axis_index_groups=planes, tiled=True)]
    unnamed x92 -> x97, local copies, waits for them, and re-layouts: 19 us -> 38.8 us
    reduce_sum x8 -> x0, other arithmetic: 6.39 us -> none  [the longest x2 2.45 us: local(): key_gain_part = jnp.sum(gk * key_hat, axis=(0, 1, 2))]
    mul x12 -> x1, local copies, waits for them, and re-layouts: 5.32 us -> 0.08 us  [rope_tables(): angles = steps[:, None] * jnp.tile(inverse, 4)[None, :]]
    dot_general x4 -> x0, matrix products: 4.81 us -> none  [the longest x2 2.84 us: last_dims(): lax.dot_general(a, b, (((1,), (1,)), ((), ())), preferred_element_type=F32)]
    all_gather x1, waiting for transfers between devices: 0.02 us -> 4.78 us  [local(): lax.all_gather(ffn_pair.reshape(2 * 32, 3 * UNITS), 'ctx', axis_index_gro...]
    pallas_call x1, Pallas kernels: 61.7 us -> 57.7 us  [backward(): pl.pallas_call(backward_body, out_shape=[jax.ShapeDtypeStruct((SLOTS, 2 *...]
    reshape x10 -> x0, local copies, waits for them, and re-layouts: 3.85 us -> none  [the longest x4 2.17 us: placed(): part = part.reshape(NCTX, 1, -1)]
  transfers between devices with their start and end apart: 2 -> 2, of which waited for: 0 -> 2; matrix products, arithmetic and copies ran while one was open for 15% -> 0% of each run, Pallas kernels for 36% -> 35%
where the time goes in v6:
time: 289 us; the launch traced here: 287 us
  Pallas kernels  195 us (67%)
  local copies, waits for them, and re-layouts  46.6 us (16%)
  waiting for transfers between devices  26 us (9%)
  between operations  14.3 us (5%)
  other arithmetic  5.1 us (2%)
    pallas_call x1, Pallas kernels, backward(): pl.pallas_call(backward_body, out_shape=[jax.ShapeDtypeStruct((SLOTS, 2 *...  57.7 us
    pallas_call x1, Pallas kernels, forward(): pl.pallas_call(forward_body, out_shape=[stack, stack, jax.ShapeDtypeStruc...  42 us
    pallas_call x1, Pallas kernels, feed_step(): pl.pallas_call(feed_body, out_shape=[jax.ShapeDtypeStruct((rows, wo.shape...  40 us
    unnamed x97, local copies, waits for them, and re-layouts  38.8 us
    pallas_call x1, Pallas kernels, last_step(): pl.pallas_call(last_body, out_shape=[jax.ShapeDtypeStruct((2, *piece), F3...  31.2 us
    pallas_call x1, Pallas kernels, gather(): pl.pallas_call(gather_body, out_shape=[jax.ShapeDtypeStruct((4, 4, 2, *w....  24.1 us
    reduce_scatter x1, waiting for transfers between devices, local(): lax.psum_scatter(ffn_grads, 'ctx', axis_index_groups=planes, tiled=True)  21.2 us
  transfers between devices with their start and end apart: 2, of which 2 were waited for; matrix products, arithmetic and copies ran while one was open for 0% of the time, Pallas kernels for 35%

profile of v6, /device:TPU:0, one launch (start us, length us, event | category | flops | bytes accessed | tf_op | source)
XLA Modules:
  0.0 287.0 jit_solution(3988754661090290243)
XLA Ops:
  7.4 1.1 stack.12
  8.6 1.0 stack.13
  9.8 1.0 stack.14
  10.9 0.6 fusion.5
  11.8 0.7 pad_add_fusion.gains
  12.5 0.8 pad_maximum_fusion.3
  13.2 0.3 fusion.6
  13.5 1.0 copy-done
  14.6 24.1 %gather.1 = (bf16[4,4,2,2,16,512]{5,4,3,2,1,0:T(8,128)(2,1)S(1)}, bf16[2,32,1920]{2,1,0:T(8,128)(2,1)}, bf16[256,1024]{1,0:T(8,128)(2,1)S(1)}, f32[256,512]{1,0:...) custom-call(bf16[2,16,512]{2,1,0:T(8,128)(2,1)S(1)} %bitcast.35, ...), custom_call_target="tpu_custom_call" | custom-call | tf_op jit(solution)/shard_map/gather/pallas_call | solution.py:301
  38.7 1.0 copy-done.4
  39.7 0.8 copy-done.10
  40.5 0.7 copy-done.36
  41.1 0.6 copy-done.40
  41.7 0.6 copy-done.42
  42.3 0.5 copy-done.44
  42.8 0.5 copy-done.46
  43.4 0.9 copy-done.37
  44.3 42.0 %attention_forward.1 = (bf16[4,256,128]{2,1,0:T(8,128)(2,1)S(1)}, bf16[4,256,128]{2,1,0:T(8,128)(2,1)S(1)}, bf16[4,4,2,2,64,128]{5,4,3,2,1,0:T(8,128)(2,1)S(1)},...) custom-call(bf16[4,256,128]{2,1,0:T(8,128)(2,1)S(1)} %get-tuple-elem, ...), custom_call_target="tpu_custom_call" | custom-call | tf_op jit(solution)/shard_map/attention_forward/pallas_call | solution.py:542
  86.4 1.0 copy-done.8
  87.3 0.8 copy-done.15
  88.1 0.8 copy-done.17
  88.9 0.7 copy-done.23
  89.6 0.7 copy-done.25
  90.3 0.7 copy-done.29
  91.0 4.8 %all-gather.2.cloned.1.call-done.w = bf16[1024,1920]{1,0:T(8,128)(2,1)} async-done(((bf16[64,1920]{1,0:T(8,128)(2,1)}), bf16[1024,1920]{1,0:T(8,128)(2,1)}) %all-gather.2.cloned.1.call-update) | async-done | bytes 3932176 | tf_op jit(solution)/shard_map/all_gather | solution.py:1015
  95.8 2.1 copy-done.2
  97.9 1.2 copy-done.9
  99.1 1.0 copy-done.18
  100.2 0.9 copy-done.30
  101.1 0.7 copy-done.43
  101.8 40.0 %feed_forward.1 = (bf16[256,256]{1,0:T(8,128)(2,1)S(1)}, bf16[4,256,128]{2,1,0:T(8,128)(2,1)S(1)}, f32[64,1024]{1,0:T(8,128)S(1)}, f32[64,1024]{1,0:T(8,128)S(1)...) custom-call(bf16[4,256,128]{2,1,0:T(8,128)(2,1)S(1)} %copy-done.30, ...), custom_call_target="tpu_custom_call" | custom-call | tf_op jit(solution)/shard_map/feed_forward/pallas_call | solution.py:776
  141.8 1.9 copy-done.3
  143.7 0.8 copy-done.12
  144.5 0.7 copy-done.19
  145.2 0.7 copy-done.27
  145.9 0.7 copy-done.32
  146.6 1.0 copy-done.16
  147.6 0.9 copy-done.24
  148.6 0.9 copy-done.26
  149.5 0.9 copy-done.28
  150.5 57.7 %attention_backward.1 = (bf16[4,256,128]{2,1,0:T(8,128)(2,1)S(1)}, bf16[4,2,64,128]{3,2,1,0:T(8,128)(2,1)S(1)}, bf16[8,64,1024]{2,1,0:T(8,128)(2,1)S(1)}) custom-call(bf16[4,256,128]{2,1,0:T(8,128)(2,1)S(1)} %copy-done.28, bf16[4,256,128]{2,1,0:T(8,128)(2,1)S(1)} %copy-done.24, bf16[4,4,2,2,64,128]{5,4,3,2,1,0:T(8,128)(2,1)S(1)} %get-tuple-element.53.kv_buf, ...), custom_call_target="tpu_custom_call" | custom-call | tf_op jit(solution)/shard_map/attention_backward/pallas_call | solution.py:627
  208.2 1.0 copy-done.6
  209.2 0.7 copy-done.21
  209.9 0.7 copy-done.34
  210.6 21.2 %reduce-scatter.2.cloned.1.call-done = bf16[64,1920]{1,0:T(8,128)(2,1)} async-done(((bf16[1024,1920]{1,0:T(8,128)(2,1)}), bf16[64,1920]{1,0:T(8,128)(2,1)}) %reduce-scatter.2.cloned.1.call-update) | async-done | bytes 245776 | tf_op jit(solution)/shard_map/reduce_scatter | solution.py:1024
  231.7 1.2 copy-done.5
  232.9 1.2 copy-done.7
  234.2 1.0 copy-done.11
  235.2 1.0 copy-done.13
  236.3 0.9 copy-done.20
  237.2 0.9 copy-done.22
  238.2 0.9 copy-done.31
  239.1 0.9 copy-done.33
  240.0 0.9 copy-done.35
  240.9 31.2 %last_step.1 = (f32[2,16,768]{2,1,0:T(8,128)S(1)}, bf16[2,32,1920]{2,1,0:T(8,128)(2,1)S(1)}, bf16[4,64,1024]{2,1,0:T(8,128)(2,1)S(1)}, bf16[4,64,1024]{2,1,0:T(8,128)(2,1)S(1)}, f32[4,8,128]{2,1,0:T(8,128)S(1)}) custom-call(bf16[4,256,128]{2,1,0:T(8,128)(2,1)S(1)} %copy-done.22, bf16[4,2,64,128]{3,2,1,0:T(8,128)(2,1)S(1)} %copy-done.35, ...), custom_call_target="tpu_custom_call" | custom-call | tf_op jit(solution)/shard_map/last_step/pallas_call | solution.py:939
  272.1 0.6 copy-done.38
  272.8 0.6 slice.47
  273.3 0.6 slice.46
  273.9 1.3 fusion.8
  275.3 1.4 fusion.7
  276.7 1.1 bitcast_convert_fusion
  277.8 0.8 pad_maximum_fusion.2
  278.6 0.8 pad_maximum_fusion
  279.4 0.8 copy.29
  (70 shorter events, 1.0 us)
Async XLA Ops:
  7.2 88.6 %copy-start.1 = (bf16[2,128,1024]{2,1,0:T(8,128)(2,1)S(1)}, bf16[2,128,1024]{2,1,0:T(8,128)(2,1)}, u32[]{:S(2)}) copy-start(bf16[2,128,1024]{2,1,0:T(8,128)(2,1)} %param.11) | copy-start | bytes 1572868
  7.2 36.2 %copy-start.39 = (bf16[32,256]{1,0:T(8,128)(2,1)S(1)}, bf16[32,256]{1,0:T(8,128)(2,1)}, u32[]{:S(2)}) copy-start(bf16[32,256]{1,0:T(8,128)(2,1)} %param.16) | copy-start | bytes 49156
  7.2 36.2 %copy-start.14 = (bf16[2,128,1024]{2,1,0:T(8,128)(2,1)S(1)}, bf16[2,128,1024]{2,1,0:T(8,128)(2,1)}, u32[]{:S(2)}) copy-start(bf16[2,128,1024]{2,1,0:T(8,128)(2,1)} %param.12) | copy-start | bytes 1572868
  7.2 88.6 %all-gather.2.cloned.1.call-start = ((), (), s32[]{:S(2)}) async-start(), calls=%async_computation.1 | async-start | bytes 4177920 | tf_op jit(solution)/shard_map/all_gather | solution.py:1015
  13.5 1.0 copy-start
  38.7 1.0 copy-start.4
  39.7 0.8 copy-start.10
  40.5 0.7 copy-start.36
  41.1 0.6 copy-start.40
  41.7 0.6 copy-start.42
  42.3 0.5 copy-start.44
  42.8 0.5 copy-start.46
  43.4 188.3 %reduce-scatter.2.cloned.1.call-start = ((), (), s32[]{:S(2)}) async-start(), calls=%async_computation.2 | async-start | bytes 4177920 | tf_op jit(solution)/shard_map/reduce_scatter | solution.py:1024
  43.4 0.9 copy-start.37
  86.3 1.0 copy-start.8
  87.3 0.8 copy-start.15
  88.1 0.8 copy-start.17
  88.9 0.7 copy-start.23
  89.6 0.7 copy-start.25
  90.3 0.7 copy-start.29
  95.8 2.1 copy-start.2
  97.9 1.2 copy-start.9
  99.1 1.0 copy-start.18
  100.2 0.9 copy-start.30
  101.1 0.7 copy-start.43
  141.8 1.9 copy-start.3
  143.7 0.8 copy-start.12
  144.5 0.7 copy-start.19
  145.2 0.7 copy-start.27
  145.9 0.7 copy-start.32
  146.5 85.2 %copy-start.41 = (f32[1,1024]{1,0:T(1,128)S(1)}, f32[1,1024]{1,0:T(1,128)}, u32[]{:S(2)}) copy-start(f32[1,1024]{1,0:T(1,128)} %copy-done.40) | copy-start | bytes 12292
  146.5 85.2 %copy-start.45 = (f32[1,128]{1,0:T(1,128)S(1)}, f32[1,128]{1,0:T(1,128)}, u32[]{:S(2)}) copy-start(f32[1,128]{1,0:T(1,128)} %copy-done.44) | copy-start | bytes 1540
  146.5 85.2 %copy-start.47 = (f32[1,128]{1,0:T(1,128)S(1)}, f32[1,128]{1,0:T(1,128)}, u32[]{:S(2)}) copy-start(f32[1,128]{1,0:T(1,128)} %copy-done.46) | copy-start | bytes 1540
  146.6 1.1 copy-start.16
  147.6 0.9 copy-start.24
  148.6 0.9 copy-start.26
  149.5 0.9 copy-start.28
  208.2 1.0 copy-start.6
  209.2 0.7 copy-start.21
  209.9 0.7 copy-start.34
  231.7 1.2 copy-start.5
  232.9 1.2 copy-start.7
  234.2 1.0 copy-start.11
  235.2 1.0 copy-start.13
  236.3 0.9 copy-start.20
  237.2 0.9 copy-start.22
  238.2 0.9 copy-start.31
  239.1 0.9 copy-start.33
  240.0 0.9 copy-start.35
  272.1 0.6 copy-start.38
Sparse Core Ops, SparseCore 0:
  43.5 52.2 all-gather.1
  146.7 84.9 reduce-scatter.1

commit v7 on v1

v7 whole, which is shorter than its diff:
```python
import functools
import types

import jax
import jax.numpy as jnp
from jax import lax
from jax.experimental import pallas as pl
from jax.experimental.pallas import tpu as pltpu
from jax.sharding import PartitionSpec as P

HEAD_SIZE = 64
EPSILON = 1e-06
ROPE_BASE = 1000000.0
MESH = pl.DeviceIdType.MESH
F32 = jnp.float32
BF16 = jnp.bfloat16
ANY = pl.BlockSpec(memory_space=pl.ANY)
VMEM = pl.BlockSpec(memory_space=pltpu.VMEM)
NCTX = 32
PAIRS = 4
WORKERS = 8
SLOTS = 4
BLOCK = 128


def group(kind):
    c, t = lax.axis_index("ctx"), lax.axis_index("tp")
    h = lax.rem(c, 2)
    if kind == "ctx":
        return NCTX, c, lambda p: (p, t)
    if kind == "tp":
        return 4, t, lambda p: (c, p)
    if kind == "pair":
        return 2, h, lambda p: (c - h + p, t)
    z, x, core = c // 8, lax.rem(c // 2, 4), lax.rem(t, 2)
    if kind == "z":
        return 4, z, lambda p: (c + (p - z) * 8, t)
    if kind == "x":
        return 4, x, lambda p: (c + (p - x) * 2, t)
    if kind == "core":
        return 2, core, lambda p: (c, t - core + p)
    if kind == "ring":
        return 4, h * 2 + t // 2, lambda p: (c - h + p // 2, lax.rem(p, 2) * 2 + core)
    return 8, h * 4 + t, lambda p: (c - h + p // 4, lax.rem(p, 4))


def push(kind, src_of, dst_of, send, recv, local=False):
    n, me, dev = group(kind)

    @pl.loop(1, n)
    def _(i):
        p = lax.rem(me + i, n)
        pltpu.make_async_remote_copy(
            src_ref=src_of(p),
            dst_ref=dst_of(me),
            send_sem=send.at[p],
            recv_sem=recv.at[me],
            device_id=dev(p),
            device_id_type=MESH,
        ).start()

    if local:
        pltpu.make_async_copy(src_of(me), dst_of(me), recv.at[me]).start()


def settle(kind, src_of, dst_of, send, recv, local=False):
    n, me, dev = group(kind)

    @pl.loop(1, n)
    def _(i):
        p = lax.rem(me + i, n)
        copy = pltpu.make_async_remote_copy(
            src_ref=src_of(p),
            dst_ref=dst_of(p),
            send_sem=send.at[p],
            recv_sem=recv.at[p],
            device_id=dev(p),
            device_id_type=MESH,
        )
        copy.wait_send()
        copy.wait_recv()

    if local:
        pltpu.make_async_copy(src_of(me), dst_of(me), recv.at[me]).wait()


def stage(*moves):
    for move in moves:
        push(*move)
    for move in moves:
        settle(*move)


class Sems:
    def __init__(self, ref):
        self.ref, self.used = ref, 0

    def two(self):
        self.used += 1
        return self.ref.at[self.used - 1, 0], self.ref.at[self.used - 1, 1]


def position():
    c = lax.axis_index("ctx")
    return c // 8, lax.rem(c // 2, 4), lax.rem(c, 2)


def iota(shape, axis):
    return lax.broadcasted_iota(jnp.int32, shape, axis)


def two_parts(v):
    high = v.astype(BF16)
    return high, (v - high.astype(F32)).astype(BF16)


def exact_dot(v, pattern):
    high, low = two_parts(v)
    return jnp.dot(high, pattern, preferred_element_type=F32) + jnp.dot(
        low, pattern, preferred_element_type=F32
    )


def head_mean(v):
    n = v.shape[1]
    same = lax.div(iota((n, n), 0), HEAD_SIZE) == lax.div(iota((n, n), 1), HEAD_SIZE)
    return exact_dot(v, jnp.where(same, 1.0 / HEAD_SIZE, 0.0).astype(BF16))


def head_scale(v):
    return lax.rsqrt(head_mean(v * v) + EPSILON)


def turned(u, cosine, sine):
    half, n = HEAD_SIZE // 2, 2 * HEAD_SIZE
    first = lax.rem(iota(u.shape, 1), HEAD_SIZE) < half
    other = jnp.where(first, pltpu.roll(u, n - half, 1), pltpu.roll(u, half, 1))
    return u * cosine + other * sine


def crossed(tile):
    return pltpu.roll(tile, HEAD_SIZE, 1)


def left_lanes(tile):
    return iota(tile.shape, 1) < HEAD_SIZE


def spread_gain(pieces, row, per, lanes):
    pattern = (lax.rem(iota((128, lanes), 1), per) == iota((128, lanes), 0)).astype(F32)
    wide = jnp.dot(pieces, pattern.astype(BF16), preferred_element_type=F32)
    r, lane = iota(wide.shape, 0), iota(wide.shape, 1)
    owner = lax.div(lax.rem(lane, NCTX * per), per)
    keep = jnp.logical_and(lax.rem(r, 16) == row, lax.div(r, 16) == owner)
    return jnp.sum(jnp.where(keep, wide, 0.0), axis=0, keepdims=True)


def owner_pieces(vector, per):
    lanes = vector.shape[1]
    shape = (NCTX, lanes)
    owner = lax.div(lax.rem(iota(shape, 1), NCTX * per), per)
    parts = jnp.where(owner == iota(shape, 0), jnp.broadcast_to(vector, shape), 0.0)
    pattern = (lax.rem(iota((lanes, 128), 0), per) == iota((lanes, 128), 1)).astype(F32)
    return exact_dot(parts, pattern.astype(BF16))


def row_scale(rows):
    return lax.rsqrt(jnp.mean(rows * rows, axis=1, keepdims=True) + EPSILON)


def twice(table):
    return jnp.concatenate([table[...], table[...]], axis=0)


def places():
    c, t = lax.axis_index("ctx"), lax.axis_index("tp")
    slot, low = c // WORKERS, lax.rem(c, WORKERS)
    to = low + lax.rem(slot, 2) * (WORKERS - 1 - 2 * low)
    return c, t, slot, low, to


def block_of(low, j):
    return j * WORKERS + (low if j % 2 == 0 else WORKERS - 1 - low)


def greet_attention(kinds):
    c, t, slot, low, to = places()
    barrier = pltpu.get_barrier_semaphore()
    total = 0
    others = [p * WORKERS + to for p in range(PAIRS)] + [block_of(low, j) for j in range(SLOTS)]
    for other in others:

        @pl.when(other != c)
        def _():
            pl.semaphore_signal(barrier, inc=1, device_id=(other, t), device_id_type=MESH)

        total = total + jnp.where(other != c, 1, 0)
    for kind in kinds:
        n, me, dev = group(kind)

        @pl.loop(1, n)
        def _(i):
            pl.semaphore_signal(
                barrier, inc=1, device_id=dev(lax.rem(me + i, n)), device_id_type=MESH
            )

        total = total + (n - 1)
    pl.semaphore_wait(barrier, total)


def to_workers(src, dst, send, recv, act):
    c, t, slot, low, to = places()
    for p in range(PAIRS):
        target = p * WORKERS + to
        far = pltpu.make_async_remote_copy(
            src_ref=src.at[p],
            dst_ref=dst.at[slot],
            send_sem=send.at[p],
            recv_sem=recv.at[slot],
            device_id=(target, t),
            device_id_type=MESH,
        )
        near = pltpu.make_async_copy(src.at[p], dst.at[slot], send.at[p])

        @pl.when(target != c)
        def _():
            far.start() if act == "start" else far.wait_send()

        @pl.when(target == c)
        def _():
            near.start() if act == "start" else near.wait()


def from_owners(src, dst, send, recv):
    c, t, slot, low, to = places()
    for j in range(SLOTS):
        owner = block_of(low, j)

        @pl.when(owner != c)
        def _():
            pltpu.make_async_remote_copy(
                src_ref=src.at[j],
                dst_ref=dst.at[j],
                send_sem=send.at[j],
                recv_sem=recv.at[j],
                device_id=(owner, t),
                device_id_type=MESH,
            ).wait_recv()


def to_owner(src, dst, send, recv, j, act):
    c, t, slot, low, to = places()
    owner = block_of(low, j)
    far = pltpu.make_async_remote_copy(
        src_ref=src.at[j],
        dst_ref=dst.at[slot],
        send_sem=send.at[j],
        recv_sem=recv.at[slot],
        device_id=(owner, t),
        device_id_type=MESH,
    )
    near = pltpu.make_async_copy(src.at[j], dst.at[slot], send.at[j])

    @pl.when(owner != c)
    def _():
        far.start() if act == "start" else far.wait_send()

    @pl.when(owner == c)
    def _():
        near.start() if act == "start" else near.wait()


def from_workers(src, dst, send, recv):
    c, t, slot, low, to = places()
    for p in range(PAIRS):
        target = p * WORKERS + to

        @pl.when(target != c)
        def _():
            pltpu.make_async_remote_copy(
                src_ref=src.at[p],
                dst_ref=dst.at[p],
                send_sem=send.at[p],
                recv_sem=recv.at[p],
                device_id=(target, t),
                device_id_type=MESH,
            ).wait_recv()


def last_dims(a, b):
    return lax.dot_general(a, b, (((1,), (1,)), ((), ())), preferred_element_type=F32)


def first_dims(a, b):
    return lax.dot_general(a, b, (((0,), (0,)), ((), ())), preferred_element_type=F32)


def causal_mask(b, i):
    shape = (2 * BLOCK, 2 * BLOCK)
    rows = lax.broadcasted_iota(jnp.int32, shape, 0)
    token = b * BLOCK + jnp.where(rows >= BLOCK, rows - BLOCK, rows)
    key = i * 2 * BLOCK + lax.broadcasted_iota(jnp.int32, shape, 1)
    return token >= key


def row_back(grads, normed, scale, gain):
    scaled = grads * gain
    return scale * (scaled - normed * jnp.mean(scaled * normed, axis=1, keepdims=True))


def summed(ref):
    total = ref[0].astype(F32)
    for k in range(1, ref.shape[0]):
        total += ref[k].astype(F32)
    return total


UNITS = 640
INPUTS = ("weights", "gains", "ffn", "wo", "cot", "rows_in", "cosine", "sine")
OUTPUTS = ("qkv_grad", "ffn_all", "output_all", "input_all", "gain_tp")
MOVES = 48


def scratch_arrays(rows, width, qkv_cols, out_cols):
    own, half = rows // 4, BLOCK // 2
    stack = (SLOTS, 2 * BLOCK, BLOCK)
    grid, piece = (4, 4, 2, 2), (16, qkv_cols + out_cols)
    units = (16, 3 * UNITS)
    return dict(
        w_all=((*grid, 16, qkv_cols), BF16),
        gains_all=((4, 4, 2, 16, 128), BF16),
        w_ffn=((*grid, *units), BF16),
        wo_all=((*grid, 16, out_cols), BF16),
        cot_all=((2, rows, width), BF16),
        hidden=((rows, width), BF16),
        raw=((rows, qkv_cols), F32),
        q_src=(stack, BF16),
        kv_src=((PAIRS, 2, half, BLOCK), BF16),
        gain_attn=((1, width), F32),
        gain_ffn=((1, width), F32),
        gain_query=((1, 128), F32),
        gain_key=((1, 128), F32),
        q_buf=(stack, BF16),
        kv_buf=((*grid, half, BLOCK), BF16),
        o_buf=(stack, BF16),
        log_buf=(stack, F32),
        att=(stack, BF16),
        acc=((2 * BLOCK, BLOCK), F32),
        den=((2 * BLOCK, BLOCK), F32),
        attended=((rows, out_cols), BF16),
        parts=((4, own, width), BF16),
        landed=((4, own, width), BF16),
        residual=((own, width), F32),
        hidden_own=((own, width), BF16),
        hidden_all=((4, 2, own, width), BF16),
        grad_units=((2 * rows, UNITS), F32),
        units=((2 * rows, UNITS), BF16),
        units_in=((2 * rows, 2 * UNITS), BF16),
        back=((4, 2, own, width), BF16),
        halved=((2, 4, own, width), BF16),
        chip=((4, own, width), BF16),
        ringed=((4, own, width), BF16),
        grad_bf=((own, width), BF16),
        grad_all=((4, own, width), BF16),
        grad_residual=((own, width), F32),
        ffn_gain=((1, width), F32),
        grads=((*grid, *units), BF16),
        ffn_part=((8, own, width), BF16),
        ffn_parts=((8, own, width), BF16),
        far_a=((4, 4, 2, *units), BF16),
        far_b=((4, 4, 2, *units), BF16),
        mid_a=((4, 2, *units), BF16),
        mid_b=((4, 2, *units), BF16),
        mid_far_a=((4, 2, *units), BF16),
        mid_far_b=((4, 2, *units), BF16),
        end_ab=((2, 2, *units), BF16),
        do_src=(stack, BF16),
        do_buf=(stack, BF16),
        dq_buf=(stack, BF16),
        dq=(stack, BF16),
        dkv_sum=((*grid, half, BLOCK), F32),
        dkv_buf=((*grid, half, BLOCK), BF16),
        kv_one_a=((4, 4, 2, half, BLOCK), BF16),
        kv_one_b=((2, 4, 4, half, BLOCK), BF16),
        kv_sum_a=((4, 2, half, BLOCK), BF16),
        kv_sum_b=((4, 4, half, BLOCK), BF16),
        kv_two_a=((2, 4, half, BLOCK), BF16),
        kv_two_b=((4, 4, half, BLOCK), BF16),
        kv_sum=((4, 2, half, BLOCK), BF16),
        dkv=((PAIRS, 2, half, BLOCK), BF16),
        parts_back=((4, own, width), BF16),
        landed_back=((4, own, width), BF16),
        grad_in=((rows, qkv_cols), BF16),
        gain_pieces=((4, 4, 2, 8, 128), F32),
        output=((own, width), BF16),
        input_bf=((own, width), BF16),
        qkv=((*grid, *piece), BF16),
        one_a=((4, 4, 2, *piece), BF16),
        one_b=((4, 4, 2, *piece), BF16),
        one_g=((4, 4, 2, 8, 128), F32),
        sum_a=((4, 2, *piece), BF16),
        sum_b=((4, 2, *piece), BF16),
        sum_g=((4, 2, 8, 128), F32),
        two_a=((4, 2, *piece), BF16),
        two_b=((4, 2, *piece), BF16),
        two_g=((4, 2, 8, 128), F32),
        part_a=((2, *piece), BF16),
        part_b=((2, *piece), BF16),
        part_g=((2, 8, 128), F32),
        three_a=((2, *piece), BF16),
        three_b=((2, *piece), BF16),
        three_g=((2, 8, 128), F32),
        gain_sum=((8, 128), F32),
    )


def project(r):
    pieces = r.gains_all[...].reshape(NCTX * 16, 128)
    r.gain_attn[...] = spread_gain(pieces, 0, 32, r.gain_attn.shape[1])
    r.gain_ffn[...] = spread_gain(pieces, 1, 32, r.gain_ffn.shape[1])
    r.gain_query[...] = spread_gain(pieces, 2, 2, 128)
    r.gain_key[...] = spread_gain(pieces, 3, 2, 128)
    rows = r.rows_in[...].astype(F32)
    r.hidden[...] = (rows * row_scale(rows) * r.gain_attn[...]).astype(BF16)
    weights = r.w_all[...].reshape(r.hidden.shape[1], r.w_all.shape[5])
    r.raw[...] = jnp.dot(r.hidden[...], weights, preferred_element_type=F32)
    cos, sin = twice(r.cosine), twice(r.sine)
    for k in range(2):
        tile = r.raw[:, k * 128 : k * 128 + 128]
        tile = turned(tile * head_scale(tile) * r.gain_query[...], cos, sin) * (HEAD_SIZE**-0.5)
        for a, one in enumerate((tile, crossed(tile))):
            one = jnp.where(left_lanes(one), one, 0.0).astype(BF16)
            for s in range(2):
                r.q_src[2 * k + s, a * BLOCK : (a + 1) * BLOCK] = one[s * BLOCK : (s + 1) * BLOCK]
    tile = r.raw[:, 256:384]
    keys = turned(tile * head_scale(tile) * r.gain_key[...], cos, sin)
    values = r.raw[:, 384:512]
    for k in range(2):
        key, value = (keys, crossed(values)) if k == 0 else (crossed(keys), values)
        one = jnp.where(left_lanes(key), key, value).astype(BF16)
        for s in range(2):
            part = one[s * BLOCK : (s + 1) * BLOCK]
            r.kv_src[2 * k + s] = part.reshape(2, BLOCK // 2, 128)


def attend(r, low, j):
    b = block_of(low, j)
    r.acc[...] = jnp.zeros_like(r.acc)
    r.den[...] = jnp.zeros_like(r.den)

    def chunk(i, masked):
        kv = r.kv_buf[i // 4, lax.rem(i, 4)].reshape(2 * BLOCK, BLOCK)
        powered = jnp.exp(last_dims(r.q_buf[j], kv))
        if masked:
            powered = jnp.where(causal_mask(b, i), powered, 0.0)
        r.den[...] += powered[:, :BLOCK] + powered[:, BLOCK:]
        r.acc[...] += jnp.dot(powered.astype(BF16), kv, preferred_element_type=F32)

    pl.loop(0, b // 2)(lambda i: chunk(i, False))
    chunk(b // 2, True)
    total = jnp.sum(r.den[...], axis=1, keepdims=True)
    lanes = iota((2 * BLOCK, BLOCK), 1)
    r.o_buf[j] = jnp.where(lanes >= HEAD_SIZE, r.acc[...] / total, 0.0).astype(BF16)
    r.log_buf[j] = jnp.broadcast_to(jnp.log(total), (2 * BLOCK, BLOCK))


def attend_back(r, low, j):
    b = block_of(low, j)
    r.acc[...] = jnp.zeros_like(r.acc)
    delta = jnp.sum(r.do_buf[j].astype(F32) * r.o_buf[j].astype(F32), axis=1, keepdims=True)

    def chunk(i, masked):
        q, do, logs = r.q_buf[j], r.do_buf[j], r.log_buf[j]
        kv = r.kv_buf[i // 4, lax.rem(i, 4)].reshape(2 * BLOCK, BLOCK)
        probs = jnp.exp(last_dims(q, kv) - jnp.concatenate([logs, logs], axis=1))
        if masked:
            probs = jnp.where(causal_mask(b, i), probs, 0.0)
        grads = (probs * (last_dims(do, kv) - delta)).astype(BF16)
        r.acc[...] += jnp.dot(grads, kv, preferred_element_type=F32)
        update = first_dims(grads, q) + first_dims(probs.astype(BF16), do)
        r.dkv_sum[i // 4, lax.rem(i, 4)] += update.reshape(2, 2, BLOCK // 2, BLOCK)

    pl.loop(0, b // 2)(lambda i: chunk(i, False))
    chunk(b // 2, True)
    r.dq_buf[j] = (r.acc[...] * (HEAD_SIZE**-0.5)).astype(BF16)


def tiles(m, n):
    return pl.ds(pl.multiple_of(m * n, n), n)


def project_back(r):
    cos, sin = twice(r.cosine), -twice(r.sine)
    own, width = r.residual.shape

    def head_back(u, tile, gain_row):
        turn = turned(u, cos, sin)
        scale = head_scale(tile)
        hat = tile * scale
        scaled = turn * gain_row
        back = scale * (scaled - hat * head_mean(scaled * hat))
        return back.astype(BF16), jnp.sum(turn * hat, axis=0, keepdims=True)

    def both(first, second):
        return jnp.concatenate([first.astype(F32), second.astype(F32)], axis=0)

    query_gain = jnp.zeros((1, 128), F32)
    for k in range(2):
        first = both(r.dq[2 * k, :BLOCK], r.dq[2 * k + 1, :BLOCK])
        second = crossed(both(r.dq[2 * k, BLOCK:], r.dq[2 * k + 1, BLOCK:]))
        lanes = slice(k * 128, (k + 1) * 128)
        back, part = head_back(
            jnp.where(left_lanes(first), first, second), r.raw[:, lanes], r.gain_query[...]
        )
        r.grad_in[:, lanes] = back
        query_gain = query_gain + part
    first, second = [
        both(r.dkv[2 * k].reshape(BLOCK, 128), r.dkv[2 * k + 1].reshape(BLOCK, 128))
        for k in range(2)
    ]
    left = left_lanes(first)
    back, key_gain = head_back(
        jnp.where(left, first, crossed(second)), r.raw[:, 256:384], r.gain_key[...]
    )
    r.grad_in[:, 256:384] = back
    r.grad_in[:, 384:] = jnp.where(left, crossed(first), second).astype(BF16)
    attn_gain = jnp.zeros((1, width), F32)
    weights = r.w_all[...].reshape(width, r.grad_in.shape[1])
    for q in range(4):
        at = slice(q * own, (q + 1) * own)
        back = last_dims(r.grad_in[at], weights)
        r.parts_back[q] = back.astype(BF16)
        rows = r.rows_in[at].astype(F32)
        attn_gain = attn_gain + jnp.sum(back * (rows * row_scale(rows)), axis=0, keepdims=True)
    return ((attn_gain, 32), (r.ffn_gain[...], 32), (query_gain, 2), (key_gain, 2))


def begin(moves):
    for move in moves:
        push(*move)


def finish(moves):
    for move in moves:
        settle(*move)


def whole_body(names, *refs):
    r = types.SimpleNamespace(**dict(zip(names, refs)))
    take = Sems(refs[-1])
    c, t, slot, low, to = places()
    z, x, h = position()
    core = lax.rem(t, 2)
    own, width = r.residual.shape

    def spread(kind, src_of, dst_of, local=False):
        return (kind, src_of, dst_of, *take.two(), local)

    def gathered(ref):
        second = [
            spread("x", lambda p: ref.at[z, x, :, 0], lambda q: ref.at[z, q, :, 0]),
            spread("z", lambda p: ref.at[z, x, :, 1], lambda q: ref.at[q, x, :, 1]),
        ]
        third = [
            spread("z", lambda p: ref.at[z, :, :, 0], lambda q: ref.at[q, :, :, 0]),
            spread("x", lambda p: ref.at[:, x, :, 1], lambda q: ref.at[:, q, :, 1]),
        ]
        return second, third

    greet_attention(["z", "x", "rows"])
    first = [
        spread("pair", lambda p: r.weights, lambda q: r.w_all.at[z, x, q], True),
        spread("pair", lambda p: r.gains, lambda q: r.gains_all.at[z, x, q], True),
    ]
    late = [
        spread("pair", lambda p: r.wo, lambda q: r.wo_all.at[z, x, q], True),
        spread("pair", lambda p: r.ffn.at[p], lambda q: r.w_ffn.at[z, x, q], True),
    ]
    begin(first)
    begin(late)
    finish(first)
    second, third = gathered(r.w_all)
    second.append(spread("x", lambda p: r.gains_all.at[z, x], lambda q: r.gains_all.at[z, q]))
    third.append(spread("z", lambda p: r.gains_all.at[z], lambda q: r.gains_all.at[q]))
    stage(*second)
    stage(*third)
    finish(late)
    out_second, out_third = gathered(r.wo_all)
    ffn_second, ffn_third = gathered(r.w_ffn)
    begin(out_second + ffn_second)
    project(r)

    q_send, q_recv = take.two()
    near = spread("z", lambda p: r.kv_src.at[p], lambda q: r.kv_buf.at[q, x, h], True)
    push(*near)
    to_workers(r.q_src, r.q_buf, q_send, q_recv, "start")
    settle(*near)
    kv = r.kv_buf
    stage(
        spread("x", lambda p: kv.at[:, x, h, 0], lambda q: kv.at[:, q, h, 0]),
        spread("pair", lambda p: kv.at[:, x, h, 1], lambda q: kv.at[:, x, q, 1]),
    )
    stage(
        spread("pair", lambda p: kv.at[:, :, h, 0], lambda q: kv.at[:, :, q, 0]),
        spread("x", lambda p: kv.at[:, x, :, 1], lambda q: kv.at[:, q, :, 1]),
    )
    finish(out_second + ffn_second)
    begin(out_third)
    begin(ffn_third)
    cot_swap = spread("pair", lambda p: r.cot, lambda q: r.cot_all.at[q], True)
    push(*cot_swap)
    to_workers(r.q_src, r.q_buf, q_send, q_recv, "wait")
    from_owners(r.q_src, r.q_buf, q_send, q_recv)
    o_send, o_recv = take.two()
    for j in range(SLOTS):
        attend(r, low, j)
        to_owner(r.o_buf, r.att, o_send, o_recv, j, "start")
    for j in range(SLOTS):
        to_owner(r.o_buf, r.att, o_send, o_recv, j, "wait")
    from_workers(r.o_buf, r.att, o_send, o_recv)

    for k in range(2):
        for s in range(2):
            left = crossed(r.att[2 * k + s, :BLOCK].astype(F32))
            right = r.att[2 * k + s, BLOCK:].astype(F32)
            one = jnp.where(left_lanes(left), left, right).astype(BF16)
            r.attended[s * BLOCK : (s + 1) * BLOCK, k * 128 : (k + 1) * 128] = one
    finish(out_third)
    out_full = r.wo_all[...].reshape(width, r.attended.shape[1])
    r.parts[...] = last_dims(r.attended[...], out_full).astype(BF16).reshape(r.parts.shape)
    stage(spread("tp", lambda p: r.parts.at[p], lambda q: r.landed.at[q], True))
    rows = r.rows_in[tiles(t, own)].astype(F32) + summed(r.landed)
    r.residual[...] = rows
    r.hidden_own[...] = (rows * row_scale(rows) * r.gain_ffn[...]).astype(BF16)
    ring = spread("ring", lambda p: r.hidden_own, lambda q: r.hidden_all.at[q, core], True)
    push(*ring)
    settle(*cot_swap)
    finish(ffn_third)
    w = r.w_ffn.reshape(width, 3 * UNITS)
    cot = r.cot_all.reshape(8 * own, width)

    @pl.loop(0, 4)
    def _(m):
        at = tiles(m, 2 * own)
        r.grad_units[at] = jnp.dot(cot[at], w[:, 2 * UNITS :], preferred_element_type=F32)

    settle(*ring)
    hidden = r.hidden_all
    stage(spread("core", lambda p: hidden.at[:, core], lambda q: hidden.at[:, q]))

    @pl.loop(0, 2)
    def _(m):
        at = tiles(m, 4 * own)
        some = hidden[pl.ds(2 * m, 2)].reshape(4 * own, width)
        gate = jnp.dot(some, w[:, :UNITS], preferred_element_type=F32)
        up = jnp.dot(some, w[:, UNITS : 2 * UNITS], preferred_element_type=F32)
        sigmoid = jax.nn.sigmoid(gate)
        activated = gate * sigmoid
        r.units[at] = (activated * up).astype(BF16)
        grad = r.grad_units[at]
        r.units_in[at, :UNITS] = (grad * up * sigmoid * (1.0 + gate * (1.0 - sigmoid))).astype(BF16)
        r.units_in[at, UNITS:] = (grad * activated).astype(BF16)
        step = last_dims(r.units_in[at], w[:, : 2 * UNITS]).astype(BF16)
        r.back[pl.ds(2 * m, 2)] = step.reshape(2, *r.back.shape[1:])

    both = spread("core", lambda p: r.back.at[:, p], lambda q: r.halved.at[q], True)
    push(*both)

    @pl.loop(0, 2)
    def _(m):
        step = last_dims(r.units[tiles(m, 4 * own)], w[:, 2 * UNITS :]).astype(BF16)
        r.ffn_part[pl.ds(4 * m, 4)] = step.reshape(4, *r.ffn_part.shape[1:])

    settle(*both)
    r.chip[...] = summed(r.halved).astype(BF16)
    ring = spread("ring", lambda p: r.chip.at[p], lambda q: r.ringed.at[q], True)
    push(*ring)

    @pl.loop(0, 4)
    def _(m):
        some = hidden[:, :, :, tiles(m, 256)].reshape(8 * own, 256)
        step = first_dims(some, r.units_in[...]).astype(BF16)
        r.grads[m, :, :, :, :, : 2 * UNITS] = step.reshape(4, 2, 2, 16, 2 * UNITS)

    settle(*ring)
    total = summed(r.ringed)
    rows = r.residual[...]
    scale = row_scale(rows)
    normed = rows * scale
    cot_own = cot[tiles(h * 4 + t, own)].astype(F32)
    result = cot_own + row_back(total, normed, scale, r.gain_ffn[...])
    r.grad_bf[...] = result.astype(BF16)
    share = spread("tp", lambda p: r.grad_bf, lambda q: r.grad_all.at[q], True)
    push(*share)
    r.grad_residual[...] = result
    r.ffn_gain[...] = jnp.sum(total * normed, axis=0, keepdims=True)

    @pl.loop(0, 4)
    def _(m):
        step = first_dims(cot[:, tiles(m, 256)], r.units[...]).astype(BF16)
        r.grads[m, :, :, :, :, 2 * UNITS :] = step.reshape(4, 2, 2, 16, UNITS)

    settle(*share)
    grad = jnp.dot(
        r.grad_all[...].reshape(4 * own, width), out_full, preferred_element_type=F32
    )
    for k in range(2):
        for s in range(2):
            tile = grad[s * BLOCK : (s + 1) * BLOCK, k * 128 : (k + 1) * 128]
            for a, one in enumerate((crossed(tile), tile)):
                one = jnp.where(left_lanes(one), 0.0, one).astype(BF16)
                r.do_src[2 * k + s, a * BLOCK : (a + 1) * BLOCK] = one

    do_send, do_recv = take.two()
    to_workers(r.do_src, r.do_buf, do_send, do_recv, "start")
    far = [
        spread("x", lambda p: r.grads.at[:, p, :, 0], lambda q: r.far_a.at[q], True),
        spread("z", lambda p: r.grads.at[p, :, :, 1], lambda q: r.far_b.at[q], True),
    ]
    begin(far)
    ffn_rows = spread("rows", lambda p: r.ffn_part.at[p], lambda q: r.ffn_parts.at[q], True)
    push(*ffn_rows)
    r.dkv_sum[...] = jnp.zeros_like(r.dkv_sum)
    to_workers(r.do_src, r.do_buf, do_send, do_recv, "wait")
    from_owners(r.do_src, r.do_buf, do_send, do_recv)
    dq_send, dq_recv = take.two()
    for j in range(SLOTS):
        attend_back(r, low, j)
        to_owner(r.dq_buf, r.dq, dq_send, dq_recv, j, "start")
    r.dkv_buf[...] = r.dkv_sum[...].astype(BF16)
    kv_first = [
        spread("x", lambda p: r.dkv_buf.at[:, p, :, 0], lambda q: r.kv_one_a.at[q], True),
        spread("pair", lambda p: r.dkv_buf.at[:, :, p, 1], lambda q: r.kv_one_b.at[q], True),
    ]
    begin(kv_first)
    finish(far)

    @pl.loop(0, 4)
    def _(m):
        for src, dst in ((r.far_a, r.mid_a), (r.far_b, r.mid_b)):
            total = src[0, m].astype(F32)
            for k in range(1, 4):
                total += src[k, m].astype(F32)
            dst[m] = total.astype(BF16)

    finish(kv_first)
    r.kv_sum_a[...] = summed(r.kv_one_a).astype(BF16)
    r.kv_sum_b[...] = summed(r.kv_one_b).astype(BF16)
    kv_second = [
        spread("pair", lambda p: r.kv_sum_a.at[:, p], lambda q: r.kv_two_a.at[q], True),
        spread("x", lambda p: r.kv_sum_b.at[:, p], lambda q: r.kv_two_b.at[q], True),
    ]
    begin(kv_second)
    mid = [
        spread("z", lambda p: r.mid_a.at[p], lambda q: r.mid_far_a.at[q], True),
        spread("x", lambda p: r.mid_b.at[p], lambda q: r.mid_far_b.at[q], True),
    ]
    finish(kv_second)
    r.kv_sum[:, 0] = summed(r.kv_two_a).astype(BF16)
    r.kv_sum[:, 1] = summed(r.kv_two_b).astype(BF16)
    kv_third = spread("z", lambda p: r.kv_sum.at[p], lambda q: r.dkv.at[q], True)
    push(*kv_third)
    begin(mid)
    settle(*kv_third)
    for j in range(SLOTS):
        to_owner(r.dq_buf, r.dq, dq_send, dq_recv, j, "wait")
    from_workers(r.dq_buf, r.dq, dq_send, dq_recv)

    vectors = project_back(r)
    sums = spread("tp", lambda p: r.parts_back.at[p], lambda q: r.landed_back.at[q], True)
    push(*sums)

    @pl.loop(0, 4)
    def _(m):
        at = tiles(m, 256)
        cols = r.grad_in.shape[1]
        step = first_dims(r.hidden[:, at], r.grad_in[...]).astype(BF16)
        r.qkv[m, :, :, :, :, :cols] = step.reshape(4, 2, 2, 16, cols)
        some = r.grad_all[:, :, at].reshape(4 * own, 256)
        step = first_dims(some, r.attended[...]).astype(BF16)
        r.qkv[m, :, :, :, :, cols:] = step.reshape(4, 2, 2, 16, r.attended.shape[1])

    pieces = jnp.zeros((NCTX, 8, 128), F32)
    for row, (vector, per) in enumerate(vectors):
        piece = jnp.broadcast_to(owner_pieces(vector, per)[:, None, :], pieces.shape)
        pieces = jnp.where(iota(pieces.shape, 1) == row, piece, pieces)
    r.gain_pieces[...] = pieces.reshape(r.gain_pieces.shape)
    one = [
        spread("x", lambda p: r.qkv.at[:, p, :, 0], lambda q: r.one_a.at[q], True),
        spread("z", lambda p: r.qkv.at[p, :, :, 1], lambda q: r.one_b.at[q], True),
        spread("x", lambda p: r.gain_pieces.at[:, p], lambda q: r.one_g.at[q], True),
    ]
    begin(one)
    finish(mid)
    r.end_ab[:, 0] = summed(r.mid_far_a).astype(BF16)
    r.end_ab[:, 1] = summed(r.mid_far_b).astype(BF16)
    swap = spread("pair", lambda p: r.end_ab.at[p], lambda q: r.ffn_all.at[q], True)
    push(*swap)
    settle(*ffn_rows)
    r.output[...] = (r.residual[...] + summed(r.ffn_parts)).astype(BF16)
    share = [spread("tp", lambda p: r.output, lambda q: r.output_all.at[q], True)]
    rows = r.rows_in[tiles(t, own)].astype(F32)
    scale = row_scale(rows)
    normed = rows * scale
    settle(*sums)
    result = r.grad_residual[...] + row_back(
        summed(r.landed_back), normed, scale, r.gain_attn[...]
    )
    r.input_bf[...] = result.astype(BF16)
    share.append(spread("tp", lambda p: r.input_bf, lambda q: r.input_all.at[q], True))
    begin(share)
    finish(one)
    r.sum_a[...] = summed(r.one_a).astype(BF16)
    r.sum_b[...] = summed(r.one_b).astype(BF16)
    r.sum_g[...] = summed(r.one_g)
    stage(
        spread("z", lambda p: r.sum_a.at[p], lambda q: r.two_a.at[q], True),
        spread("x", lambda p: r.sum_b.at[p], lambda q: r.two_b.at[q], True),
        spread("z", lambda p: r.sum_g.at[p], lambda q: r.two_g.at[q], True),
    )
    r.part_a[...] = summed(r.two_a).astype(BF16)
    r.part_b[...] = summed(r.two_b).astype(BF16)
    r.part_g[...] = summed(r.two_g)
    stage(
        spread("pair", lambda p: r.part_a.at[p], lambda q: r.three_a.at[q], True),
        spread("pair", lambda p: r.part_b.at[p], lambda q: r.three_b.at[q], True),
        spread("pair", lambda p: r.part_g.at[p], lambda q: r.three_g.at[q], True),
    )
    r.gain_sum[...] = summed(r.three_g)
    share.append(spread("tp", lambda p: r.gain_sum, lambda q: r.gain_tp.at[q], True))
    push(*share[-1])
    r.qkv_grad[0] = summed(r.three_a)
    r.qkv_grad[1] = summed(r.three_b)
    finish(share)
    settle(*swap)


def whole(weights, gains, ffn, wo, cot, rows_in, cosine, sine):
    rows, width = rows_in.shape
    arrays = scratch_arrays(rows, width, weights.shape[2], wo.shape[2])
    names = INPUTS + OUTPUTS + tuple(arrays)
    return pl.pallas_call(
        functools.partial(whole_body, names),
        out_shape=[
            jax.ShapeDtypeStruct((2, 16, weights.shape[2] + wo.shape[2]), F32),
            jax.ShapeDtypeStruct(ffn.shape, BF16),
            jax.ShapeDtypeStruct((4, rows // 4, width), BF16),
            jax.ShapeDtypeStruct((4, rows // 4, width), BF16),
            jax.ShapeDtypeStruct((4, 8, 128), F32),
        ],
        in_specs=[ANY] * 5 + [VMEM] * 3,
        out_specs=[VMEM] + [ANY] * 4,
        scratch_shapes=[pltpu.VMEM(shape, dtype) for shape, dtype in arrays.values()]
        + [pltpu.SemaphoreType.DMA((MOVES + 32, 2, 8))],
        compiler_params=pltpu.CompilerParams(
            collective_id=1, has_side_effects=True, vmem_limit_bytes=60 * 2**20
        ),
        name="block",
    )(weights, gains, ffn, wo, cot, rows_in, cosine, sine)


def rope_tables(tokens, offset):
    half = HEAD_SIZE // 2
    inverse = ROPE_BASE ** (-(jnp.arange(half, dtype=F32) * 2.0 / HEAD_SIZE))
    steps = (offset + jnp.arange(tokens, dtype=jnp.int32)).astype(F32)
    angles = steps[:, None] * jnp.tile(inverse, 4)[None, :]
    signs = jnp.where(jnp.arange(4 * half) % HEAD_SIZE < half, -1.0, 1.0)
    return jnp.cos(angles), jnp.sin(angles) * signs[None, :]


def halves(*weights):
    rows, cols = weights[0].shape
    w = jnp.stack(weights).reshape(len(weights), rows, 2, cols // 2)
    w = jnp.pad(w, ((0, 0), (0, 0), (0, 0), (0, UNITS - cols // 2)))
    return w.transpose(2, 1, 0, 3).reshape(2, rows, len(weights) * UNITS)


def local(
    block_input, cotangent, w_query, key_weight, w_value, w_out, w_gate, w_up, w_down,
    norm_gains, head_gains,
):
    seqs, tokens, width = block_input.shape
    rows = seqs * tokens
    unit_half = w_gate.shape[1] // 2
    rows_in = block_input.reshape(rows, width)
    cot_rows = cotangent.reshape(rows, width)
    cosine, sine = rope_tables(tokens, lax.axis_index("ctx") * tokens)
    weight_rows = jnp.concatenate([w_query, key_weight, w_value], axis=1)
    gains = jnp.pad(norm_gains, ((0, 14), (0, 96))) + jnp.pad(head_gains, ((2, 12), (0, 126)))
    ffn = halves(w_gate, w_up, w_down)
    qkv_grad, pair_grads, output_all, input_all, gain_tp = whole(
        weight_rows.reshape(2, 16, weight_rows.shape[1]),
        gains,
        ffn.reshape(2, 2, 16, ffn.shape[2]),
        w_out.reshape(2, 16, w_out.shape[1]),
        cot_rows,
        rows_in,
        cosine,
        sine,
    )
    pair_grads = pair_grads.reshape(ffn.shape)
    pair_grads = pair_grads.astype(F32)
    gain_sum = jnp.sum(gain_tp, axis=0)
    qkv_grad = qkv_grad.reshape(32, 768)

    def joined(first):
        last = first + unit_half
        return jnp.concatenate([pair_grads[0, :, first:last], pair_grads[1, :, first:last]], axis=1)

    gate_grad, up_grad, down_grad = joined(0), joined(UNITS), joined(2 * UNITS)
    return (
        output_all.reshape(seqs, tokens, width),
        input_all.astype(F32).reshape(seqs, tokens, width),
        qkv_grad[:, :256],
        qkv_grad[:, 256:384],
        qkv_grad[:, 384:512],
        qkv_grad[:, 512:],
        gate_grad,
        up_grad,
        down_grad,
        gain_sum[0:2, :32],
        gain_sum[2:4, :2],
    )


def solution(mesh):
    tokens, weights = P(None, "ctx", None), P("ctx", "tp")
    return jax.shard_map(
        local,
        mesh=mesh,
        in_specs=(tokens,) * 2 + (weights,) * 7 + (P(None, "ctx"),) * 2,
        out_specs=(tokens,) * 2 + (weights,) * 7 + (P(None, "ctx"),) * 2,
        check_vma=False,
    )
```

time: 401 us -> 225 us (0.56)
  Pallas kernels: 307 us -> 207 us
  local copies, waits for them, and re-layouts: 34.3 us -> 7.23 us
  other arithmetic: 34.1 us -> 8.66 us
  matrix products: 22 us -> 0 us
    pallas_call x9 -> x1, Pallas kernels: 307 us -> 207 us  [whole(): pl.pallas_call(functools.partial(whole_body, names), out_shape=[jax.Shape...]
    dot_general x12 -> x0, matrix products: 22 us -> none  [the longest x4 8 us: first_dims(): lax.dot_general(a, b, (((0,), (0,)), ((), ())), preferred_element_type=F32)]
    reduce_sum x20 -> x0, other arithmetic: 14.6 us -> none  [the longest x4 3.94 us: rms_scale(): return lax.rsqrt(jnp.mean(rows * rows, axis=-1, keepdims=True) + EPSILON)]
    unnamed x169 -> x13, local copies, waits for them, and re-layouts: 16.6 us -> 2.3 us
    convert_element_type x8 -> x2, other arithmetic: 8.89 us -> 0.98 us  [the longest x1 0.98 us: local(): pair_grads = pair_grads.astype(F32)]
    convert_element_type x8 -> x0, local copies, waits for them, and re-layouts: 4.41 us -> none  [the longest x1 1.78 us: local(): grad_dn = first_dims(cot_rows, hidden_units).astype(BF16)]
where the time goes in v7:
time: 225 us; the launch traced here: 223 us
  Pallas kernels  207 us (92%)
  other arithmetic  8.66 us (4%)
  local copies, waits for them, and re-layouts  7.23 us (3%)
    pallas_call x1, Pallas kernels, whole(): pl.pallas_call(functools.partial(whole_body, names), out_shape=[jax.Shape...  207 us

profile of v7, /device:TPU:0, one launch (start us, length us, event | category | flops | bytes accessed | tf_op | source)
XLA Modules:
  0.0 223.4 jit_solution(1596582460849981566)
XLA Ops:
  0.6 0.0 copy-start.3
  0.7 0.1 mul.31
  0.8 1.3 pad_add_fusion.refs_1_
  2.1 1.4 pad_maximum_fusion.3
  3.4 0.0 copy-done.3
  3.4 0.1 stack.12
  3.6 0.0 copy-start.4
  3.6 0.1 copy.25
  3.7 0.7 copy-done.4
  4.5 0.1 stack.13
  4.6 0.0 copy-start.5
  4.6 0.1 copy.26
  4.8 0.7 copy-done.5
  5.5 0.1 stack.14
  5.6 0.1 copy.27
  5.8 0.6 fusion.5
  6.4 0.9 reshape_reshape.3.refs_2_
  7.3 1.0 fusion.6
  8.3 206.8 %block.1 = (f32[2,16,768]{2,1,0:T(8,128)}, bf16[2,2,16,1920]{3,2,1,0:T(8,128)(2,1)}, bf16[4,64,1024]{2,1,0:T(8,128)(2,1)}, bf16[4,64,1024]{2,1,0:T(8,128)(2,1)}, f32[4,8,128]{2,1,0:T(8,128)}) custom-call(bf16[2,16,512]{2,1,0:T(8,128)(2,1)} %bitcast.31, bf16[16,128]{1,0:T(8,128)(2,1)} %pad_add_fusion.refs_1_, ...), custom_call_target="tpu_custom_call" | custom-call | tf_op jit(solution)/shard_map/block/pallas_call | solution.py:842
  215.1 0.0 copy-start.2
  215.1 0.8 reduce_sum.9
  215.8 0.6 slice.47
  216.4 0.6 slice.46
  217.0 1.3 fusion.8
  218.3 0.0 copy-done.2
  218.3 0.6 fusion.7
  219.0 1.0 bitcast_convert_fusion.1
  220.0 0.0 copy-start
  220.0 0.8 pad_maximum_fusion.2
  220.7 0.8 pad_maximum_fusion
  221.6 0.0 copy-done
  221.6 0.0 copy-start.1
  221.6 1.1 bitcast_convert_fusion
  222.7 0.0 copy-done.1
  222.7 0.8 copy.29
  (5 shorter events, 0.1 us)
Async XLA Ops:
  0.6 2.8 %copy-start.3 = (bf16[32,1152]{1,0:T(8,128)(2,1)S(1)}, bf16[32,1152]{1,0:T(8,128)(2,1)}, u32[]{:S(2)}) copy-start(bf16[32,1152]{1,0:T(8,128)(2,1)} %param.17) | copy-start | bytes 221188
  3.6 0.9 copy-start.4
  4.6 0.9 copy-start.5
  215.1 3.2 %copy-start.2 = (f32[2,16,768]{2,1,0:T(8,128)S(1)}, f32[2,16,768]{2,1,0:T(8,128)}, u32[]{:S(2)}) copy-start(f32[2,16,768]{2,1,0:T(8,128)} %get-tuple-element.18) | copy-start | bytes 294916
  220.0 1.6 copy-start
  221.6 1.1 copy-start.1

commit v8 on v7

--- a/solution.py
+++ b/solution.py
@@ -39,6 +39,8 @@
         return 4, x, lambda p: (c + (p - x) * 2, t)
     if kind == "core":
         return 2, core, lambda p: (c, t - core + p)
+    if kind == "near":
+        return 2, t // 2, lambda p: (c, p * 2 + core)
     if kind == "ring":
         return 4, h * 2 + t // 2, lambda p: (c - h + p // 2, lax.rem(p, 2) * 2 + core)
     return 8, h * 4 + t, lambda p: (c - h + p // 4, lax.rem(p, 4))
@@ -95,9 +97,10 @@
     def __init__(self, ref):
         self.ref, self.used = ref, 0
 
-    def two(self):
-        self.used += 1
-        return self.ref.at[self.used - 1, 0], self.ref.at[self.used - 1, 1]
+    def two(self, n):
+        at = self.used
+        self.used += 2 * n
+        return self.ref.at[pl.ds(at, n)], self.ref.at[pl.ds(at + n, n)]
 
 
 def position():
@@ -318,7 +321,8 @@
 UNITS = 640
 INPUTS = ("weights", "gains", "ffn", "wo", "cot", "rows_in", "cosine", "sine")
 OUTPUTS = ("qkv_grad", "ffn_all", "output_all", "input_all", "gain_tp")
-MOVES = 48
+SIZES = {"tp": 4, "pair": 2, "rows": 8, "z": 4, "x": 4, "core": 2, "ring": 4, "near": 2}
+SEMAPHORES = 412
 
 
 def scratch_arrays(rows, width, qkv_cols, out_cols):
@@ -348,8 +352,10 @@
         acc=((2 * BLOCK, BLOCK), F32),
         den=((2 * BLOCK, BLOCK), F32),
         attended=((rows, out_cols), BF16),
-        parts=((4, own, width), BF16),
-        landed=((4, own, width), BF16),
+        parts=((2, 2, own, width), BF16),
+        parts_half=((2, 2, own, width), BF16),
+        parts_chip=((2, own, width), BF16),
+        landed=((2, own, width), BF16),
         residual=((own, width), F32),
         hidden_own=((own, width), BF16),
         hidden_all=((4, 2, own, width), BF16),
@@ -361,7 +367,7 @@
         chip=((4, own, width), BF16),
         ringed=((4, own, width), BF16),
         grad_bf=((own, width), BF16),
-        grad_all=((4, own, width), BF16),
+        grad_all=((2, 2, own, width), BF16),
         grad_residual=((own, width), F32),
         ffn_gain=((1, width), F32),
         grads=((*grid, *units), BF16),
@@ -388,8 +394,10 @@
         kv_two_b=((4, 4, half, BLOCK), BF16),
         kv_sum=((4, 2, half, BLOCK), BF16),
         dkv=((PAIRS, 2, half, BLOCK), BF16),
-        parts_back=((4, own, width), BF16),
-        landed_back=((4, own, width), BF16),
+        parts_back=((2, 2, own, width), BF16),
+        back_half=((2, 2, own, width), BF16),
+        back_chip=((2, own, width), BF16),
+        landed_back=((2, own, width), BF16),
         grad_in=((rows, qkv_cols), BF16),
         gain_pieces=((4, 4, 2, 8, 128), F32),
         output=((own, width), BF16),
@@ -529,7 +537,7 @@
     for q in range(4):
         at = slice(q * own, (q + 1) * own)
         back = last_dims(r.grad_in[at], weights)
-        r.parts_back[q] = back.astype(BF16)
+        r.parts_back[q // 2, q % 2] = back.astype(BF16)
         rows = r.rows_in[at].astype(F32)
         attn_gain = attn_gain + jnp.sum(back * (rows * row_scale(rows)), axis=0, keepdims=True)
     return ((attn_gain, 32), (r.ffn_gain[...], 32), (query_gain, 2), (key_gain, 2))
@@ -554,7 +562,7 @@
     own, width = r.residual.shape
 
     def spread(kind, src_of, dst_of, local=False):
-        return (kind, src_of, dst_of, *take.two(), local)
+        return (kind, src_of, dst_of, *take.two(SIZES[kind]), local)
 
     def gathered(ref):
         second = [
@@ -590,7 +598,7 @@
     begin(out_second + ffn_second)
     project(r)
 
-    q_send, q_recv = take.two()
+    q_send, q_recv = take.two(SLOTS)
     near = spread("z", lambda p: r.kv_src.at[p], lambda q: r.kv_buf.at[q, x, h], True)
     push(*near)
     to_workers(r.q_src, r.q_buf, q_send, q_recv, "start")
@@ -611,7 +619,7 @@
     push(*cot_swap)
     to_workers(r.q_src, r.q_buf, q_send, q_recv, "wait")
     from_owners(r.q_src, r.q_buf, q_send, q_recv)
-    o_send, o_recv = take.two()
+    o_send, o_recv = take.two(SLOTS)
     for j in range(SLOTS):
         attend(r, low, j)
         to_owner(r.o_buf, r.att, o_send, o_recv, j, "start")
@@ -628,7 +636,9 @@
     finish(out_third)
     out_full = r.wo_all[...].reshape(width, r.attended.shape[1])
     r.parts[...] = last_dims(r.attended[...], out_full).astype(BF16).reshape(r.parts.shape)
-    stage(spread("tp", lambda p: r.parts.at[p], lambda q: r.landed.at[q], True))
+    stage(spread("core", lambda p: r.parts.at[:, p], lambda q: r.parts_half.at[q], True))
+    r.parts_chip[...] = summed(r.parts_half).astype(BF16)
+    stage(spread("near", lambda p: r.parts_chip.at[p], lambda q: r.landed.at[q], True))
     rows = r.rows_in[tiles(t, own)].astype(F32) + summed(r.landed)
     r.residual[...] = rows
     r.hidden_own[...] = (rows * row_scale(rows) * r.gain_ffn[...]).astype(BF16)
@@ -666,10 +676,10 @@
     both = spread("core", lambda p: r.back.at[:, p], lambda q: r.halved.at[q], True)
     push(*both)
 
-    @pl.loop(0, 2)
+    @pl.loop(0, 4)
     def _(m):
-        step = last_dims(r.units[tiles(m, 4 * own)], w[:, 2 * UNITS :]).astype(BF16)
-        r.ffn_part[pl.ds(4 * m, 4)] = step.reshape(4, *r.ffn_part.shape[1:])
+        step = first_dims(cot[:, tiles(m, 256)], r.units[...]).astype(BF16)
+        r.grads[m, :, :, :, :, 2 * UNITS :] = step.reshape(4, 2, 2, 16, UNITS)
 
     settle(*both)
     r.chip[...] = summed(r.halved).astype(BF16)
@@ -682,6 +692,11 @@
         step = first_dims(some, r.units_in[...]).astype(BF16)
         r.grads[m, :, :, :, :, : 2 * UNITS] = step.reshape(4, 2, 2, 16, 2 * UNITS)
 
+    far = [
+        spread("x", lambda p: r.grads.at[:, p, :, 0], lambda q: r.far_a.at[q], True),
+        spread("z", lambda p: r.grads.at[p, :, :, 1], lambda q: r.far_b.at[q], True),
+    ]
+    begin(far)
     settle(*ring)
     total = summed(r.ringed)
     rows = r.residual[...]
@@ -690,17 +705,19 @@
     cot_own = cot[tiles(h * 4 + t, own)].astype(F32)
     result = cot_own + row_back(total, normed, scale, r.gain_ffn[...])
     r.grad_bf[...] = result.astype(BF16)
-    share = spread("tp", lambda p: r.grad_bf, lambda q: r.grad_all.at[q], True)
+    share = spread("near", lambda p: r.grad_bf, lambda q: r.grad_all.at[q, core], True)
     push(*share)
     r.grad_residual[...] = result
     r.ffn_gain[...] = jnp.sum(total * normed, axis=0, keepdims=True)
 
-    @pl.loop(0, 4)
+    @pl.loop(0, 2)
     def _(m):
-        step = first_dims(cot[:, tiles(m, 256)], r.units[...]).astype(BF16)
-        r.grads[m, :, :, :, :, 2 * UNITS :] = step.reshape(4, 2, 2, 16, UNITS)
+        step = last_dims(r.units[tiles(m, 4 * own)], w[:, 2 * UNITS :]).astype(BF16)
+        r.ffn_part[pl.ds(4 * m, 4)] = step.reshape(4, *r.ffn_part.shape[1:])
 
     settle(*share)
+    grad_all = r.grad_all
+    stage(spread("core", lambda p: grad_all.at[:, core], lambda q: grad_all.at[:, q]))
     grad = jnp.dot(
         r.grad_all[...].reshape(4 * own, width), out_full, preferred_element_type=F32
     )
@@ -711,19 +728,14 @@
                 one = jnp.where(left_lanes(one), 0.0, one).astype(BF16)
                 r.do_src[2 * k + s, a * BLOCK : (a + 1) * BLOCK] = one
 
-    do_send, do_recv = take.two()
+    do_send, do_recv = take.two(SLOTS)
     to_workers(r.do_src, r.do_buf, do_send, do_recv, "start")
-    far = [
-        spread("x", lambda p: r.grads.at[:, p, :, 0], lambda q: r.far_a.at[q], True),
-        spread("z", lambda p: r.grads.at[p, :, :, 1], lambda q: r.far_b.at[q], True),
-    ]
-    begin(far)
     ffn_rows = spread("rows", lambda p: r.ffn_part.at[p], lambda q: r.ffn_parts.at[q], True)
     push(*ffn_rows)
     r.dkv_sum[...] = jnp.zeros_like(r.dkv_sum)
     to_workers(r.do_src, r.do_buf, do_send, do_recv, "wait")
     from_owners(r.do_src, r.do_buf, do_send, do_recv)
-    dq_send, dq_recv = take.two()
+    dq_send, dq_recv = take.two(SLOTS)
     for j in range(SLOTS):
         attend_back(r, low, j)
         to_owner(r.dq_buf, r.dq, dq_send, dq_recv, j, "start")
@@ -767,7 +779,9 @@
     from_workers(r.dq_buf, r.dq, dq_send, dq_recv)
 
     vectors = project_back(r)
-    sums = spread("tp", lambda p: r.parts_back.at[p], lambda q: r.landed_back.at[q], True)
+    stage(spread("core", lambda p: r.parts_back.at[:, p], lambda q: r.back_half.at[q], True))
+    r.back_chip[...] = summed(r.back_half).astype(BF16)
+    sums = spread("near", lambda p: r.back_chip.at[p], lambda q: r.landed_back.at[q], True)
     push(*sums)
 
     @pl.loop(0, 4)
@@ -776,7 +790,7 @@
         cols = r.grad_in.shape[1]
         step = first_dims(r.hidden[:, at], r.grad_in[...]).astype(BF16)
         r.qkv[m, :, :, :, :, :cols] = step.reshape(4, 2, 2, 16, cols)
-        some = r.grad_all[:, :, at].reshape(4 * own, 256)
+        some = r.grad_all[:, :, :, at].reshape(4 * own, 256)
         step = first_dims(some, r.attended[...]).astype(BF16)
         r.qkv[m, :, :, :, :, cols:] = step.reshape(4, 2, 2, 16, r.attended.shape[1])
 
@@ -851,7 +865,7 @@
         in_specs=[ANY] * 5 + [VMEM] * 3,
         out_specs=[VMEM] + [ANY] * 4,
         scratch_shapes=[pltpu.VMEM(shape, dtype) for shape, dtype in arrays.values()]
-        + [pltpu.SemaphoreType.DMA((MOVES + 32, 2, 8))],
+        + [pltpu.SemaphoreType.DMA((SEMAPHORES,))],
         compiler_params=pltpu.CompilerParams(
             collective_id=1, has_side_effects=True, vmem_limit_bytes=60 * 2**20
         ),

time: 225 us -> 221 us (0.982)
  Pallas kernels: 207 us -> 203 us
    pallas_call x1, Pallas kernels: 207 us -> 203 us  [whole(): pl.pallas_call(functools.partial(whole_body, names), out_shape=[jax.Shape...]
where the time goes in v8:
time: 221 us; the launch traced here: 220 us
  Pallas kernels  203 us (92%)
  other arithmetic  8.66 us (4%)
  local copies, waits for them, and re-layouts  7.23 us (3%)
    pallas_call x1, Pallas kernels, whole(): pl.pallas_call(functools.partial(whole_body, names), out_shape=[jax.Shape...  203 us

profile of v8, /device:TPU:0, one launch (start us, length us, event | category | flops | bytes accessed | tf_op | source)
XLA Modules:
  0.0 219.7 jit_solution(4283854019073428821)
XLA Ops:
  0.6 0.0 copy-start.3
  0.7 0.1 mul.31
  0.8 1.3 pad_add_fusion.refs_1_
  2.1 1.4 pad_maximum_fusion.3
  3.4 0.0 copy-done.3
  3.4 0.1 stack.12
  3.6 0.0 copy-start.4
  3.6 0.1 copy.25
  3.7 0.7 copy-done.4
  4.5 0.1 stack.13
  4.6 0.0 copy-start.5
  4.6 0.1 copy.26
  4.8 0.7 copy-done.5
  5.5 0.1 stack.14
  5.6 0.1 copy.27
  5.8 0.6 fusion.5
  6.4 0.9 reshape_reshape.3.refs_2_
  7.3 1.0 fusion.6
  8.3 203.1 %block.1 = (f32[2,16,768]{2,1,0:T(8,128)}, bf16[2,2,16,1920]{3,2,1,0:T(8,128)(2,1)}, bf16[4,64,1024]{2,1,0:T(8,128)(2,1)}, bf16[4,64,1024]{2,1,0:T(8,128)(2,1)}, f32[4,8,128]{2,1,0:T(8,128)}) custom-call(bf16[2,16,512]{2,1,0:T(8,128)(2,1)} %bitcast.31, bf16[16,128]{1,0:T(8,128)(2,1)} %pad_add_fusion.refs_1_, ...), custom_call_target="tpu_custom_call" | custom-call | tf_op jit(solution)/shard_map/block/pallas_call | solution.py:856
  211.4 0.0 copy-start.2
  211.4 0.8 reduce_sum.9
  212.1 0.6 slice.47
  212.7 0.6 slice.46
  213.3 1.3 fusion.8
  214.6 0.0 copy-done.2
  214.6 0.6 fusion.7
  215.3 1.0 bitcast_convert_fusion.1
  216.3 0.0 copy-start
  216.3 0.8 pad_maximum_fusion.2
  217.0 0.8 pad_maximum_fusion
  217.9 0.0 copy-done
  217.9 0.0 copy-start.1
  217.9 1.1 bitcast_convert_fusion
  219.0 0.0 copy-done.1
  219.0 0.8 copy.29
  (5 shorter events, 0.1 us)
Async XLA Ops:
  0.6 2.8 %copy-start.3 = (bf16[32,1152]{1,0:T(8,128)(2,1)S(1)}, bf16[32,1152]{1,0:T(8,128)(2,1)}, u32[]{:S(2)}) copy-start(bf16[32,1152]{1,0:T(8,128)(2,1)} %param.17) | copy-start | bytes 221188
  3.6 0.9 copy-start.4
  4.6 0.9 copy-start.5
  211.4 3.2 %copy-start.2 = (f32[2,16,768]{2,1,0:T(8,128)S(1)}, f32[2,16,768]{2,1,0:T(8,128)}, u32[]{:S(2)}) copy-start(f32[2,16,768]{2,1,0:T(8,128)} %get-tuple-element.18) | copy-start | bytes 294916
  216.3 1.6 copy-start
  217.9 1.1 copy-start.1

commit v9 on v8

--- a/solution.py
+++ b/solution.py
@@ -21,6 +21,7 @@
 WORKERS = 8
 SLOTS = 4
 BLOCK = 128
+CHUNK = 512
 
 
 def group(kind):
@@ -150,12 +151,13 @@
 
 
 def spread_gain(pieces, row, per, lanes):
+    n = pieces.shape[0]
+    pick = iota((NCTX, n), 1) == iota((NCTX, n), 0) * (n // NCTX) + row
+    mine = jnp.dot(pick.astype(F32).astype(BF16), pieces, preferred_element_type=F32).astype(BF16)
     pattern = (lax.rem(iota((128, lanes), 1), per) == iota((128, lanes), 0)).astype(F32)
-    wide = jnp.dot(pieces, pattern.astype(BF16), preferred_element_type=F32)
-    r, lane = iota(wide.shape, 0), iota(wide.shape, 1)
-    owner = lax.div(lax.rem(lane, NCTX * per), per)
-    keep = jnp.logical_and(lax.rem(r, 16) == row, lax.div(r, 16) == owner)
-    return jnp.sum(jnp.where(keep, wide, 0.0), axis=0, keepdims=True)
+    wide = jnp.dot(mine, pattern.astype(BF16), preferred_element_type=F32)
+    owner = lax.div(lax.rem(iota(wide.shape, 1), NCTX * per), per)
+    return jnp.sum(jnp.where(owner == iota(wide.shape, 0), wide, 0.0), axis=0, keepdims=True)
 
 
 def owner_pieces(vector, per):
@@ -299,10 +301,10 @@
 
 
 def causal_mask(b, i):
-    shape = (2 * BLOCK, 2 * BLOCK)
+    shape = (2 * BLOCK, CHUNK)
     rows = lax.broadcasted_iota(jnp.int32, shape, 0)
     token = b * BLOCK + jnp.where(rows >= BLOCK, rows - BLOCK, rows)
-    key = i * 2 * BLOCK + lax.broadcasted_iota(jnp.int32, shape, 1)
+    key = i * CHUNK + lax.broadcasted_iota(jnp.int32, shape, 1)
     return token >= key
 
 
@@ -322,7 +324,7 @@
 INPUTS = ("weights", "gains", "ffn", "wo", "cot", "rows_in", "cosine", "sine")
 OUTPUTS = ("qkv_grad", "ffn_all", "output_all", "input_all", "gain_tp")
 SIZES = {"tp": 4, "pair": 2, "rows": 8, "z": 4, "x": 4, "core": 2, "ring": 4, "near": 2}
-SEMAPHORES = 412
+SEMAPHORES = 484
 
 
 def scratch_arrays(rows, width, qkv_cols, out_cols):
@@ -387,10 +389,10 @@
         dkv_sum=((*grid, half, BLOCK), F32),
         dkv_buf=((*grid, half, BLOCK), BF16),
         kv_one_a=((4, 4, 2, half, BLOCK), BF16),
-        kv_one_b=((2, 4, 4, half, BLOCK), BF16),
+        kv_one_b=((4, 2, 4, half, BLOCK), BF16),
         kv_sum_a=((4, 2, half, BLOCK), BF16),
         kv_sum_b=((4, 4, half, BLOCK), BF16),
-        kv_two_a=((2, 4, half, BLOCK), BF16),
+        kv_two_a=((4, 2, half, BLOCK), BF16),
         kv_two_b=((4, 4, half, BLOCK), BF16),
         kv_sum=((4, 2, half, BLOCK), BF16),
         dkv=((PAIRS, 2, half, BLOCK), BF16),
@@ -422,16 +424,29 @@
     )
 
 
-def project(r):
+def project_keys(r):
     pieces = r.gains_all[...].reshape(NCTX * 16, 128)
     r.gain_attn[...] = spread_gain(pieces, 0, 32, r.gain_attn.shape[1])
-    r.gain_ffn[...] = spread_gain(pieces, 1, 32, r.gain_ffn.shape[1])
     r.gain_query[...] = spread_gain(pieces, 2, 2, 128)
     r.gain_key[...] = spread_gain(pieces, 3, 2, 128)
     rows = r.rows_in[...].astype(F32)
     r.hidden[...] = (rows * row_scale(rows) * r.gain_attn[...]).astype(BF16)
-    weights = r.w_all[...].reshape(r.hidden.shape[1], r.w_all.shape[5])
-    r.raw[...] = jnp.dot(r.hidden[...], weights, preferred_element_type=F32)
+    weights = r.w_all[:, :, :, :, :, 256:].reshape(r.hidden.shape[1], 256)
+    r.raw[:, 256:] = jnp.dot(r.hidden[...], weights, preferred_element_type=F32)
+    tile = r.raw[:, 256:384]
+    keys = turned(tile * head_scale(tile) * r.gain_key[...], twice(r.cosine), twice(r.sine))
+    values = r.raw[:, 384:512]
+    for k in range(2):
+        key, value = (keys, crossed(values)) if k == 0 else (crossed(keys), values)
+        one = jnp.where(left_lanes(key), key, value).astype(BF16)
+        for s in range(2):
+            part = one[s * BLOCK : (s + 1) * BLOCK]
+            r.kv_src[2 * k + s] = part.reshape(2, BLOCK // 2, 128)
+
+
+def project_queries(r):
+    weights = r.w_all[:, :, :, :, :, :256].reshape(r.hidden.shape[1], 256)
+    r.raw[:, :256] = jnp.dot(r.hidden[...], weights, preferred_element_type=F32)
     cos, sin = twice(r.cosine), twice(r.sine)
     for k in range(2):
         tile = r.raw[:, k * 128 : k * 128 + 128]
@@ -440,15 +455,8 @@
             one = jnp.where(left_lanes(one), one, 0.0).astype(BF16)
             for s in range(2):
                 r.q_src[2 * k + s, a * BLOCK : (a + 1) * BLOCK] = one[s * BLOCK : (s + 1) * BLOCK]
-    tile = r.raw[:, 256:384]
-    keys = turned(tile * head_scale(tile) * r.gain_key[...], cos, sin)
-    values = r.raw[:, 384:512]
-    for k in range(2):
-        key, value = (keys, crossed(values)) if k == 0 else (crossed(keys), values)
-        one = jnp.where(left_lanes(key), key, value).astype(BF16)
-        for s in range(2):
-            part = one[s * BLOCK : (s + 1) * BLOCK]
-            r.kv_src[2 * k + s] = part.reshape(2, BLOCK // 2, 128)
+    pieces = r.gains_all[...].reshape(NCTX * 16, 128)
+    r.gain_ffn[...] = spread_gain(pieces, 1, 32, r.gain_ffn.shape[1])
 
 
 def attend(r, low, j):
@@ -457,15 +465,16 @@
     r.den[...] = jnp.zeros_like(r.den)
 
     def chunk(i, masked):
-        kv = r.kv_buf[i // 4, lax.rem(i, 4)].reshape(2 * BLOCK, BLOCK)
+        kv = r.kv_buf[i // 2, pl.ds(2 * lax.rem(i, 2), 2)].reshape(CHUNK, BLOCK)
         powered = jnp.exp(last_dims(r.q_buf[j], kv))
         if masked:
             powered = jnp.where(causal_mask(b, i), powered, 0.0)
-        r.den[...] += powered[:, :BLOCK] + powered[:, BLOCK:]
+        r.den[...] += sum(powered[:, k : k + BLOCK] for k in range(0, CHUNK, BLOCK))
         r.acc[...] += jnp.dot(powered.astype(BF16), kv, preferred_element_type=F32)
 
-    pl.loop(0, b // 2)(lambda i: chunk(i, False))
-    chunk(b // 2, True)
+    last = b // (CHUNK // BLOCK)
+    pl.loop(0, last)(lambda i: chunk(i, False))
+    chunk(last, True)
     total = jnp.sum(r.den[...], axis=1, keepdims=True)
     lanes = iota((2 * BLOCK, BLOCK), 1)
     r.o_buf[j] = jnp.where(lanes >= HEAD_SIZE, r.acc[...] / total, 0.0).astype(BF16)
@@ -479,17 +488,19 @@
 
     def chunk(i, masked):
         q, do, logs = r.q_buf[j], r.do_buf[j], r.log_buf[j]
-        kv = r.kv_buf[i // 4, lax.rem(i, 4)].reshape(2 * BLOCK, BLOCK)
-        probs = jnp.exp(last_dims(q, kv) - jnp.concatenate([logs, logs], axis=1))
+        kv = r.kv_buf[i // 2, pl.ds(2 * lax.rem(i, 2), 2)].reshape(CHUNK, BLOCK)
+        probs = jnp.exp(last_dims(q, kv) - jnp.concatenate([logs] * (CHUNK // BLOCK), axis=1))
         if masked:
             probs = jnp.where(causal_mask(b, i), probs, 0.0)
         grads = (probs * (last_dims(do, kv) - delta)).astype(BF16)
         r.acc[...] += jnp.dot(grads, kv, preferred_element_type=F32)
         update = first_dims(grads, q) + first_dims(probs.astype(BF16), do)
-        r.dkv_sum[i // 4, lax.rem(i, 4)] += update.reshape(2, 2, BLOCK // 2, BLOCK)
-
-    pl.loop(0, b // 2)(lambda i: chunk(i, False))
-    chunk(b // 2, True)
+        at = pl.ds(2 * lax.rem(i, 2), 2)
+        r.dkv_sum[i // 2, at] += update.reshape(2, 2, 2, BLOCK // 2, BLOCK)
+
+    last = b // (CHUNK // BLOCK)
+    pl.loop(0, last)(lambda i: chunk(i, False))
+    chunk(last, True)
     r.dq_buf[j] = (r.acc[...] * (HEAD_SIZE**-0.5)).astype(BF16)
 
 
@@ -596,11 +607,12 @@
     out_second, out_third = gathered(r.wo_all)
     ffn_second, ffn_third = gathered(r.w_ffn)
     begin(out_second + ffn_second)
-    project(r)
+    project_keys(r)
 
     q_send, q_recv = take.two(SLOTS)
     near = spread("z", lambda p: r.kv_src.at[p], lambda q: r.kv_buf.at[q, x, h], True)
     push(*near)
+    project_queries(r)
     to_workers(r.q_src, r.q_buf, q_send, q_recv, "start")
     settle(*near)
     kv = r.kv_buf
@@ -736,15 +748,34 @@
     to_workers(r.do_src, r.do_buf, do_send, do_recv, "wait")
     from_owners(r.do_src, r.do_buf, do_send, do_recv)
     dq_send, dq_recv = take.two(SLOTS)
-    for j in range(SLOTS):
+
+    def kv_first(k):
+        r.dkv_buf[k] = r.dkv_sum[k].astype(BF16)
+        moves = [
+            spread("x", lambda p: r.dkv_buf.at[k, p, :, 0], lambda q: r.kv_one_a.at[k, q], True),
+            spread("pair", lambda p: r.dkv_buf.at[k, :, p, 1], lambda q: r.kv_one_b.at[k, q], True),
+        ]
+        begin(moves)
+        return moves
+
+    def kv_second(k, moves):
+        finish(moves)
+        r.kv_sum_a[k] = summed(r.kv_one_a.at[k]).astype(BF16)
+        r.kv_sum_b[k] = summed(r.kv_one_b.at[k]).astype(BF16)
+        moves = [
+            spread("pair", lambda p: r.kv_sum_a.at[k, p], lambda q: r.kv_two_a.at[k, q], True),
+            spread("x", lambda p: r.kv_sum_b.at[k, p], lambda q: r.kv_two_b.at[k, q], True),
+        ]
+        begin(moves)
+        return moves
+
+    firsts, seconds = {}, []
+    for j in reversed(range(SLOTS)):
         attend_back(r, low, j)
         to_owner(r.dq_buf, r.dq, dq_send, dq_recv, j, "start")
-    r.dkv_buf[...] = r.dkv_sum[...].astype(BF16)
-    kv_first = [
-        spread("x", lambda p: r.dkv_buf.at[:, p, :, 0], lambda q: r.kv_one_a.at[q], True),
-        spread("pair", lambda p: r.dkv_buf.at[:, :, p, 1], lambda q: r.kv_one_b.at[q], True),
-    ]
-    begin(kv_first)
+        firsts[j] = kv_first(j)
+        if j + 1 in firsts:
+            seconds += kv_second(j + 1, firsts[j + 1])
     finish(far)
 
     @pl.loop(0, 4)
@@ -755,21 +786,15 @@
                 total += src[k, m].astype(F32)
             dst[m] = total.astype(BF16)
 
-    finish(kv_first)
-    r.kv_sum_a[...] = summed(r.kv_one_a).astype(BF16)
-    r.kv_sum_b[...] = summed(r.kv_one_b).astype(BF16)
-    kv_second = [
-        spread("pair", lambda p: r.kv_sum_a.at[:, p], lambda q: r.kv_two_a.at[q], True),
-        spread("x", lambda p: r.kv_sum_b.at[:, p], lambda q: r.kv_two_b.at[q], True),
-    ]
-    begin(kv_second)
+    seconds += kv_second(0, firsts[0])
     mid = [
         spread("z", lambda p: r.mid_a.at[p], lambda q: r.mid_far_a.at[q], True),
         spread("x", lambda p: r.mid_b.at[p], lambda q: r.mid_far_b.at[q], True),
     ]
-    finish(kv_second)
-    r.kv_sum[:, 0] = summed(r.kv_two_a).astype(BF16)
-    r.kv_sum[:, 1] = summed(r.kv_two_b).astype(BF16)
+    finish(seconds)
+    for k in range(4):
+        r.kv_sum[k, 0] = summed(r.kv_two_a.at[k]).astype(BF16)
+        r.kv_sum[k, 1] = summed(r.kv_two_b.at[k]).astype(BF16)
     kv_third = spread("z", lambda p: r.kv_sum.at[p], lambda q: r.dkv.at[q], True)
     push(*kv_third)
     begin(mid)

time: 221 us -> 212 us (0.959)
  Pallas kernels: 203 us -> 194 us
    pallas_call x1, Pallas kernels: 203 us -> 194 us  [whole(): pl.pallas_call(functools.partial(whole_body, names), out_shape=[jax.Shape...]
where the time goes in v9:
time: 212 us; the launch traced here: 211 us
  Pallas kernels  194 us (92%)
  other arithmetic  8.66 us (4%)
  local copies, waits for them, and re-layouts  7.23 us (3%)
    pallas_call x1, Pallas kernels, whole(): pl.pallas_call(functools.partial(whole_body, names), out_shape=[jax.Shape...  194 us

profile of v9, /device:TPU:0, one launch (start us, length us, event | category | flops | bytes accessed | tf_op | source)
XLA Modules:
  0.0 210.7 jit_solution(6858856162179014423)
XLA Ops:
  0.6 0.0 copy-start.3
  0.7 0.1 mul.31
  0.8 1.3 pad_add_fusion.refs_1_
  2.1 1.4 pad_maximum_fusion.3
  3.4 0.0 copy-done.3
  3.4 0.1 stack.12
  3.6 0.0 copy-start.4
  3.6 0.1 copy.25
  3.7 0.7 copy-done.4
  4.5 0.1 stack.13
  4.6 0.0 copy-start.5
  4.6 0.1 copy.26
  4.8 0.7 copy-done.5
  5.5 0.1 stack.14
  5.6 0.1 copy.27
  5.8 0.6 fusion.5
  6.4 0.9 reshape_reshape.3.refs_2_
  7.3 1.0 fusion.6
  8.3 194.0 %block.1 = (f32[2,16,768]{2,1,0:T(8,128)}, bf16[2,2,16,1920]{3,2,1,0:T(8,128)(2,1)}, bf16[4,64,1024]{2,1,0:T(8,128)(2,1)}, bf16[4,64,1024]{2,1,0:T(8,128)(2,1)}, f32[4,8,128]{2,1,0:T(8,128)}) custom-call(bf16[2,16,512]{2,1,0:T(8,128)(2,1)} %bitcast.31, bf16[16,128]{1,0:T(8,128)(2,1)} %pad_add_fusion.refs_1_, ...), custom_call_target="tpu_custom_call" | custom-call | tf_op jit(solution)/shard_map/block/pallas_call | solution.py:881
  202.3 0.0 copy-start.2
  202.3 0.8 reduce_sum.9
  203.0 0.6 slice.47
  203.6 0.6 slice.46
  204.2 1.3 fusion.8
  205.5 0.0 copy-done.2
  205.5 0.6 fusion.7
  206.2 1.0 bitcast_convert_fusion.1
  207.2 0.0 copy-start
  207.2 0.8 pad_maximum_fusion.2
  207.9 0.8 pad_maximum_fusion
  208.8 0.0 copy-done
  208.8 0.0 copy-start.1
  208.8 1.1 bitcast_convert_fusion
  209.9 0.0 copy-done.1
  209.9 0.8 copy.29
  (5 shorter events, 0.1 us)
Async XLA Ops:
  0.6 2.8 %copy-start.3 = (bf16[32,1152]{1,0:T(8,128)(2,1)S(1)}, bf16[32,1152]{1,0:T(8,128)(2,1)}, u32[]{:S(2)}) copy-start(bf16[32,1152]{1,0:T(8,128)(2,1)} %param.17) | copy-start | bytes 221188
  3.6 0.9 copy-start.4
  4.6 0.9 copy-start.5
  202.3 3.2 %copy-start.2 = (f32[2,16,768]{2,1,0:T(8,128)S(1)}, f32[2,16,768]{2,1,0:T(8,128)}, u32[]{:S(2)}) copy-start(f32[2,16,768]{2,1,0:T(8,128)} %get-tuple-element.18) | copy-start | bytes 294916
  207.2 1.6 copy-start
  208.8 1.1 copy-start.1

commit v10 on v9

--- a/solution.py
+++ b/solution.py
@@ -324,7 +324,7 @@
 INPUTS = ("weights", "gains", "ffn", "wo", "cot", "rows_in", "cosine", "sine")
 OUTPUTS = ("qkv_grad", "ffn_all", "output_all", "input_all", "gain_tp")
 SIZES = {"tp": 4, "pair": 2, "rows": 8, "z": 4, "x": 4, "core": 2, "ring": 4, "near": 2}
-SEMAPHORES = 484
+SEMAPHORES = 572
 
 
 def scratch_arrays(rows, width, qkv_cols, out_cols):
@@ -508,40 +508,40 @@
     return pl.ds(pl.multiple_of(m * n, n), n)
 
 
-def project_back(r):
-    cos, sin = twice(r.cosine), -twice(r.sine)
-    own, width = r.residual.shape
-
-    def head_back(u, tile, gain_row):
-        turn = turned(u, cos, sin)
-        scale = head_scale(tile)
-        hat = tile * scale
-        scaled = turn * gain_row
-        back = scale * (scaled - hat * head_mean(scaled * hat))
-        return back.astype(BF16), jnp.sum(turn * hat, axis=0, keepdims=True)
-
-    def both(first, second):
-        return jnp.concatenate([first.astype(F32), second.astype(F32)], axis=0)
-
+def both_rows(first, second):
+    return jnp.concatenate([first.astype(F32), second.astype(F32)], axis=0)
+
+
+def head_back(r, u, tile, gain_row):
+    turn = turned(u, twice(r.cosine), -twice(r.sine))
+    scale = head_scale(tile)
+    hat = tile * scale
+    scaled = turn * gain_row
+    back = scale * (scaled - hat * head_mean(scaled * hat))
+    return back.astype(BF16), jnp.sum(turn * hat, axis=0, keepdims=True)
+
+
+def queries_back(r):
     query_gain = jnp.zeros((1, 128), F32)
     for k in range(2):
-        first = both(r.dq[2 * k, :BLOCK], r.dq[2 * k + 1, :BLOCK])
-        second = crossed(both(r.dq[2 * k, BLOCK:], r.dq[2 * k + 1, BLOCK:]))
+        first = both_rows(r.dq[2 * k, :BLOCK], r.dq[2 * k + 1, :BLOCK])
+        second = crossed(both_rows(r.dq[2 * k, BLOCK:], r.dq[2 * k + 1, BLOCK:]))
         lanes = slice(k * 128, (k + 1) * 128)
-        back, part = head_back(
-            jnp.where(left_lanes(first), first, second), r.raw[:, lanes], r.gain_query[...]
-        )
-        r.grad_in[:, lanes] = back
+        u = jnp.where(left_lanes(first), first, second)
+        r.grad_in[:, lanes], part = head_back(r, u, r.raw[:, lanes], r.gain_query[...])
         query_gain = query_gain + part
+    return query_gain
+
+
+def keys_back(r):
+    own, width = r.residual.shape
     first, second = [
-        both(r.dkv[2 * k].reshape(BLOCK, 128), r.dkv[2 * k + 1].reshape(BLOCK, 128))
+        both_rows(r.dkv[2 * k].reshape(BLOCK, 128), r.dkv[2 * k + 1].reshape(BLOCK, 128))
         for k in range(2)
     ]
     left = left_lanes(first)
-    back, key_gain = head_back(
-        jnp.where(left, first, crossed(second)), r.raw[:, 256:384], r.gain_key[...]
-    )
-    r.grad_in[:, 256:384] = back
+    u = jnp.where(left, first, crossed(second))
+    r.grad_in[:, 256:384], key_gain = head_back(r, u, r.raw[:, 256:384], r.gain_key[...])
     r.grad_in[:, 384:] = jnp.where(left, crossed(first), second).astype(BF16)
     attn_gain = jnp.zeros((1, width), F32)
     weights = r.w_all[...].reshape(width, r.grad_in.shape[1])
@@ -551,7 +551,7 @@
         r.parts_back[q // 2, q % 2] = back.astype(BF16)
         rows = r.rows_in[at].astype(F32)
         attn_gain = attn_gain + jnp.sum(back * (rows * row_scale(rows)), axis=0, keepdims=True)
-    return ((attn_gain, 32), (r.ffn_gain[...], 32), (query_gain, 2), (key_gain, 2))
+    return key_gain, attn_gain
 
 
 def begin(moves):
@@ -616,14 +616,22 @@
     to_workers(r.q_src, r.q_buf, q_send, q_recv, "start")
     settle(*near)
     kv = r.kv_buf
-    stage(
-        spread("x", lambda p: kv.at[:, x, h, 0], lambda q: kv.at[:, q, h, 0]),
-        spread("pair", lambda p: kv.at[:, x, h, 1], lambda q: kv.at[:, x, q, 1]),
-    )
-    stage(
-        spread("pair", lambda p: kv.at[:, :, h, 0], lambda q: kv.at[:, :, q, 0]),
-        spread("x", lambda p: kv.at[:, x, :, 1], lambda q: kv.at[:, q, :, 1]),
-    )
+
+    def planes(k):
+        return [
+            spread("x", lambda p: kv.at[k, x, h, 0], lambda q: kv.at[k, q, h, 0]),
+            spread("pair", lambda p: kv.at[k, x, h, 1], lambda q: kv.at[k, x, q, 1]),
+        ], [
+            spread("pair", lambda p: kv.at[k, :, h, 0], lambda q: kv.at[k, :, q, 0]),
+            spread("x", lambda p: kv.at[k, x, :, 1], lambda q: kv.at[k, q, :, 1]),
+        ]
+
+    plane_moves = [planes(k) for k in range(4)]
+    for early, _ in plane_moves:
+        begin(early)
+    for early, then in plane_moves:
+        finish(early)
+        begin(then)
     finish(out_second + ffn_second)
     begin(out_third)
     begin(ffn_third)
@@ -633,6 +641,7 @@
     from_owners(r.q_src, r.q_buf, q_send, q_recv)
     o_send, o_recv = take.two(SLOTS)
     for j in range(SLOTS):
+        finish(plane_moves[j][1])
         attend(r, low, j)
         to_owner(r.o_buf, r.att, o_send, o_recv, j, "start")
     for j in range(SLOTS):
@@ -745,6 +754,13 @@
     ffn_rows = spread("rows", lambda p: r.ffn_part.at[p], lambda q: r.ffn_parts.at[q], True)
     push(*ffn_rows)
     r.dkv_sum[...] = jnp.zeros_like(r.dkv_sum)
+
+    @pl.loop(0, 4)
+    def _(m):
+        some = r.grad_all[:, :, :, tiles(m, 256)].reshape(4 * own, 256)
+        step = first_dims(some, r.attended[...]).astype(BF16)
+        r.qkv[m, :, :, :, :, 256:512] = step.reshape(4, 2, 2, 16, 256)
+
     to_workers(r.do_src, r.do_buf, do_send, do_recv, "wait")
     from_owners(r.do_src, r.do_buf, do_send, do_recv)
     dq_send, dq_recv = take.two(SLOTS)
@@ -798,12 +814,39 @@
     kv_third = spread("z", lambda p: r.kv_sum.at[p], lambda q: r.dkv.at[q], True)
     push(*kv_third)
     begin(mid)
-    settle(*kv_third)
     for j in range(SLOTS):
         to_owner(r.dq_buf, r.dq, dq_send, dq_recv, j, "wait")
     from_workers(r.dq_buf, r.dq, dq_send, dq_recv)
 
-    vectors = project_back(r)
+    query_gain = queries_back(r)
+
+    @pl.loop(0, 4)
+    def _(m):
+        step = first_dims(r.hidden[:, tiles(m, 256)], r.grad_in[:, :256]).astype(BF16)
+        r.qkv[m, :, :, :, :, :256] = step.reshape(4, 2, 2, 16, 256)
+
+    def columns(first, last):
+        at = pl.ds(first, last - first)
+        return [
+            spread(
+                "x",
+                lambda p: r.qkv.at[:, p, :, 0, :, at],
+                lambda q: r.one_a.at[q, :, :, :, at],
+                True,
+            ),
+            spread(
+                "z",
+                lambda p: r.qkv.at[p, :, :, 1, :, at],
+                lambda q: r.one_b.at[q, :, :, :, at],
+                True,
+            ),
+        ]
+
+    one = columns(0, 512)
+    begin(one)
+    settle(*kv_third)
+    key_gain, attn_gain = keys_back(r)
+    vectors = ((attn_gain, 32), (r.ffn_gain[...], 32), (query_gain, 2), (key_gain, 2))
     stage(spread("core", lambda p: r.parts_back.at[:, p], lambda q: r.back_half.at[q], True))
     r.back_chip[...] = summed(r.back_half).astype(BF16)
     sums = spread("near", lambda p: r.back_chip.at[p], lambda q: r.landed_back.at[q], True)
@@ -811,25 +854,18 @@
 
     @pl.loop(0, 4)
     def _(m):
-        at = tiles(m, 256)
-        cols = r.grad_in.shape[1]
-        step = first_dims(r.hidden[:, at], r.grad_in[...]).astype(BF16)
-        r.qkv[m, :, :, :, :, :cols] = step.reshape(4, 2, 2, 16, cols)
-        some = r.grad_all[:, :, :, at].reshape(4 * own, 256)
-        step = first_dims(some, r.attended[...]).astype(BF16)
-        r.qkv[m, :, :, :, :, cols:] = step.reshape(4, 2, 2, 16, r.attended.shape[1])
+        step = first_dims(r.hidden[:, tiles(m, 256)], r.grad_in[:, 256:]).astype(BF16)
+        r.qkv[m, :, :, :, :, 512:] = step.reshape(4, 2, 2, 16, 256)
 
     pieces = jnp.zeros((NCTX, 8, 128), F32)
     for row, (vector, per) in enumerate(vectors):
         piece = jnp.broadcast_to(owner_pieces(vector, per)[:, None, :], pieces.shape)
         pieces = jnp.where(iota(pieces.shape, 1) == row, piece, pieces)
     r.gain_pieces[...] = pieces.reshape(r.gain_pieces.shape)
-    one = [
-        spread("x", lambda p: r.qkv.at[:, p, :, 0], lambda q: r.one_a.at[q], True),
-        spread("z", lambda p: r.qkv.at[p, :, :, 1], lambda q: r.one_b.at[q], True),
-        spread("x", lambda p: r.gain_pieces.at[:, p], lambda q: r.one_g.at[q], True),
-    ]
-    begin(one)
+    rest = columns(512, 768)
+    rest.append(spread("x", lambda p: r.gain_pieces.at[:, p], lambda q: r.one_g.at[q], True))
+    begin(rest)
+    one += rest
     finish(mid)
     r.end_ab[:, 0] = summed(r.mid_far_a).astype(BF16)
     r.end_ab[:, 1] = summed(r.mid_far_b).astype(BF16)
@@ -951,9 +987,9 @@
         output_all.reshape(seqs, tokens, width),
         input_all.astype(F32).reshape(seqs, tokens, width),
         qkv_grad[:, :256],
-        qkv_grad[:, 256:384],
-        qkv_grad[:, 384:512],
-        qkv_grad[:, 512:],
+        qkv_grad[:, 512:640],
+        qkv_grad[:, 640:],
+        qkv_grad[:, 256:512],
         gate_grad,
         up_grad,
         down_grad,

time: 212 us -> 208 us (0.981)
  Pallas kernels: 194 us -> 190 us
    pallas_call x1, Pallas kernels: 194 us -> 190 us  [whole(): pl.pallas_call(functools.partial(whole_body, names), out_shape=[jax.Shape...]
where the time goes in v10:
time: 208 us; the launch traced here: 207 us
  Pallas kernels  190 us (91%)
  other arithmetic  8.66 us (4%)
  local copies, waits for them, and re-layouts  7.23 us (3%)
    pallas_call x1, Pallas kernels, whole(): pl.pallas_call(functools.partial(whole_body, names), out_shape=[jax.Shape...  190 us

profile of v10, /device:TPU:0, one launch (start us, length us, event | category | flops | bytes accessed | tf_op | source)
XLA Modules:
  0.0 206.7 jit_solution(55397750006247684)
XLA Ops:
  0.6 0.0 copy-start.3
  0.7 0.1 mul.31
  0.8 1.3 pad_add_fusion.refs_1_
  2.1 1.4 pad_maximum_fusion.3
  3.4 0.0 copy-done.3
  3.4 0.1 stack.12
  3.6 0.0 copy-start.4
  3.6 0.1 copy.25
  3.7 0.7 copy-done.4
  4.5 0.1 stack.13
  4.6 0.0 copy-start.5
  4.6 0.1 copy.26
  4.8 0.7 copy-done.5
  5.5 0.1 stack.14
  5.6 0.1 copy.27
  5.8 0.6 fusion.5
  6.4 0.9 reshape_reshape.3.refs_2_
  7.3 1.0 fusion.6
  8.3 190.1 %block.1 = (f32[2,16,768]{2,1,0:T(8,128)}, bf16[2,2,16,1920]{3,2,1,0:T(8,128)(2,1)}, bf16[4,64,1024]{2,1,0:T(8,128)(2,1)}, bf16[4,64,1024]{2,1,0:T(8,128)(2,1)}, f32[4,8,128]{2,1,0:T(8,128)}) custom-call(bf16[2,16,512]{2,1,0:T(8,128)(2,1)} %bitcast.31, bf16[16,128]{1,0:T(8,128)(2,1)} %pad_add_fusion.refs_1_, ...), custom_call_target="tpu_custom_call" | custom-call | tf_op jit(solution)/shard_map/block/pallas_call | solution.py:917
  198.3 0.0 copy-start.2
  198.4 0.8 reduce_sum.9
  199.1 0.6 slice.47
  199.7 0.6 slice.46
  200.2 1.3 fusion.8
  201.6 0.0 copy-done.2
  201.6 0.6 fusion.7
  202.2 1.0 bitcast_convert_fusion.1
  203.3 0.0 copy-start
  203.3 0.8 pad_maximum_fusion.2
  204.0 0.8 pad_maximum_fusion
  204.8 0.0 copy-done
  204.8 0.0 copy-start.1
  204.8 1.1 bitcast_convert_fusion
  205.9 0.0 copy-done.1
  205.9 0.8 copy.29
  (5 shorter events, 0.1 us)
Async XLA Ops:
  0.6 2.8 %copy-start.3 = (bf16[32,1152]{1,0:T(8,128)(2,1)S(1)}, bf16[32,1152]{1,0:T(8,128)(2,1)}, u32[]{:S(2)}) copy-start(bf16[32,1152]{1,0:T(8,128)(2,1)} %param.17) | copy-start | bytes 221188
  3.6 0.9 copy-start.4
  4.6 0.9 copy-start.5
  198.3 3.2 %copy-start.2 = (f32[2,16,768]{2,1,0:T(8,128)S(1)}, f32[2,16,768]{2,1,0:T(8,128)}, u32[]{:S(2)}) copy-start(f32[2,16,768]{2,1,0:T(8,128)} %get-tuple-element.18) | copy-start | bytes 294916
  203.3 1.6 copy-start
  204.8 1.1 copy-start.1

commit v11 on v10

--- a/solution.py
+++ b/solution.py
@@ -321,10 +321,10 @@
 
 
 UNITS = 640
-INPUTS = ("weights", "gains", "ffn", "wo", "cot", "rows_in", "cosine", "sine")
+INPUTS = ("w_query", "w_key", "w_value", "gains", "ffn", "wo", "cot", "rows_in", "cosine", "sine")
 OUTPUTS = ("qkv_grad", "ffn_all", "output_all", "input_all", "gain_tp")
 SIZES = {"tp": 4, "pair": 2, "rows": 8, "z": 4, "x": 4, "core": 2, "ring": 4, "near": 2}
-SEMAPHORES = 572
+SEMAPHORES = 580
 
 
 def scratch_arrays(rows, width, qkv_cols, out_cols):
@@ -333,6 +333,7 @@
     grid, piece = (4, 4, 2, 2), (16, qkv_cols + out_cols)
     units = (16, 3 * UNITS)
     return dict(
+        w_own=((2, 16, qkv_cols), BF16),
         w_all=((*grid, 16, qkv_cols), BF16),
         gains_all=((4, 4, 2, 16, 128), BF16),
         w_ffn=((*grid, *units), BF16),
@@ -586,9 +587,20 @@
         ]
         return second, third
 
+    loads, first = [], 0
+    load_sems = take.two(4)[0]
+    for k, ref in enumerate((r.w_query, r.w_key, r.w_value)):
+        cols = ref.shape[2]
+        at = pl.ds(first, cols)
+        loads.append(pltpu.make_async_copy(ref, r.w_own.at[:, :, at], load_sems.at[k]))
+        first += cols
+    for load in loads:
+        load.start()
     greet_attention(["z", "x", "rows"])
+    for load in loads:
+        load.wait()
     first = [
-        spread("pair", lambda p: r.weights, lambda q: r.w_all.at[z, x, q], True),
+        spread("pair", lambda p: r.w_own, lambda q: r.w_all.at[z, x, q], True),
         spread("pair", lambda p: r.gains, lambda q: r.gains_all.at[z, x, q], True),
     ]
     late = [
@@ -910,20 +922,21 @@
     settle(*swap)
 
 
-def whole(weights, gains, ffn, wo, cot, rows_in, cosine, sine):
+def whole(w_query, w_key, w_value, gains, ffn, wo, cot, rows_in, cosine, sine):
     rows, width = rows_in.shape
-    arrays = scratch_arrays(rows, width, weights.shape[2], wo.shape[2])
+    cols = w_query.shape[2] + w_key.shape[2] + w_value.shape[2]
+    arrays = scratch_arrays(rows, width, cols, wo.shape[2])
     names = INPUTS + OUTPUTS + tuple(arrays)
     return pl.pallas_call(
         functools.partial(whole_body, names),
         out_shape=[
-            jax.ShapeDtypeStruct((2, 16, weights.shape[2] + wo.shape[2]), F32),
+            jax.ShapeDtypeStruct((2, 16, cols + wo.shape[2]), F32),
             jax.ShapeDtypeStruct(ffn.shape, BF16),
             jax.ShapeDtypeStruct((4, rows // 4, width), BF16),
             jax.ShapeDtypeStruct((4, rows // 4, width), BF16),
             jax.ShapeDtypeStruct((4, 8, 128), F32),
         ],
-        in_specs=[ANY] * 5 + [VMEM] * 3,
+        in_specs=[ANY] * 7 + [VMEM] * 3,
         out_specs=[VMEM] + [ANY] * 4,
         scratch_shapes=[pltpu.VMEM(shape, dtype) for shape, dtype in arrays.values()]
         + [pltpu.SemaphoreType.DMA((SEMAPHORES,))],
@@ -931,7 +944,7 @@
             collective_id=1, has_side_effects=True, vmem_limit_bytes=60 * 2**20
         ),
         name="block",
-    )(weights, gains, ffn, wo, cot, rows_in, cosine, sine)
+    )(w_query, w_key, w_value, gains, ffn, wo, cot, rows_in, cosine, sine)
 
 
 def rope_tables(tokens, offset):
@@ -960,11 +973,10 @@
     rows_in = block_input.reshape(rows, width)
     cot_rows = cotangent.reshape(rows, width)
     cosine, sine = rope_tables(tokens, lax.axis_index("ctx") * tokens)
-    weight_rows = jnp.concatenate([w_query, key_weight, w_value], axis=1)
     gains = jnp.pad(norm_gains, ((0, 14), (0, 96))) + jnp.pad(head_gains, ((2, 12), (0, 126)))
     ffn = halves(w_gate, w_up, w_down)
     qkv_grad, pair_grads, output_all, input_all, gain_tp = whole(
-        weight_rows.reshape(2, 16, weight_rows.shape[1]),
+        *(w.reshape(2, 16, w.shape[1]) for w in (w_query, key_weight, w_value)),
         gains,
         ffn.reshape(2, 2, 16, ffn.shape[2]),
         w_out.reshape(2, 16, w_out.shape[1]),

time: 208 us -> 207 us (level)
  no operation moved by 1% of the time
where the time goes in v11:
time: 207 us; the launch traced here: 206 us
  Pallas kernels  190 us (92%)
  local copies, waits for them, and re-layouts  8.68 us (4%)
  other arithmetic  6.62 us (3%)
    pallas_call x1, Pallas kernels, whole(): pl.pallas_call(functools.partial(whole_body, names), out_shape=[jax.Shape...  190 us

profile of v11, /device:TPU:0, one launch (start us, length us, event | category | flops | bytes accessed | tf_op | source)
XLA Modules:
  0.0 205.8 jit_solution(15309408095278267338)
XLA Ops:
  0.7 0.0 copy-start.5
  0.7 0.0 copy-start.6
  0.7 0.1 mul.31
  0.8 0.6 copy-done.5
  1.4 0.0 copy-done.6
  1.4 0.6 pad_add_fusion.refs_3_
  2.0 1.0 stack.12
  3.0 0.0 copy-start.3
  3.0 0.1 copy.25
  3.1 0.7 copy-done.3
  3.9 0.1 stack.13
  4.0 0.0 copy-start.4
  4.0 0.1 copy.26
  4.2 0.7 copy-done.4
  4.9 0.1 stack.14
  5.0 0.1 copy.27
  5.2 0.6 fusion.5
  5.8 0.9 reshape_reshape.3.refs_4_
  6.7 1.0 fusion.6
  7.7 189.7 %block.1 = (f32[2,16,768]{2,1,0:T(8,128)}, bf16[2,2,16,1920]{3,2,1,0:T(8,128)(2,1)}, bf16[4,64,1024]{2,1,0:T(8,128)(2,1)}, bf16[4,64,1024]{2,1,0:T(8,128)(2,1)}, f32[4,8,128]{2,1,0:T(8,128)}) custom-call(bf16[2,16,256]{2,1,0:T(8,128)(2,1)} %bitcast.35, bf16[2,16,128]{2,1,0:T(8,128)(2,1)} %bitcast.37, bf16[2,16,128]{2,1,0:T(8,128)(2,1)} %bitcast.38, ...), custom_call_target="tpu_custom_call" | custom-call | tf_op jit(solution)/shard_map/block/pallas_call | solution.py:930
  197.5 0.0 copy-start.2
  197.5 0.8 reduce_sum.9
  198.2 0.6 slice.47
  198.8 0.6 slice.46
  199.3 1.3 fusion.8
  200.7 0.0 copy-done.2
  200.7 0.6 fusion.7
  201.3 1.0 bitcast_convert_fusion.1
  202.4 0.0 copy-start
  202.4 0.8 pad_maximum_fusion.2
  203.1 0.8 pad_maximum_fusion
  203.9 0.0 copy-done
  203.9 0.0 copy-start.1
  203.9 1.1 bitcast_convert_fusion
  205.0 0.0 copy-done.1
  205.0 0.8 copy.29
  (5 shorter events, 0.1 us)
Async XLA Ops:
  0.7 0.7 copy-start.5
  0.7 0.7 copy-start.6
  3.0 0.9 copy-start.3
  4.0 0.9 copy-start.4
  197.5 3.2 %copy-start.2 = (f32[2,16,768]{2,1,0:T(8,128)S(1)}, f32[2,16,768]{2,1,0:T(8,128)}, u32[]{:S(2)}) copy-start(f32[2,16,768]{2,1,0:T(8,128)} %get-tuple-element.18) | copy-start | bytes 294916
  202.4 1.6 copy-start
  203.9 1.1 copy-start.1

commit v12 on v11

--- a/solution.py
+++ b/solution.py
@@ -340,6 +340,7 @@
         wo_all=((*grid, 16, out_cols), BF16),
         cot_all=((2, rows, width), BF16),
         hidden=((rows, width), BF16),
+        normed=((rows, width), F32),
         raw=((rows, qkv_cols), F32),
         q_src=(stack, BF16),
         kv_src=((PAIRS, 2, half, BLOCK), BF16),
@@ -430,8 +431,7 @@
     r.gain_attn[...] = spread_gain(pieces, 0, 32, r.gain_attn.shape[1])
     r.gain_query[...] = spread_gain(pieces, 2, 2, 128)
     r.gain_key[...] = spread_gain(pieces, 3, 2, 128)
-    rows = r.rows_in[...].astype(F32)
-    r.hidden[...] = (rows * row_scale(rows) * r.gain_attn[...]).astype(BF16)
+    r.hidden[...] = (r.normed[...] * r.gain_attn[...]).astype(BF16)
     weights = r.w_all[:, :, :, :, :, 256:].reshape(r.hidden.shape[1], 256)
     r.raw[:, 256:] = jnp.dot(r.hidden[...], weights, preferred_element_type=F32)
     tile = r.raw[:, 256:384]
@@ -550,8 +550,7 @@
         at = slice(q * own, (q + 1) * own)
         back = last_dims(r.grad_in[at], weights)
         r.parts_back[q // 2, q % 2] = back.astype(BF16)
-        rows = r.rows_in[at].astype(F32)
-        attn_gain = attn_gain + jnp.sum(back * (rows * row_scale(rows)), axis=0, keepdims=True)
+        attn_gain = attn_gain + jnp.sum(back * r.normed[at], axis=0, keepdims=True)
     return key_gain, attn_gain
 
 
@@ -609,6 +608,8 @@
     ]
     begin(first)
     begin(late)
+    rows = r.rows_in[...].astype(F32)
+    r.normed[...] = rows * row_scale(rows)
     finish(first)
     second, third = gathered(r.w_all)
     second.append(spread("x", lambda p: r.gains_all.at[z, x], lambda q: r.gains_all.at[z, q]))

time: 207 us -> 207 us (level)
  no operation moved by 1% of the time
where the time goes in v12:
time: 207 us; the launch traced here: 206 us
  Pallas kernels  190 us (92%)
  local copies, waits for them, and re-layouts  8.68 us (4%)
  other arithmetic  6.62 us (3%)
    pallas_call x1, Pallas kernels, whole(): pl.pallas_call(functools.partial(whole_body, names), out_shape=[jax.Shape...  190 us

profile of v12, /device:TPU:0, one launch (start us, length us, event | category | flops | bytes accessed | tf_op | source)
XLA Modules:
  0.0 205.8 jit_solution(9551573710868598538)
XLA Ops:
  0.7 0.0 copy-start.5
  0.7 0.0 copy-start.6
  0.7 0.1 mul.31
  0.8 0.6 copy-done.5
  1.4 0.0 copy-done.6
  1.4 0.6 pad_add_fusion.refs_3_
  2.0 1.0 stack.12
  3.0 0.0 copy-start.3
  3.0 0.1 copy.25
  3.1 0.7 copy-done.3
  3.9 0.1 stack.13
  4.0 0.0 copy-start.4
  4.0 0.1 copy.26
  4.2 0.7 copy-done.4
  4.9 0.1 stack.14
  5.0 0.1 copy.27
  5.2 0.6 fusion.5
  5.8 0.9 reshape_reshape.3.refs_4_
  6.7 1.0 fusion.6
  7.7 189.7 %block.1 = (f32[2,16,768]{2,1,0:T(8,128)}, bf16[2,2,16,1920]{3,2,1,0:T(8,128)(2,1)}, bf16[4,64,1024]{2,1,0:T(8,128)(2,1)}, bf16[4,64,1024]{2,1,0:T(8,128)(2,1)}, f32[4,8,128]{2,1,0:T(8,128)}) custom-call(bf16[2,16,256]{2,1,0:T(8,128)(2,1)} %bitcast.35, bf16[2,16,128]{2,1,0:T(8,128)(2,1)} %bitcast.37, bf16[2,16,128]{2,1,0:T(8,128)(2,1)} %bitcast.38, ...), custom_call_target="tpu_custom_call" | custom-call | tf_op jit(solution)/shard_map/block/pallas_call | solution.py:931
  197.4 0.0 copy-start.2
  197.4 0.8 reduce_sum.9
  198.2 0.6 slice.47
  198.7 0.6 slice.46
  199.3 1.3 fusion.8
  200.6 0.0 copy-done.2
  200.6 0.6 fusion.7
  201.3 1.0 bitcast_convert_fusion.1
  202.3 0.0 copy-start
  202.3 0.8 pad_maximum_fusion.2
  203.1 0.8 pad_maximum_fusion
  203.9 0.0 copy-done
  203.9 0.0 copy-start.1
  203.9 1.1 bitcast_convert_fusion
  205.0 0.0 copy-done.1
  205.0 0.8 copy.29
  (5 shorter events, 0.1 us)
Async XLA Ops:
  0.7 0.7 copy-start.5
  0.7 0.7 copy-start.6
  3.0 0.9 copy-start.3
  4.0 0.9 copy-start.4
  197.4 3.2 %copy-start.2 = (f32[2,16,768]{2,1,0:T(8,128)S(1)}, f32[2,16,768]{2,1,0:T(8,128)}, u32[]{:S(2)}) copy-start(f32[2,16,768]{2,1,0:T(8,128)} %get-tuple-element.18) | copy-start | bytes 294916
  202.3 1.6 copy-start
  203.9 1.1 copy-start.1
